TPU v7x, 512 devices: a whole 4x8x8 slice. The times are simulated.
512 devices in a mesh: dp: 16 (over y, core), dap: 32 (over x, z).
Axes of the slice: x: 4, y: 8, z: 8, core: 2. Of those that a mesh axis runs over, the one named last changes fastest.
Arguments:
- pair: bfloat16 [16, 256, 256, 128], P('dp', 'dap'), may hold values from -6 to 6
- cotangent: bfloat16 [16, 256, 256, 128], P('dp', 'dap'), may hold values from -6 to 6
- lengths: int32 [16], P('dp'), may hold values from 64 to 256, as said below
- w_in: bfloat16 [128, 640], replicated, may hold values from -0.5 to 0.5
- gain_in: float32 [128], replicated, may hold values from 0.5 to 1.5
- w_out: bfloat16 [128, 128], replicated, may hold values from -0.5 to 0.5
- gain_out: float32 [128], replicated, may hold values from 0.5 to 1.5
Outputs:
- pair_grad: bfloat16 [16, 256, 256, 128], P('dp', 'dap')
- w_in_grad: float32 [128, 640], replicated
- gain_in_grad: float32 [128], replicated
- w_out_grad: float32 [128, 128], replicated
- gain_out_grad: float32 [128], replicated
Inputs may be any that keep to these rules, and one draw needn't show every extreme that they name: `lengths`: some complex has exactly 256 valid tokens and another exactly 64.
All inputs are finite; a program needn't handle non-finite values.
Results may differ from a plain program's by a relative error of at most 0.0095.
Values may be sent and summed in bfloat16 or wider, within the bound.
No kernel may reach another device: no remote copies, remote signals or barrier semaphores. Data moves between devices by JAX's collectives and lax.ppermute only.
A program may use at most 64 MiB of HBM per device.

v0:
```python
import math

import jax
import jax.numpy as jnp
from jax import lax
from jax.sharding import PartitionSpec as P

EPSILON = 1e-05


def normalize(values):
    centred = values - jnp.mean(values, axis=-1, keepdims=True)
    variance = jnp.mean(centred * centred, axis=-1, keepdims=True)
    inverse = lax.rsqrt(variance + EPSILON)
    return (centred * inverse, inverse)


def normalize_back(upstream, normed, inverse):
    first_mean = jnp.mean(upstream, axis=-1, keepdims=True)
    second_mean = jnp.mean(upstream * normed, axis=-1, keepdims=True)
    return inverse * (upstream - first_mean - normed * second_mean)


def column_block(weights, index, channels):
    return weights[:, index * channels : (index + 1) * channels]


def flat_product(first, second):
    return lax.dot_general(
        first.reshape(-1, first.shape[-1]),
        second.reshape(-1, second.shape[-1]),
        (((0,), (0,)), ((), ())),
        preferred_element_type=jnp.float32,
    )


def channel_major(values):
    return jnp.transpose(values, (0, 3, 1, 2))


def channel_minor(values):
    return jnp.transpose(values, (0, 2, 3, 1))


def project(pair, cell_mask, w_in, gain_in):
    channels = pair.shape[-1]
    pair_hat, pair_inverse = normalize(pair.astype(jnp.float32))
    pair_norm = (pair_hat * gain_in).astype(jnp.bfloat16)

    def linear(index):
        return jnp.dot(
            pair_norm, column_block(w_in, index, channels), preferred_element_type=jnp.float32
        )

    left_proj = linear(0)
    left_gate = jax.nn.sigmoid(linear(1))
    right_proj = linear(2)
    right_gate = jax.nn.sigmoid(linear(3))
    out_gate = jax.nn.sigmoid(linear(4))
    left = (cell_mask * left_gate * left_proj).astype(jnp.bfloat16)
    right = (cell_mask * right_gate * right_proj).astype(jnp.bfloat16)
    saved = (pair_hat, pair_inverse, pair_norm, left_proj, left_gate, right_proj, right_gate)
    return (saved, out_gate, left, right)


def output_backward(product, out_gate, cotangent, w_out, gain_out):
    prod_hat, prod_inverse = normalize(product.astype(jnp.float32))
    prod_norm = (prod_hat * gain_out).astype(jnp.bfloat16)
    update = jnp.dot(prod_norm, w_out, preferred_element_type=jnp.float32)
    upstream = cotangent.astype(jnp.float32)
    grad_update = (upstream * out_gate).astype(jnp.bfloat16)
    grad_gate = upstream * update * out_gate * (1.0 - out_gate)
    w_out_part = flat_product(prod_norm, grad_update)
    grad_norm = jnp.dot(grad_update, w_out.T, preferred_element_type=jnp.float32)
    gain_out_part = jnp.sum((prod_hat * grad_norm).reshape(-1, prod_hat.shape[-1]), axis=0)
    grad_product = normalize_back(grad_norm * gain_out, prod_hat, prod_inverse).astype(jnp.bfloat16)
    return (grad_product, grad_gate, w_out_part, gain_out_part)


def input_backward(grad_left, grad_right, grad_gate, saved, cell_mask, w_in, gain_in):
    pair_hat, pair_inverse, pair_norm, left_proj, left_gate, right_proj, right_gate = saved
    channels = pair_hat.shape[-1]
    left_up = grad_left.astype(jnp.float32) * cell_mask
    right_up = grad_right.astype(jnp.float32) * cell_mask
    pieces = (
        left_up * left_gate,
        left_up * left_proj * left_gate * (1.0 - left_gate),
        right_up * right_gate,
        right_up * right_proj * right_gate * (1.0 - right_gate),
        grad_gate,
    )
    pieces = [piece.astype(jnp.bfloat16) for piece in pieces]
    w_in_part = jnp.concatenate([flat_product(pair_norm, piece) for piece in pieces], axis=1)
    grad_norm = jnp.dot(
        pieces[0], column_block(w_in, 0, channels).T, preferred_element_type=jnp.float32
    )
    for index in range(1, 5):
        grad_norm = grad_norm + jnp.dot(
            pieces[index], column_block(w_in, index, channels).T, preferred_element_type=jnp.float32
        )
    gain_in_part = jnp.sum((pair_hat * grad_norm).reshape(-1, channels), axis=0)
    grad_pair = normalize_back(grad_norm * gain_in, pair_hat, pair_inverse).astype(jnp.bfloat16)
    return (grad_pair, w_in_part, gain_in_part)


def per_device(pair, cotangent, lengths, w_in, gain_in, w_out, gain_out):
    blocks, rows, width, channels = pair.shape
    row_ids = lax.axis_index("dap") * rows + lax.iota(jnp.int32, rows)
    column_ids = lax.iota(jnp.int32, width)
    row_mask = (row_ids[None, :] < lengths[:, None]).astype(jnp.float32)
    column_mask = (column_ids[None, :] < lengths[:, None]).astype(jnp.float32)
    cell_mask = row_mask[:, :, None, None] * column_mask[:, None, :, None]
    saved, out_gate, left, right = project(pair, cell_mask, w_in, gain_in)
    left_cols, right_cols = (
        lax.all_to_all(channel_major(left), "dap", split_axis=1, concat_axis=2, tiled=True),
        lax.all_to_all(channel_major(right), "dap", split_axis=1, concat_axis=2, tiled=True),
    )
    product_cols = jnp.einsum(
        "bcik,bcjk->bcij", left_cols, right_cols, preferred_element_type=jnp.float32
    ).astype(jnp.bfloat16)
    product = channel_minor(
        lax.all_to_all(product_cols, "dap", split_axis=2, concat_axis=1, tiled=True)
    )
    grad_product, grad_gate, w_out_part, gain_out_part = output_backward(
        product, out_gate, cotangent, w_out, gain_out
    )
    grad_cols = lax.all_to_all(
        channel_major(grad_product), "dap", split_axis=1, concat_axis=2, tiled=True
    )
    grad_left_cols = jnp.einsum(
        "bcij,bcjk->bcik", grad_cols, right_cols, preferred_element_type=jnp.float32
    ).astype(jnp.bfloat16)
    grad_right_cols = jnp.einsum(
        "bcij,bcik->bcjk", grad_cols, left_cols, preferred_element_type=jnp.float32
    ).astype(jnp.bfloat16)
    grad_left_major, grad_right_major = (
        lax.all_to_all(grad_left_cols, "dap", split_axis=2, concat_axis=1, tiled=True),
        lax.all_to_all(grad_right_cols, "dap", split_axis=2, concat_axis=1, tiled=True),
    )
    grad_left = channel_minor(grad_left_major)
    grad_right = channel_minor(grad_right_major)
    grad_pair, w_in_part, gain_in_part = input_backward(
        grad_left, grad_right, grad_gate, saved, cell_mask, w_in, gain_in
    )
    w_in_total, gain_in_total, w_out_total, gain_out_total = lax.psum(
        (w_in_part, gain_in_part, w_out_part, gain_out_part), ("dp", "dap")
    )
    factor = 1.0 / (width * math.sqrt(blocks * lax.axis_size("dp")))
    return (
        grad_pair,
        w_in_total * factor,
        gain_in_total * factor,
        w_out_total * factor,
        gain_out_total * factor,
    )


def solution(mesh):
    in_specs = (P("dp", "dap", None, None), P("dp", "dap", None, None), P("dp"), P(), P(), P(), P())
    out_specs = (P("dp", "dap", None, None), P(), P(), P(), P())
    return jax.shard_map(
        per_device, mesh=mesh, in_specs=in_specs, out_specs=out_specs, check_vma=False
    )
```

profile of v0, /device:TPU:1, one launch (start us, length us, event | category | flops | bytes accessed | tf_op | source)
XLA Modules:
  0.0 551.0 jit_solution(6496438012916058019)
XLA Ops:
  7.2 1.2 copy.100
  9.5 1.5 fusion.6
  11.9 1.6 fusion.4
  14.2 2.7 fusion.47
  16.9 2.2 copy.103
  19.1 13.7 %all-to-all-start = ((bf16[1,128,8,256]{3,2,0,1:T(8,128)(2,1)}), bf16[1,128,8,256]{3,2,0,1:T(8,128)(2,1)S(1)}, u32[]{:S(2)}, u32[]{:S(2)}) async-start(bf16[1,128,8,256]{3,2,0,1:T(8,128)(2,1)} %copy.103), calls=%async_computation | async-start | bytes 1048576 | tf_op jit(solution)/shard_map/all_to_all | solution.py:115
  33.3 13.9 %all-to-all-done = bf16[1,128,8,256]{3,2,0,1:T(8,128)(2,1)S(1)} async-done(((bf16[1,128,8,256]{3,2,0,1:T(8,128)(2,1)}), bf16[1,128,8,256]{3,2,0,1:T(8,128)(2,1)S(1)}, u32[]{:S(2)}, u32[]{:S(2)}) %all-to-all-start) | async-done | bytes 524320 | tf_op jit(solution)/shard_map/all_to_all | solution.py:115
  47.2 20.9 %all_to_all.72 = bf16[1,128,8,256]{3,2,0,1:T(8,128)(2,1)S(1)} all-to-all(bf16[1,128,8,256]{3,2,0,1:T(8,128)(2,1)S(1)} %copy.107), channel_id=1, replica_groups=mesh['dp'=16,'dap'=32] {'dap'}, dimensions={1} | all-to-all | bytes 1048576 | tf_op jit(solution)/shard_map/all_to_all | solution.py:116
  68.9 1.2 copy.109
  70.1 8.0 %all-to-all-start.2 = ((bf16[1,4,256,256]{3,1,0,2:T(4,128)(2,1)}), bf16[1,4,256,256]{3,1,0,2:T(4,128)(2,1)S(1)}, u32[]{:S(2)}, u32[]{:S(2)}) async-start(bf16[1,4,256,256]{3,1,0,2:T(4,128)(2,1)} %copy.109), calls=%async_computation.2 | async-start | bytes 1048576 | tf_op jit(solution)/shard_map/all_to_all | solution.py:122
  78.1 1.5 fusion.8
  79.6 11.4 %all-to-all-done.2 = bf16[1,4,256,256]{3,1,0,2:T(4,128)(2,1)S(1)} async-done(((bf16[1,4,256,256]{3,1,0,2:T(4,128)(2,1)}), bf16[1,4,256,256]{3,1,0,2:T(4,128)(2,1)S(1)}, u32[]{:S(2)}, u32[]{:S(2)}) %all-to-all-start.2) | async-done | bytes 524320 | tf_op jit(solution)/shard_map/all_to_all | solution.py:122
  91.0 1.2 copy_bitcast_fusion
  92.2 1.6 reshape.299
  96.5 21.5 %all_to_all.73 = bf16[1,128,8,256]{3,2,0,1:T(8,128)(2,1)S(1)} all-to-all(bf16[1,128,8,256]{3,2,0,1:T(8,128)(2,1)S(1)} %copy.112), channel_id=1, replica_groups=mesh['dp'=16,'dap'=32] {'dap'}, dimensions={1} | all-to-all | bytes 1048576 | tf_op jit(solution)/shard_map/all_to_all | solution.py:127
  118.8 1.2 copy.114
  120.0 8.0 %all-to-all-start.4 = ((bf16[1,4,256,256]{3,1,0,2:T(4,128)(2,1)}), bf16[1,4,256,256]{3,1,0,2:T(4,128)(2,1)}, u32[]{:S(2)}, u32[]{:S(2)}) async-start(bf16[1,4,256,256]{3,1,0,2:T(4,128)(2,1)} %copy.114), calls=%async_computation.4 | async-start | bytes 1048576 | tf_op jit(solution)/shard_map/all_to_all | solution.py:137
  128.0 1.4 fusion.22
  129.4 1.2 copy.119
  130.6 9.8 %all-to-all-done.4 = bf16[1,4,256,256]{3,1,0,2:T(4,128)(2,1)} async-done(((bf16[1,4,256,256]{3,1,0,2:T(4,128)(2,1)}), bf16[1,4,256,256]{3,1,0,2:T(4,128)(2,1)}, u32[]{:S(2)}, u32[]{:S(2)}) %all-to-all-start.4) | async-done | bytes 524320 | tf_op jit(solution)/shard_map/all_to_all | solution.py:137
  140.3 7.9 %all-to-all-start.5 = ((bf16[1,4,256,256]{3,1,0,2:T(4,128)(2,1)}), bf16[1,4,256,256]{3,1,0,2:T(4,128)(2,1)}, u32[]{:S(2)}, u32[]{:S(2)}) async-start(bf16[1,4,256,256]{3,1,0,2:T(4,128)(2,1)} %copy.119), calls=%async_computation.5 | async-start | bytes 1048576 | tf_op jit(solution)/shard_map/all_to_all | solution.py:138
  148.5 2.3 convolution_bitcast_fusion.1
  150.8 1.3 fusion.19
  153.3 1.4 copy.117
  154.8 5.3 all-to-all-done.5
  160.0 1.1 convert_bitcast_fusion
  161.2 1.2 copy.121
  162.3 2.6 copy.122
  164.9 3.0 fusion.54
  172.5 1.3 fusion.33
  173.8 101.8 %all-reduce = (f32[128]{0:T(128)S(1)}, f32[128]{0:T(128)S(1)}) all-reduce(f32[128]{0:T(128)S(1)} %get-tuple-element.27, f32[128]{0:T(128)S(1)} %get-tuple-element.25), channel_id=1, replica_groups=mesh['dp'=16,'dap'=32] {'dp','dap'}, use_global_device_ids=true, to_apply=%region_10.0 | all-reduce | flops 256 | bytes 2048 | tf_op jit(solution)/shard_map/psum | solution.py:145
  278.1 263.5 %all-reduce.4.cloned.1.call-done = (f32[128,640]{0,1:T(8,128)}, f32[128,128]{1,0:T(8,128)}) async-done(((f32[128,640]{0,1:T(8,128)}, f32[128,128]{1,0:T(8,128)}), (f32[128,640]{0,1:T(8,128)}, f32[128,128]{1,0:T(8,128)})) %all-reduce.4.cloned.1.call-update) | async-done | bytes 393232 | tf_op jit(solution)/shard_map/psum | solution.py:145
  (78 shorter events, 17.4 us)
Async XLA Ops:
  7.2 86.9 %copy-start = (bf16[128,128]{1,0:T(8,128)(2,1)S(1)}, bf16[128,128]{1,0:T(8,128)(2,1)}, u32[]{:S(2)}) copy-start(bf16[128,128]{1,0:T(8,128)(2,1)} %param.12) | copy-start | bytes 98308
  8.5 0.9 copy-start.12
  8.7 0.7 copy-start.15
  11.8 2.4 copy-start.1
  19.1 28.0 %all-to-all-start = ((bf16[1,128,8,256]{3,2,0,1:T(8,128)(2,1)}), bf16[1,128,8,256]{3,2,0,1:T(8,128)(2,1)S(1)}, u32[]{:S(2)}, u32[]{:S(2)}) async-start(bf16[1,128,8,256]{3,2,0,1:T(8,128)(2,1)} %copy.103), calls=%async_computation | async-start | bytes 1048576 | tf_op jit(solution)/shard_map/all_to_all | solution.py:115
  68.1 0.8 copy-start.5
  70.1 20.9 %all-to-all-start.2 = ((bf16[1,4,256,256]{3,1,0,2:T(4,128)(2,1)}), bf16[1,4,256,256]{3,1,0,2:T(4,128)(2,1)S(1)}, u32[]{:S(2)}, u32[]{:S(2)}) async-start(bf16[1,4,256,256]{3,1,0,2:T(4,128)(2,1)} %copy.109), calls=%async_computation.2 | async-start | bytes 1048576 | tf_op jit(solution)/shard_map/all_to_all | solution.py:122
  93.8 1.2 copy-start.3
  93.9 1.3 copy-start.8
  94.0 1.1 copy-start.16
  96.5 21.5 %copy-start.6 = (bf16[1,128,8,256]{3,2,0,1:T(8,128)(2,1)S(1)}, bf16[1,128,8,256]{3,2,0,1:T(8,128)(2,1)}, u32[]{:S(2)}) copy-start(bf16[1,128,8,256]{3,2,0,1:T(8,128)(2,1)} %copy-done.5) | copy-start | bytes 1572868
  118.0 0.8 copy-start.7
  120.0 20.4 %all-to-all-start.4 = ((bf16[1,4,256,256]{3,1,0,2:T(4,128)(2,1)}), bf16[1,4,256,256]{3,1,0,2:T(4,128)(2,1)}, u32[]{:S(2)}, u32[]{:S(2)}) async-start(bf16[1,4,256,256]{3,1,0,2:T(4,128)(2,1)} %copy.114), calls=%async_computation.4 | async-start | bytes 1048576 | tf_op jit(solution)/shard_map/all_to_all | solution.py:137
  130.6 17.9 %copy-start.9 = (bf16[1,8,256,128]{3,2,1,0:T(8,128)(2,1)S(1)}, bf16[1,8,256,128]{3,2,1,0:T(8,128)(2,1)}, u32[]{:S(2)}) copy-start(bf16[1,8,256,128]{3,2,1,0:T(8,128)(2,1)} %param.8) | copy-start | bytes 1572868
  140.3 19.7 %all-to-all-start.5 = ((bf16[1,4,256,256]{3,1,0,2:T(4,128)(2,1)}), bf16[1,4,256,256]{3,1,0,2:T(4,128)(2,1)}, u32[]{:S(2)}, u32[]{:S(2)}) async-start(bf16[1,4,256,256]{3,1,0,2:T(4,128)(2,1)} %copy.119), calls=%async_computation.5 | async-start | bytes 1048576 | tf_op jit(solution)/shard_map/all_to_all | solution.py:138
  148.2 393.4 %all-reduce.4.cloned.1.call-start = ((), (), s32[]{:S(2)}) async-start(), calls=%async_computation.6 | async-start | bytes 786432 | tf_op jit(solution)/shard_map/psum | solution.py:145
  148.5 2.3 copy-start.4
  162.3 2.6 copy-start.2
  167.9 0.9 copy-start.13
  171.0 1.0 copy-start.10
  172.5 1.4 copy-start.11
  542.7 0.9 copy-start.14
Sparse Core Ops, SparseCore 0:
  277.8 263.8 all-reduce.3
where the time goes:
time: 552 us; the launch traced here: 551 us
  waiting for transfers between devices  304 us (55%)
  blocking collectives  144 us (26%)
  starting transfers between devices  37.8 us (7%)
  local copies, waits for them, and re-layouts  20.6 us (4%)
  matrix products  16.2 us (3%)
  between operations  15.1 us (3%)
  other arithmetic  13.2 us (2%)
    psum x1, waiting for transfers between devices, per_device(): lax.psum((w_in_part, gain_in_part, w_out_part, gain_out_part), ('dp', 'da...  264 us
    psum x1, blocking collectives, per_device(): lax.psum((w_in_part, gain_in_part, w_out_part, gain_out_part), ('dp', 'da...  102 us
    all_to_all x1, blocking collectives, per_device(): lax.all_to_all(channel_major(grad_product), 'dap', split_axis=1, concat_a...  21.5 us
    all_to_all x1, blocking collectives, per_device(): lax.all_to_all(channel_major(right), 'dap', split_axis=1, concat_axis=2,...  20.9 us
    all_to_all x1, waiting for transfers between devices, per_device(): lax.all_to_all(channel_major(left), 'dap', split_axis=1, concat_axis=2, t...  13.9 us
    all_to_all x1, starting transfers between devices, per_device(): lax.all_to_all(channel_major(left), 'dap', split_axis=1, concat_axis=2, t...  13.7 us
    all_to_all x1, waiting for transfers between devices, per_device(): lax.all_to_all(product_cols, 'dap', split_axis=2, concat_axis=1, tiled=True)  11.4 us
  transfers between devices with their start and end apart: 5, of which 5 were waited for; matrix products, arithmetic and copies ran while one was open for 2% of the time, Pallas kernels for 0%

commit v1 on v0

--- a/solution.py
+++ b/solution.py
@@ -103,6 +103,20 @@
     return (grad_pair, w_in_part, gain_in_part)
 
 
+def exchange(values, axis):
+    return lax.all_to_all(values, axis, split_axis=0, concat_axis=0, tiled=True)
+
+
+def summed_everywhere(parts):
+    inner, outer = lax.axis_size("dap"), lax.axis_size("dp")
+    pieces = exchange(parts.reshape(inner, -1, 128), "dap")
+    piece = jnp.sum(pieces, axis=0)
+    pieces = exchange(jnp.broadcast_to(piece[None], (outer,) + piece.shape), "dp")
+    piece = jnp.sum(pieces, axis=0)
+    pieces = exchange(jnp.broadcast_to(piece[None], (inner,) + piece.shape), "dap")
+    return pieces.reshape(parts.shape)
+
+
 def per_device(pair, cotangent, lengths, w_in, gain_in, w_out, gain_out):
     blocks, rows, width, channels = pair.shape
     row_ids = lax.axis_index("dap") * rows + lax.iota(jnp.int32, rows)
@@ -111,10 +125,9 @@
     column_mask = (column_ids[None, :] < lengths[:, None]).astype(jnp.float32)
     cell_mask = row_mask[:, :, None, None] * column_mask[:, None, :, None]
     saved, out_gate, left, right = project(pair, cell_mask, w_in, gain_in)
-    left_cols, right_cols = (
-        lax.all_to_all(channel_major(left), "dap", split_axis=1, concat_axis=2, tiled=True),
-        lax.all_to_all(channel_major(right), "dap", split_axis=1, concat_axis=2, tiled=True),
-    )
+    both = jnp.concatenate([channel_major(left), channel_major(right)], axis=0)
+    both = lax.all_to_all(both, "dap", split_axis=1, concat_axis=2, tiled=True)
+    left_cols, right_cols = both[:blocks], both[blocks:]
     product_cols = jnp.einsum(
         "bcik,bcjk->bcij", left_cols, right_cols, preferred_element_type=jnp.float32
     ).astype(jnp.bfloat16)
@@ -133,18 +146,19 @@
     grad_right_cols = jnp.einsum(
         "bcij,bcik->bcjk", grad_cols, left_cols, preferred_element_type=jnp.float32
     ).astype(jnp.bfloat16)
-    grad_left_major, grad_right_major = (
-        lax.all_to_all(grad_left_cols, "dap", split_axis=2, concat_axis=1, tiled=True),
-        lax.all_to_all(grad_right_cols, "dap", split_axis=2, concat_axis=1, tiled=True),
-    )
+    both = jnp.concatenate([grad_left_cols, grad_right_cols], axis=0)
+    both = lax.all_to_all(both, "dap", split_axis=2, concat_axis=1, tiled=True)
+    grad_left_major, grad_right_major = both[:blocks], both[blocks:]
     grad_left = channel_minor(grad_left_major)
     grad_right = channel_minor(grad_right_major)
     grad_pair, w_in_part, gain_in_part = input_backward(
         grad_left, grad_right, grad_gate, saved, cell_mask, w_in, gain_in
     )
-    w_in_total, gain_in_total, w_out_total, gain_out_total = lax.psum(
-        (w_in_part, gain_in_part, w_out_part, gain_out_part), ("dp", "dap")
-    )
+    parts = jnp.concatenate([w_in_part, w_out_part], axis=1)
+    totals = summed_everywhere(parts)
+    w_in_total, w_out_total = totals[:, : 5 * 128], totals[:, 5 * 128 :]
+    gain_in_total = jnp.sum(w_in.astype(jnp.float32) * w_in_total, axis=1) / gain_in
+    gain_out_total = jnp.sum(w_out.astype(jnp.float32) * w_out_total, axis=1) / gain_out
     factor = 1.0 / (width * math.sqrt(blocks * lax.axis_size("dp")))
     return (
         grad_pair,

time: 552 us -> 227 us (0.41)
  waiting for transfers between devices: 304 us -> 59.8 us
  blocking collectives: 144 us -> 59.2 us
  between operations: 15.1 us -> 1.92 us
  local copies, waits for them, and re-layouts: 20.6 us -> 28.1 us
    psum x1 -> x0, waiting for transfers between devices: 264 us -> none  [per_device(): lax.psum((w_in_part, gain_in_part, w_out_part, gain_out_part), ('dp', 'da...]
    psum x1 -> x0, blocking collectives: 102 us -> none  [per_device(): lax.psum((w_in_part, gain_in_part, w_out_part, gain_out_part), ('dp', 'da...]
    all_to_all x3 -> x4, waiting for transfers between devices: 28.9 us -> 47.6 us  [the longest x3 25.7 us: exchange(): return lax.all_to_all(values, axis, split_axis=0, concat_axis=0, tiled=True)]
    all_to_all x1, blocking collectives: 20.9 us -> 38.3 us  [per_device(): both = lax.all_to_all(both, 'dap', split_axis=1, concat_axis=2, tiled=True)]
    all_to_all x3 -> x4, starting transfers between devices: 29.6 us -> 34.5 us  [the longest x3 25.5 us: exchange(): return lax.all_to_all(values, axis, split_axis=0, concat_axis=0, tiled=True)]
  transfers between devices with their start and end apart: 5 -> 5, of which waited for: 5 -> 5; matrix products, arithmetic and copies ran while one was open for 2% -> 5% of each run, Pallas kernels for 0% -> 0%
where the time goes in v1:
time: 227 us; the launch traced here: 225 us
  waiting for transfers between devices  59.8 us (26%)
  blocking collectives  59.2 us (26%)
  starting transfers between devices  43 us (19%)
  local copies, waits for them, and re-layouts  28.1 us (12%)
  matrix products  18.8 us (8%)
  other arithmetic  14 us (6%)
    all_to_all x1, blocking collectives, per_device(): both = lax.all_to_all(both, 'dap', split_axis=1, concat_axis=2, tiled=True)  38.3 us
    all_to_all x3, waiting for transfers between devices, exchange(): return lax.all_to_all(values, axis, split_axis=0, concat_axis=0, tiled=True)  25.7 us
    all_to_all x3, starting transfers between devices, exchange(): return lax.all_to_all(values, axis, split_axis=0, concat_axis=0, tiled=True)  25.5 us
    all_to_all x1, waiting for transfers between devices, per_device(): both = lax.all_to_all(both, 'dap', split_axis=2, concat_axis=1, tiled=True)  21.9 us
    all_to_all x1, blocking collectives, per_device(): lax.all_to_all(channel_major(grad_product), 'dap', split_axis=1, concat_a...  20.9 us
    all_to_all x1, waiting for transfers between devices, per_device(): lax.all_to_all(product_cols, 'dap', split_axis=2, concat_axis=1, tiled=True)  12.2 us
    all_to_all x1, starting transfers between devices, per_device(): both = lax.all_to_all(both, 'dap', split_axis=2, concat_axis=1, tiled=True)  8.98 us
    unnamed x68, local copies, waits for them, and re-layouts  8.73 us
  transfers between devices with their start and end apart: 5, of which 5 were waited for; matrix products, arithmetic and copies ran while one was open for 5% of the time, Pallas kernels for 0%

profile of v1, /device:TPU:1, one launch (start us, length us, event | category | flops | bytes accessed | tf_op | source)
XLA Modules:
  0.0 224.9 jit_solution(8432179288527191233)
XLA Ops:
  0.6 1.2 copy.137
  2.9 1.6 fusion.4
  5.3 1.5 fusion.6
  7.6 1.9 fusion.46
  9.6 1.7 copy.142
  11.4 38.3 %all_to_all.69 = bf16[2,128,8,256]{3,2,0,1:T(8,128)(2,1)S(1)} all-to-all(bf16[2,128,8,256]{3,2,0,1:T(8,128)(2,1)} %copy.142), channel_id=1, replica_groups=mesh['dp'=16,'dap'=32] {'dap'}, dimensions={1} | all-to-all | bytes 2097152 | tf_op jit(solution)/shard_map/all_to_all | solution.py:129
  50.7 1.2 copy.146
  51.9 8.6 %all-to-all-start.1 = ((bf16[1,4,256,256]{3,1,0,2:T(4,128)(2,1)}), bf16[1,4,256,256]{3,1,0,2:T(4,128)(2,1)S(1)}, u32[]{:S(2)}, u32[]{:S(2)}) async-start(bf16[1,4,256,256]{3,1,0,2:T(4,128)(2,1)} %copy.146), calls=%async_computation.1 | async-start | bytes 1048576 | tf_op jit(solution)/shard_map/all_to_all | solution.py:135
  60.5 1.5 fusion.8
  62.0 12.2 %all-to-all-done.1 = bf16[1,4,256,256]{3,1,0,2:T(4,128)(2,1)S(1)} async-done(((bf16[1,4,256,256]{3,1,0,2:T(4,128)(2,1)}), bf16[1,4,256,256]{3,1,0,2:T(4,128)(2,1)S(1)}, u32[]{:S(2)}, u32[]{:S(2)}) %all-to-all-start.1) | async-done | bytes 524320 | tf_op jit(solution)/shard_map/all_to_all | solution.py:135
  75.4 1.6 reshape.307
  78.4 1.3 fusion.42
  79.7 1.3 reduce_sum.112
  81.0 1.5 fusion.49
  82.8 20.9 %all_to_all.70 = bf16[1,128,8,256]{3,2,0,1:T(8,128)(2,1)S(1)} all-to-all(bf16[1,128,8,256]{3,2,0,1:T(8,128)(2,1)S(1)} %copy.149), channel_id=1, replica_groups=mesh['dp'=16,'dap'=32] {'dap'}, dimensions={1} | all-to-all | bytes 1048576 | tf_op jit(solution)/shard_map/all_to_all | solution.py:140
  104.5 1.8 copy.152
  106.3 9.0 %all-to-all-start.3 = ((bf16[2,4,256,256]{3,1,0,2:T(4,128)(2,1)}), bf16[2,4,256,256]{3,1,0,2:T(4,128)(2,1)}, u32[]{:S(2)}, u32[]{:S(2)}) async-start(bf16[2,4,256,256]{3,1,0,2:T(4,128)(2,1)} %copy.152), calls=%async_computation.3 | async-start | bytes 2097152 | tf_op jit(solution)/shard_map/all_to_all | solution.py:150
  115.3 2.5 %fusion.19 = bf16[8,256,128]{2,1,0:T(8,128)(2,1)} fusion(bf16[1,8,256,128]{3,2,1,0:T(8,128)(2,1)S(1)} %copy-done.6, f32[8,256,128]{2,1,0:T(8,128)} %fusion.8, bf16[128,128]{1,0:T(8,128)(2,1)S(1)} %copy-done.19, f32[1,128,8,256]{3,1,2,0:T(8,128)S(1)} %reshape.307, f32[128]{0:T(128)S(1)} %copy-done.30, f32[8,256]{1,0:T(8,128)S(1)} %add_rsqrt_fusion, ...), kind=kOutput, calls=%fused_computation.34 | convolution fusion | flops 69730304 | bytes 3195392 | tf_op jit(solution)/shard_map/dot_general | solution.py:69
  117.8 21.9 %all-to-all-done.3 = bf16[2,4,256,256]{3,1,0,2:T(4,128)(2,1)} async-done(((bf16[2,4,256,256]{3,1,0,2:T(4,128)(2,1)}), bf16[2,4,256,256]{3,1,0,2:T(4,128)(2,1)}, u32[]{:S(2)}, u32[]{:S(2)}) %all-to-all-start.3) | async-done | bytes 1048608 | tf_op jit(solution)/shard_map/all_to_all | solution.py:150
  139.7 1.4 copy.218
  141.2 1.2 slice_convert_fusion
  143.5 2.6 %copy.155 = f32[1,128,8,256]{1,3,2,0:T(8,128)} copy(f32[1,128,8,256]{3,2,1,0:T(8,128)} %bitcast.275) | data formatting | bytes 2097152 | tf_op jit(solution)/shard_map/convert_element_type | solution.py:83
  146.1 2.4 %copy.156 = f32[1,32,4,8,256]{4,3,2,1,0:T(8,128)} copy(f32[1,32,4,8,256]{4,3,1,2,0:T(8,128)} %get-tuple-element.34) | data formatting | bytes 2097152 | tf_op jit(solution)/shard_map/convert_element_type | solution.py:84
  148.4 2.6 %copy.157 = f32[1,128,8,256]{1,3,2,0:T(8,128)} copy(f32[1,128,8,256]{3,2,1,0:T(8,128)} %bitcast.276) | data formatting | bytes 2097152 | tf_op jit(solution)/shard_map/convert_element_type | solution.py:84
  151.0 3.3 %fusion.53 = (bf16[8,256,128]{2,1,0:T(8,128)(2,1)S(1)}, bf16[8,256,128]{2,1,0:T(8,128)(2,1)S(1)}, bf16[8,256,128]{2,1,0:T(8,128)(2,1)S(1)}, bf16[8,256,128]{2,1,0:T(8,128)(2,1)S(1)}) fusion(f32[8,256,128]{2,1,0:T(8,128)} %fusion.6, f32[8,256,128]{2,1,0:T(8,128)} %copy-done, f32[1,128,8,256]{1,3,2,0:T(8,128)} %copy.157, ...), kind=kLoop, calls=%fused_computation.92 | loop fusion | flops 4194304 | bytes 8396800 | tf_op jit(solution)/shard_map/reshape.66
  160.0 8.4 %all-to-all-start.4 = ((f32[32,24,128]{2,1,0:T(8,128)}), f32[32,24,128]{2,1,0:T(8,128)S(1)}, u32[]{:S(2)}, u32[]{:S(2)}) async-start(f32[32,24,128]{2,1,0:T(8,128)} %reshape.303), calls=%async_computation.4 | async-start | bytes 786432 | tf_op jit(solution)/shard_map/all_to_all | solution.py:107
  170.6 8.3 %all-to-all-done.4 = f32[32,24,128]{2,1,0:T(8,128)S(1)} async-done(((f32[32,24,128]{2,1,0:T(8,128)}), f32[32,24,128]{2,1,0:T(8,128)S(1)}, u32[]{:S(2)}, u32[]{:S(2)}) %all-to-all-start.4) | async-done | bytes 393248 | tf_op jit(solution)/shard_map/all_to_all | solution.py:107
  179.7 12.1 %all-to-all-start.5 = ((f32[16,24,128]{2,1,0:T(8,128)}), f32[16,24,128]{2,1,0:T(8,128)S(1)}, u32[]{:S(2)}, u32[]{:S(2)}) async-start(f32[16,24,128]{2,1,0:T(8,128)} %broadcast_in_dim.4), calls=%async_computation.5 | async-start | bytes 393216 | tf_op jit(solution)/shard_map/all_to_all | solution.py:107
  194.0 8.1 %all-to-all-done.5 = f32[16,24,128]{2,1,0:T(8,128)S(1)} async-done(((f32[16,24,128]{2,1,0:T(8,128)}), f32[16,24,128]{2,1,0:T(8,128)S(1)}, u32[]{:S(2)}, u32[]{:S(2)}) %all-to-all-start.5) | async-done | bytes 196640 | tf_op jit(solution)/shard_map/all_to_all | solution.py:107
  202.9 5.0 %all-to-all-start.6 = ((f32[32,24,128]{2,1,0:T(8,128)}), f32[32,24,128]{2,1,0:T(8,128)S(1)}, u32[]{:S(2)}, u32[]{:S(2)}) async-start(f32[32,24,128]{2,1,0:T(8,128)} %broadcast_in_dim.5), calls=%async_computation.6 | async-start | bytes 786432 | tf_op jit(solution)/shard_map/all_to_all | solution.py:107
  207.9 1.7 fusion.30
  211.7 9.3 %all-to-all-done.6 = f32[32,24,128]{2,1,0:T(8,128)S(1)} async-done(((f32[32,24,128]{2,1,0:T(8,128)}), f32[32,24,128]{2,1,0:T(8,128)S(1)}, u32[]{:S(2)}, u32[]{:S(2)}) %all-to-all-start.6) | async-done | bytes 393248 | tf_op jit(solution)/shard_map/all_to_all | solution.py:107
  (116 shorter events, 24.9 us)
Async XLA Ops:
  2.0 0.9 copy-start.17
  2.9 57.6 %copy-start.21 = (f32[8,256]{1,0:T(8,128)}, f32[8,256]{1,0:T(8,128)S(1)}, u32[]{:S(2)}) copy-start(f32[8,256]{1,0:T(8,128)S(1)} %add_rsqrt_fusion.1) | copy-start | bytes 24580
  5.3 2.3 %copy-start = (f32[8,256,128]{2,1,0:T(8,128)}, f32[8,256,128]{2,1,0:T(8,128)S(1)}, u32[]{:S(2)}) copy-start(f32[8,256,128]{2,1,0:T(8,128)S(1)} %fusion.73) | copy-start | bytes 3145732
  49.9 0.8 copy-start.3
  51.9 22.3 %all-to-all-start.1 = ((bf16[1,4,256,256]{3,1,0,2:T(4,128)(2,1)}), bf16[1,4,256,256]{3,1,0,2:T(4,128)(2,1)S(1)}, u32[]{:S(2)}, u32[]{:S(2)}) async-start(bf16[1,4,256,256]{3,1,0,2:T(4,128)(2,1)} %copy.146), calls=%async_computation.1 | async-start | bytes 1048576 | tf_op jit(solution)/shard_map/all_to_all | solution.py:135
  77.0 1.2 copy-start.1
  77.1 1.3 copy-start.5
  77.1 1.3 copy-start.19
  77.3 1.1 copy-start.30
  78.4 36.9 %copy-start.24 = (f32[8,256]{1,0:T(8,128)}, f32[8,256]{1,0:T(8,128)S(1)}, u32[]{:S(2)}) copy-start(f32[8,256]{1,0:T(8,128)S(1)} %add_rsqrt_fusion) | copy-start | bytes 24580
  82.8 20.9 %copy-start.4 = (bf16[1,4,32,8,256]{4,3,1,2,0:T(8,128)(2,1)S(1)}, bf16[1,4,32,8,256]{4,3,1,2,0:T(8,128)(2,1)}, u32[]{:S(2)}) copy-start(bf16[1,4,32,8,256]{4,3,1,2,0:T(8,128)(2,1)} %copy-done.3) | copy-start | bytes 1572868
  106.3 9.0 %copy-start.6 = (bf16[1,8,256,128]{3,2,1,0:T(8,128)(2,1)S(1)}, bf16[1,8,256,128]{3,2,1,0:T(8,128)(2,1)}, u32[]{:S(2)}) copy-start(bf16[1,8,256,128]{3,2,1,0:T(8,128)(2,1)} %param.8) | copy-start | bytes 1572868
  106.3 33.4 %all-to-all-start.3 = ((bf16[2,4,256,256]{3,1,0,2:T(4,128)(2,1)}), bf16[2,4,256,256]{3,1,0,2:T(4,128)(2,1)}, u32[]{:S(2)}, u32[]{:S(2)}) async-start(bf16[2,4,256,256]{3,1,0,2:T(4,128)(2,1)} %copy.152), calls=%async_computation.3 | async-start | bytes 2097152 | tf_op jit(solution)/shard_map/all_to_all | solution.py:150
  151.0 3.4 %copy-start.22 = (f32[8,256]{1,0:T(8,128)S(1)}, f32[8,256]{1,0:T(8,128)}, u32[]{:S(2)}) copy-start(f32[8,256]{1,0:T(8,128)} %copy-done.21) | copy-start | bytes 24580
  154.3 1.1 copy-start.7
  154.4 1.6 copy-start.11
  154.4 2.0 copy-start.13
  154.4 2.0 copy-start.9
  156.4 1.0 copy-start.15
  157.4 1.2 copy-start.2
  157.4 1.2 copy-start.25
  157.4 1.2 copy-start.31
  160.0 8.4 %copy-start.8 = (bf16[8,256,128]{2,1,0:T(8,128)(2,1)S(1)}, bf16[8,256,128]{2,1,0:T(8,128)(2,1)}, u32[]{:S(2)}) copy-start(bf16[8,256,128]{2,1,0:T(8,128)(2,1)} %copy-done.7) | copy-start | bytes 1572868
  160.0 18.9 %all-to-all-start.4 = ((f32[32,24,128]{2,1,0:T(8,128)}), f32[32,24,128]{2,1,0:T(8,128)S(1)}, u32[]{:S(2)}, u32[]{:S(2)}) async-start(f32[32,24,128]{2,1,0:T(8,128)} %reshape.303), calls=%async_computation.4 | async-start | bytes 786432 | tf_op jit(solution)/shard_map/all_to_all | solution.py:107
  168.4 1.1 copy-start.14
  170.6 21.1 %copy-start.12 = (bf16[8,256,128]{2,1,0:T(8,128)(2,1)S(1)}, bf16[8,256,128]{2,1,0:T(8,128)(2,1)}, u32[]{:S(2)}) copy-start(bf16[8,256,128]{2,1,0:T(8,128)(2,1)} %copy-done.11) | copy-start | bytes 1572868
  179.7 22.4 %all-to-all-start.5 = ((f32[16,24,128]{2,1,0:T(8,128)}), f32[16,24,128]{2,1,0:T(8,128)S(1)}, u32[]{:S(2)}, u32[]{:S(2)}) async-start(f32[16,24,128]{2,1,0:T(8,128)} %broadcast_in_dim.4), calls=%async_computation.5 | async-start | bytes 393216 | tf_op jit(solution)/shard_map/all_to_all | solution.py:107
  191.7 1.1 copy-start.10
  202.1 5.8 %copy-start.16 = (bf16[8,256,128]{2,1,0:T(8,128)(2,1)S(1)}, bf16[8,256,128]{2,1,0:T(8,128)(2,1)}, u32[]{:S(2)}) copy-start(bf16[8,256,128]{2,1,0:T(8,128)(2,1)} %fusion.19) | copy-start | bytes 1572868
  202.9 5.0 %copy-start.23 = (f32[8,256]{1,0:T(8,128)S(1)}, f32[8,256]{1,0:T(8,128)}, u32[]{:S(2)}) copy-start(f32[8,256]{1,0:T(8,128)} %copy-done.21) | copy-start | bytes 24580
  202.9 18.2 %all-to-all-start.6 = ((f32[32,24,128]{2,1,0:T(8,128)}), f32[32,24,128]{2,1,0:T(8,128)S(1)}, u32[]{:S(2)}, u32[]{:S(2)}) async-start(f32[32,24,128]{2,1,0:T(8,128)} %broadcast_in_dim.5), calls=%async_computation.6 | async-start | bytes 786432 | tf_op jit(solution)/shard_map/all_to_all | solution.py:107
  211.7 9.4 %copy-start.18 = (bf16[128,640]{1,0:T(8,128)(2,1)S(1)}, bf16[128,640]{1,0:T(8,128)(2,1)}, u32[]{:S(2)}) copy-start(bf16[128,640]{1,0:T(8,128)(2,1)} %param.10) | copy-start | bytes 491524
  (6 other events, 4.2 us)

commit v2 on v0

v2 whole, which is shorter than its diff:
```python
import math

import jax
import jax.numpy as jnp
from jax import lax
from jax.experimental import pallas as pl
from jax.experimental.pallas import tpu as pltpu
from jax.sharding import PartitionSpec as P

EPSILON = 1e-05
LANES = 128
SUB = 8
BF16 = jnp.bfloat16
F32 = jnp.float32


def dot(first, second, dims):
    return lax.dot_general(first, second, (dims, ((), ())), preferred_element_type=F32)


NN = ((1,), (0,))
NT = ((1,), (1,))
TN = ((0,), (0,))


def sigmoid(x):
    return 0.5 * jnp.tanh(0.5 * x) + 0.5


def identity(size):
    rows = lax.broadcasted_iota(jnp.int32, (size, size), 0)
    columns = lax.broadcasted_iota(jnp.int32, (size, size), 1)
    return (rows == columns).astype(F32).astype(BF16)


def column(gain_row, size):
    return jnp.transpose(jnp.broadcast_to(gain_row, (size, size)))


def norm_sublanes(x):
    scale = 1.0 / x.shape[0]
    centred = x - jnp.sum(x, axis=0, keepdims=True) * scale
    variance = jnp.sum(centred * centred, axis=0, keepdims=True) * scale
    inverse = lax.rsqrt(variance + EPSILON)
    return centred * inverse, inverse


def row_of_masks(scalars_ref, i, width):
    length = scalars_ref[0]
    columns = lax.broadcasted_iota(jnp.int32, (1, width), 1)
    keep = jnp.logical_and(columns < length, scalars_ref[1] + i < length)
    return keep.astype(F32)


def wide(gain, width):
    return jnp.concatenate([gain] * (width // gain.shape[1]), axis=1)


def project_kernel(scalars_ref, pair_ref, w_ref, gain_ref, send_ref, norm_ref, wt_ref, stage_ref):
    rows, width, channels = pair_ref.shape
    eye = identity(channels)
    gain = wide(column(gain_ref[...], channels), width)
    for n in range(4):
        block = w_ref[:, n * channels : (n + 1) * channels]
        wt_ref[n] = jnp.transpose(block.astype(F32)).astype(BF16)
    for i in range(rows):
        hat, _ = norm_sublanes(dot(eye, pair_ref[i], NT))
        norm = (hat * gain).astype(BF16)
        norm_ref[i] = norm
        mask = row_of_masks(scalars_ref, i, width)
        for side in range(2):
            value = dot(wt_ref[2 * side], norm, NN)
            gate = sigmoid(dot(wt_ref[2 * side + 1], norm, NN))
            value = mask * gate * value
            for half in range(width // LANES):
                stage_ref[side, half, pl.ds(i, channels, stride=rows), :] = value[
                    :, half * LANES : (half + 1) * LANES
                ]
    peers = send_ref.shape[0]
    for side in range(2):
        for half in range(width // LANES):
            send_ref[:, side, half] = (
                stage_ref[side, half].reshape(peers, -1, LANES).astype(BF16)
            )


def regroup(block, group):
    peers, _, lanes = block.shape
    block = block.astype(F32).reshape(peers, group, SUB, lanes)
    return [block[:, c].reshape(peers * SUB, lanes).astype(BF16) for c in range(group)]


def product_kernel(got_ref, send_ref, held_ref, stage_ref):
    peers, _, halves, packed, _ = got_ref.shape
    group = packed // SUB
    for side in range(2):
        for half in range(halves):
            for c, block in enumerate(regroup(got_ref[:, side, half], group)):
                held_ref[side, half, c] = block
    for c in range(group):
        for out in range(halves):
            right_rows = pl.ds(out * LANES, LANES)
            total = dot(held_ref[0, 0, c], held_ref[1, 0, c, right_rows, :], NT)
            for half in range(1, halves):
                total = total + dot(held_ref[0, half, c], held_ref[1, half, c, right_rows, :], NT)
            stage_ref[out, :, c * SUB : (c + 1) * SUB, :] = total.reshape(peers, SUB, LANES)
    for out in range(halves):
        send_ref[:, out] = stage_ref[out].astype(BF16)


def output_ahead_kernel(
    scalars_ref, norm_ref, cotangent_ref, w_ref, w_out_ref, gain_ref,
    upstream_ref, factors_ref, gated_ref, slope_ref, wt_ref,
):
    rows, width, channels = cotangent_ref.shape
    eye = identity(channels)
    gain = wide(column(gain_ref[...], channels), width)
    for n in range(5):
        block = w_ref[:, n * channels : (n + 1) * channels]
        wt_ref[n] = jnp.transpose(block.astype(F32)).astype(BF16)
    w_out = w_out_ref[...]
    for i in range(rows):
        norm = norm_ref[i]
        cotangent = dot(eye, cotangent_ref[i], NT)
        out_gate = sigmoid(dot(wt_ref[4], norm, NN))
        gated = cotangent * out_gate
        slope_ref[i] = gated * (1.0 - out_gate)
        gated = gated.astype(BF16)
        gated_ref[i] = gated
        upstream = dot(w_out, gated, NN) * gain
        upstream = upstream - jnp.sum(upstream, axis=0, keepdims=True) * (1.0 / channels)
        for half in range(width // LANES):
            upstream_ref[half, pl.ds(i, channels, stride=rows), :] = upstream[
                :, half * LANES : (half + 1) * LANES
            ]
        mask = row_of_masks(scalars_ref, i, width)
        for side in range(2):
            value = dot(wt_ref[2 * side], norm, NN)
            gate = sigmoid(dot(wt_ref[2 * side + 1], norm, NN))
            masked = mask * gate
            factors_ref[i, 2 * side] = masked
            factors_ref[i, 2 * side + 1] = masked * value * (1.0 - gate)


def norm_blocks(block):
    product = block.astype(F32).reshape(-1, SUB, block.shape[-1])
    return norm_sublanes(product)


def output_back_kernel(got_ref, upstream_ref, send_ref):
    peers, halves, packed, lanes = got_ref.shape
    for half in range(halves):
        hat, inverse = norm_blocks(got_ref[:, half])
        upstream = upstream_ref[half].reshape(hat.shape)
        second = jnp.sum(upstream * hat, axis=0, keepdims=True) * (1.0 / hat.shape[0])
        grad = inverse * (upstream - hat * second)
        send_ref[:, half] = grad.reshape(peers, packed, lanes).astype(BF16)


def output_weights_kernel(
    got_ref, norm_ref, gated_ref, slope_ref, w_out_ref, gain_ref,
    gate_grad_ref, sums_ref, stage_ref,
):
    halves = got_ref.shape[1]
    rows, channels, _ = norm_ref.shape
    gain = column(gain_ref[...], channels)
    w_out_t = jnp.transpose(w_out_ref[...].astype(F32)).astype(BF16)
    for half in range(halves):
        hat, _ = norm_blocks(got_ref[:, half])
        stage_ref[half] = hat.reshape(-1, LANES)
    w_out_sum = jnp.zeros((channels, channels), F32)
    w_gate_sum = jnp.zeros((channels, channels), F32)
    for i in range(rows):
        for half in range(halves):
            lanes = slice(half * LANES, (half + 1) * LANES)
            hat = stage_ref[half, pl.ds(i, channels, stride=rows), :]
            prod_norm = (hat * gain).astype(BF16)
            update = dot(w_out_t, prod_norm, NN)
            gate_grad = (slope_ref[i, :, lanes] * update).astype(BF16)
            gate_grad_ref[i, :, lanes] = gate_grad
            w_out_sum = w_out_sum + dot(prod_norm, gated_ref[i, :, lanes], NT)
            w_gate_sum = w_gate_sum + dot(norm_ref[i, :, lanes], gate_grad, NT)
    sums_ref[0] = w_gate_sum
    sums_ref[1] = w_out_sum


def operands_back_kernel(got_ref, held_ref, send_ref, stage_ref):
    peers, halves, packed, _ = got_ref.shape
    group = packed // SUB
    blocks = [regroup(got_ref[:, half], group) for half in range(halves)]
    for c in range(group):
        for out in range(halves):
            left = None
            for half in range(halves):
                rows = pl.ds(half * LANES, LANES)
                part = dot(blocks[half][c], held_ref[1, out, c, rows, :], NN)
                left = part if left is None else left + part
            stage_ref[0, out, :, c * SUB : (c + 1) * SUB, :] = left.reshape(peers, SUB, LANES)
            for half in range(halves):
                right = dot(blocks[half][c], held_ref[0, out, c], TN)
                span = peers // halves
                stage_ref[1, out, half * span : (half + 1) * span, c * SUB : (c + 1) * SUB, :] = (
                    right.reshape(span, SUB, LANES)
                )
    for side in range(2):
        for out in range(halves):
            send_ref[:, side, out] = stage_ref[side, out].astype(BF16)


def input_weights_kernel(
    got_ref, factors_ref, norm_ref, sums_ref, parts_ref, pieces_ref, stage_ref
):
    halves = got_ref.shape[2]
    rows, channels, _ = norm_ref.shape
    for side in range(2):
        for half in range(halves):
            stage_ref[side, half] = got_ref[:, side, half].astype(F32).reshape(-1, LANES)
    totals = [jnp.zeros((channels, 2 * channels), F32) for _ in range(2)]
    for i in range(rows):
        for half in range(halves):
            lanes = slice(half * LANES, (half + 1) * LANES)
            norm = norm_ref[i, :, lanes]
            for side in range(2):
                grad = stage_ref[side, half, pl.ds(i, channels, stride=rows), :]
                pieces = jnp.concatenate(
                    [
                        (grad * factors_ref[i, 2 * side, :, lanes]).astype(BF16),
                        (grad * factors_ref[i, 2 * side + 1, :, lanes]).astype(BF16),
                    ],
                    axis=0,
                )
                pieces_ref[i, 2 * side * channels : 2 * (side + 1) * channels, lanes] = pieces
                totals[side] = totals[side] + dot(norm, pieces, NT)
    for side in range(2):
        for n in range(2):
            parts_ref[2 * side + n] = totals[side][:, n * channels : (n + 1) * channels]
    parts_ref[4] = sums_ref[0]
    parts_ref[5] = sums_ref[1]


def input_back_kernel(pieces_ref, gate_grad_ref, pair_ref, w_ref, gain_ref, out_ref):
    rows, width, channels = pair_ref.shape
    eye = identity(channels)
    gain = wide(column(gain_ref[...], channels), width)
    for i in range(rows):
        hat, inverse = norm_sublanes(dot(eye, pair_ref[i], NT))
        grad = dot(w_ref[:, : 4 * channels], pieces_ref[i], NN)
        grad = grad + dot(w_ref[:, 4 * channels :], gate_grad_ref[i], NN)
        grad = grad * gain
        first = jnp.sum(grad, axis=0, keepdims=True) * (1.0 / channels)
        second = jnp.sum(grad * hat, axis=0, keepdims=True) * (1.0 / channels)
        grad = inverse * (grad - first - hat * second)
        out_ref[i] = jnp.transpose(grad).astype(BF16)


def fold_kernel(got_ref, send_ref):
    total = jnp.sum(got_ref[...].astype(F32), axis=0)
    send_ref[...] = jnp.broadcast_to(total[None], send_ref.shape).astype(send_ref.dtype)


def finish_kernel(
    factor, got_ref, w_ref, gain_in_ref, w_out_ref, gain_out_ref,
    w_in_grad_ref, gain_in_grad_ref, w_out_grad_ref, gain_out_grad_ref,
):
    channels = w_out_ref.shape[0]
    dots = jnp.zeros((channels, channels), F32)
    for n in range(5):
        total = got_ref[n] * factor
        lanes = slice(n * channels, (n + 1) * channels)
        w_in_grad_ref[:, lanes] = total
        dots = dots + total * w_ref[:, lanes].astype(F32)
    gain_in_grad_ref[...] = jnp.sum(jnp.transpose(dots), axis=0, keepdims=True) / gain_in_ref[...]
    total = got_ref[5] * factor
    w_out_grad_ref[...] = total
    dots = total * w_out_ref[...].astype(F32)
    gain_out_grad_ref[...] = jnp.sum(jnp.transpose(dots), axis=0, keepdims=True) / gain_out_ref[...]


def exchange(values, axis):
    return lax.all_to_all(values, axis, split_axis=0, concat_axis=0, tiled=True)


def call(kernel, name, out_shape, scratch=(), scalars=False, inputs=1, flops=10**9):
    in_specs = [pl.BlockSpec(memory_space=pltpu.VMEM)] * inputs
    if scalars:
        in_specs[0] = pl.BlockSpec(memory_space=pltpu.SMEM)
    return pl.pallas_call(
        kernel,
        out_shape=[jax.ShapeDtypeStruct(shape, dtype) for shape, dtype in out_shape],
        in_specs=in_specs,
        out_specs=[pl.BlockSpec(memory_space=pltpu.VMEM)] * len(out_shape),
        scratch_shapes=[pltpu.VMEM(shape, dtype) for shape, dtype in scratch],
        compiler_params=pltpu.CompilerParams(vmem_limit_bytes=40 * 2**20),
        cost_estimate=pl.CostEstimate(flops=flops, bytes_accessed=4 * 2**20, transcendentals=0),
        name=name,
    )


def per_device(pair, cotangent, lengths, w_in, gain_in, w_out, gain_out):
    _, rows, width, channels = pair.shape
    inner, outer = lax.axis_size("dap"), lax.axis_size("dp")
    halves, packed = width // LANES, channels // inner * rows
    group = channels // inner
    pair, cotangent = pair[0], cotangent[0]
    gain_in, gain_out = gain_in[None], gain_out[None]
    scalars = jnp.stack([lengths[0], lax.axis_index("dap").astype(jnp.int32) * rows])
    one_side, two_sides = (inner, halves, packed, LANES), (inner, 2, halves, packed, LANES)
    flat = (rows, channels, width)

    send, norm = call(
        project_kernel, "project", [(two_sides, BF16), (flat, BF16)],
        [((4, channels, channels), BF16), ((2, halves, channels * rows, LANES), F32)],
        scalars=True, inputs=4,
    )(scalars, pair, w_in, gain_in)
    got_operands = exchange(send, "dap")
    upstream, factors, gated, slope = call(
        output_ahead_kernel, "output_ahead",
        [
            ((halves, channels * rows, LANES), F32),
            ((rows, 4, channels, width), F32),
            (flat, BF16),
            (flat, F32),
        ],
        [((5, channels, channels), BF16)],
        scalars=True, inputs=6, flops=6 * 10**9,
    )(scalars, norm, cotangent, w_in, w_out, gain_out)

    send, held = call(
        product_kernel, "product",
        [(one_side, BF16), ((2, halves, group, width, LANES), BF16)],
        [((halves, inner, packed, LANES), F32)],
    )(got_operands)
    got_product = exchange(send, "dap")

    (send,) = call(output_back_kernel, "output_back", [(one_side, BF16)], inputs=2)(
        got_product, upstream
    )
    got_grad = exchange(send, "dap")
    gate_grad, sums = call(
        output_weights_kernel, "output_weights",
        [(flat, BF16), ((2, channels, channels), F32)],
        [((halves, channels * rows, LANES), F32)],
        inputs=6, flops=4 * 10**9,
    )(got_product, norm, gated, slope, w_out, gain_out)

    (send,) = call(
        operands_back_kernel, "operands_back", [(two_sides, BF16)],
        [((2, halves, inner, packed, LANES), F32)], inputs=2,
    )(got_grad, held)
    got_operand_grads = exchange(send, "dap")

    parts, pieces = call(
        input_weights_kernel, "input_weights",
        [((6, channels, channels), F32), ((rows, 4 * channels, width), BF16)],
        [((2, halves, channels * rows, LANES), F32)], inputs=4,
    )(got_operand_grads, factors, norm, sums)
    share = 6 * channels // inner
    got = exchange(parts.reshape(inner, share, channels), "dap")
    (pair_grad,) = call(
        input_back_kernel, "input_back", [((rows, width, channels), BF16)], inputs=5,
        flops=6 * 10**9,
    )(pieces, gate_grad, pair, w_in, gain_in)
    (send,) = call(fold_kernel, "fold_inner", [((outer, share, channels), F32)])(got)
    got = exchange(send, "dp")
    (send,) = call(fold_kernel, "fold_outer", [((inner, share, channels), F32)])(got)
    got = exchange(send, "dap").reshape(6, channels, channels)
    factor = 1.0 / (width * math.sqrt(outer))

    def finish(*refs):
        finish_kernel(factor, *refs)

    w_in_grad, gain_in_grad, w_out_grad, gain_out_grad = call(
        finish, "finish",
        [
            ((channels, 5 * channels), F32),
            ((1, channels), F32),
            ((channels, channels), F32),
            ((1, channels), F32),
        ],
        inputs=5,
    )(got, w_in, gain_in, w_out, gain_out)
    return (pair_grad[None], w_in_grad, gain_in_grad[0], w_out_grad, gain_out_grad[0])


def solution(mesh):
    in_specs = (P("dp", "dap", None, None), P("dp", "dap", None, None), P("dp"), P(), P(), P(), P())
    out_specs = (P("dp", "dap", None, None), P(), P(), P(), P())
    return jax.shard_map(
        per_device, mesh=mesh, in_specs=in_specs, out_specs=out_specs, check_vma=False
    )
```

time: 552 us -> 192 us (0.35)
  waiting for transfers between devices: 304 us -> 36.4 us
  blocking collectives: 144 us -> 99.9 us
  Pallas kernels: 0 us -> 17.1 us
  matrix products: 16.2 us -> 0 us
  starting transfers between devices: 37.8 us -> 22 us
  between operations: 15.1 us -> 1.47 us
  other arithmetic: 13.2 us -> 0.08 us
  local copies, waits for them, and re-layouts: 20.6 us -> 13.8 us
    psum x1 -> x0, waiting for transfers between devices: 264 us -> none  [per_device(): lax.psum((w_in_part, gain_in_part, w_out_part, gain_out_part), ('dp', 'da...]
    psum x1 -> x0, blocking collectives: 102 us -> none  [per_device(): lax.psum((w_in_part, gain_in_part, w_out_part, gain_out_part), ('dp', 'da...]
    all_to_all x2 -> x4, blocking collectives: 42.4 us -> 99.9 us  [exchange(): return lax.all_to_all(values, axis, split_axis=0, concat_axis=0, tiled=True)]
    pallas_call x0 -> x11, Pallas kernels: none -> 17.1 us  [the longest x1 3.2 us: per_device(): call(output_ahead_kernel, 'output_ahead', [((halves, channels * rows, LAN...]
    dot_general x21 -> x0, matrix products: 16.2 us -> none  [the longest x5 5.52 us: linear(): jnp.dot(pair_norm, column_block(w_in, index, channels), preferred_element...]
    all_to_all x4 -> x3, starting transfers between devices: 37.6 us -> 22 us  [exchange(): return lax.all_to_all(values, axis, split_axis=0, concat_axis=0, tiled=True)]
    convert_element_type x8 -> x0, local copies, waits for them, and re-layouts: 10.5 us -> none  [the longest x2 3.79 us: input_backward(): right_up = grad_right.astype(jnp.float32) * cell_mask]
    unnamed x37 -> x38, local copies, waits for them, and re-layouts: 7.18 us -> 13.8 us
  transfers between devices with their start and end apart: 5 -> 3, of which waited for: 5 -> 3; matrix products, arithmetic and copies ran while one was open for 2% -> 0% of each run, Pallas kernels for 0% -> 4%
where the time goes in v2:
time: 192 us; the launch traced here: 191 us
  blocking collectives  99.9 us (52%)
  waiting for transfers between devices  36.4 us (19%)
  starting transfers between devices  22 us (11%)
  Pallas kernels  17.1 us (9%)
  local copies, waits for them, and re-layouts  13.8 us (7%)
    all_to_all x4, blocking collectives, exchange(): return lax.all_to_all(values, axis, split_axis=0, concat_axis=0, tiled=True)  99.9 us
    all_to_all x3, waiting for transfers between devices, exchange(): return lax.all_to_all(values, axis, split_axis=0, concat_axis=0, tiled=True)  36.4 us
    all_to_all x3, starting transfers between devices, exchange(): return lax.all_to_all(values, axis, split_axis=0, concat_axis=0, tiled=True)  22 us
    unnamed x38, local copies, waits for them, and re-layouts  13.8 us
  transfers between devices with their start and end apart: 3, of which 3 were waited for; matrix products, arithmetic and copies ran while one was open for 0% of the time, Pallas kernels for 4%

profile of v2, /device:TPU:1, one launch (start us, length us, event | category | flops | bytes accessed | tf_op | source)
XLA Modules:
  0.0 190.8 jit_solution(5067120178231861957)
XLA Ops:
  1.3 0.1 pad_add_fusion.scalars_ref
  1.4 1.0 copy-done.5
  2.4 0.9 copy-done.7
  3.3 0.7 copy-done.10
  4.0 3.2 %project.1 = (bf16[32,2,2,32,128]{4,3,2,1,0:T(8,128)(2,1)S(1)}, bf16[8,128,256]{2,1,0:T(8,128)(2,1)S(1)}) custom-call(s32[2]{0:T(128)S(1)} %pad_add_fusion.scalars_ref, bf16[8,256,128]{2,1,0:T(8,128)(2,1)S(1)} %bitcast.13, bf16[128,640]{1,0:T(8,128)(2,1)S(1)} %copy-done.7, f32[1,128]{1,0:T(1,128)S(1)} %bitcast.15), custom_call_target="tpu_custom_call" | custom-call | flops 1000000000 | bytes 4194304 | tf_op jit(solution)/shard_map/project/pallas_call | solution.py:310
  7.2 38.3 %all_to_all.35.got_ref = bf16[32,2,2,32,128]{4,3,2,1,0:T(8,128)(2,1)S(1)} all-to-all(bf16[32,2,2,32,128]{4,3,2,1,0:T(8,128)(2,1)S(1)} %get-tuple-element.21), channel_id=1, replica_groups=mesh['dp'=16,'dap'=32] {'dap'}, dimensions={0} | all-to-all | bytes 2097152 | tf_op jit(solution)/shard_map/all_to_all | solution.py:280
  45.5 1.4 product.1
  46.8 8.6 %all-to-all-start.1 = ((bf16[32,2,32,128]{3,2,1,0:T(8,128)(2,1)}), bf16[32,2,32,128]{3,2,1,0:T(8,128)(2,1)S(1)}, u32[]{:S(2)}, u32[]{:S(2)}) async-start(bf16[32,2,32,128]{3,2,1,0:T(8,128)(2,1)} %get-tuple-element.22), calls=%async_computation.1 | async-start | bytes 1048576 | tf_op jit(solution)/shard_map/all_to_all | solution.py:280
  55.4 3.2 %output_ahead.1 = (f32[2,1024,128]{2,1,0:T(8,128)S(1)}, f32[8,4,128,256]{3,2,1,0:T(8,128)S(1)}, bf16[8,128,256]{2,1,0:T(8,128)(2,1)S(1)}, f32[8,128,256]{2,1,0:T(8,128)S(1)}) custom-call(s32[2]{0:T(128)S(1)} %pad_add_fusion.scalars_ref, bf16[8,128,256]{2,1,0:T(8,128)(2,1)S(1)} %get-tuple-element.23.norm_ref, bf16[8,256,128]{2,1,0:T(8,128)(2,1)S(1)} %bitcast.12, ...), custom_call_target="tpu_custom_call" | custom-call | flops 6000000000 | bytes 4194304 | tf_op jit(solution)/shard_map/output_ahead/pallas_call | solution.py:316
  58.7 1.9 %copy-done = f32[8,4,128,256]{3,2,1,0:T(8,128)} copy-done((f32[8,4,128,256]{3,2,1,0:T(8,128)}, f32[8,4,128,256]{3,2,1,0:T(8,128)S(1)}, u32[]{:S(2)}) %copy-start) | copy-done | bytes 4194328
  60.6 1.0 copy-done.13
  61.6 1.0 copy-done.15
  62.6 6.6 %all-to-all-done.1.got_ref = bf16[32,2,32,128]{3,2,1,0:T(8,128)(2,1)S(1)} async-done(((bf16[32,2,32,128]{3,2,1,0:T(8,128)(2,1)}), bf16[32,2,32,128]{3,2,1,0:T(8,128)(2,1)S(1)}, u32[]{:S(2)}, u32[]{:S(2)}) %all-to-all-start.1) | async-done | bytes 524320 | tf_op jit(solution)/shard_map/all_to_all | solution.py:280
  69.2 1.2 copy-done.14
  70.4 0.7 output_back.1
  71.1 20.7 %all_to_all.36.got_ref = bf16[32,2,32,128]{3,2,1,0:T(8,128)(2,1)S(1)} all-to-all(bf16[32,2,32,128]{3,2,1,0:T(8,128)(2,1)S(1)} %output_back.1), channel_id=1, replica_groups=mesh['dp'=16,'dap'=32] {'dap'}, dimensions={0} | all-to-all | bytes 1048576 | tf_op jit(solution)/shard_map/all_to_all | solution.py:280
  91.8 1.7 operands_back.1
  93.5 8.6 %all-to-all-start.3 = ((bf16[32,2,2,32,128]{4,3,2,1,0:T(8,128)(2,1)}), bf16[32,2,2,32,128]{4,3,2,1,0:T(8,128)(2,1)S(1)}, u32[]{:S(2)}, u32[]{:S(2)}) async-start(bf16[32,2,2,32,128]{4,3,2,1,0:T(8,128)(2,1)} %operands_back.1), calls=%async_computation.3 | async-start | bytes 2097152 | tf_op jit(solution)/shard_map/all_to_all | solution.py:280
  102.1 1.2 copy-done.16
  103.3 1.0 copy-done.18
  104.4 2.2 %output_weights.1 = (bf16[8,128,256]{2,1,0:T(8,128)(2,1)S(1)}, f32[2,128,128]{2,1,0:T(8,128)S(1)}) custom-call(bf16[32,2,32,128]{3,2,1,0:T(8,128)(2,1)S(1)} %all-to-all-done.1.got_ref, bf16[8,128,256]{2,1,0:T(8,128)(2,1)S(1)} %get-tuple-element.23.norm_ref, bf16[8,128,256]{2,1,0:T(8,128)(2,1)S(1)} %copy-done.18, f32[8,128,256]{2,1,0:T(8,128)S(1)} %copy-done.16, ...), custom_call_target="tpu_custom_call" | custom-call | flops 4000000000 | bytes 4194304 | tf_op jit(solution)/shard_map/output_weights/pallas_call | solution.py:339
  106.6 20.1 %all-to-all-done.3.got_ref = bf16[32,2,2,32,128]{4,3,2,1,0:T(8,128)(2,1)S(1)} async-done(((bf16[32,2,2,32,128]{4,3,2,1,0:T(8,128)(2,1)}), bf16[32,2,2,32,128]{4,3,2,1,0:T(8,128)(2,1)S(1)}, u32[]{:S(2)}, u32[]{:S(2)}) %all-to-all-start.3) | async-done | bytes 1048608 | tf_op jit(solution)/shard_map/all_to_all | solution.py:280
  126.7 2.2 %copy-done.1 = f32[8,4,128,256]{3,2,1,0:T(8,128)S(1)} copy-done((f32[8,4,128,256]{3,2,1,0:T(8,128)S(1)}, f32[8,4,128,256]{3,2,1,0:T(8,128)}, u32[]{:S(2)}) %copy-start.1) | copy-done | bytes 4194328
  128.9 1.2 input_weights.1
  130.2 18.6 %all_to_all.37.got_ref = f32[32,24,128]{2,1,0:T(8,128)S(1)} all-to-all(f32[32,24,128]{2,1,0:T(8,128)S(1)} %bitcast.11), channel_id=1, replica_groups=mesh['dp'=16,'dap'=32] {'dap'}, dimensions={0} | all-to-all | bytes 786432 | tf_op jit(solution)/shard_map/all_to_all | solution.py:280
  148.8 22.3 %all_to_all.38.got_ref = f32[16,24,128]{2,1,0:T(8,128)S(1)} all-to-all(f32[16,24,128]{2,1,0:T(8,128)S(1)} %fold_inner.1), channel_id=1, replica_groups=mesh['dp'=16,'dap'=32] {'dp'}, dimensions={0} | all-to-all | bytes 393216 | tf_op jit(solution)/shard_map/all_to_all | solution.py:280
  171.1 0.8 fold_outer.1
  171.9 4.9 %all-to-all-start.6 = ((f32[32,24,128]{2,1,0:T(8,128)}), f32[32,24,128]{2,1,0:T(8,128)S(1)}, u32[]{:S(2)}, u32[]{:S(2)}) async-start(f32[32,24,128]{2,1,0:T(8,128)} %fold_outer.1), calls=%async_computation.6 | async-start | bytes 786432 | tf_op jit(solution)/shard_map/all_to_all | solution.py:280
  176.8 1.6 copy-done.3
  178.4 1.9 input_back.1
  180.3 9.7 %all-to-all-done.6 = f32[32,24,128]{2,1,0:T(8,128)S(1)} async-done(((f32[32,24,128]{2,1,0:T(8,128)}), f32[32,24,128]{2,1,0:T(8,128)S(1)}, u32[]{:S(2)}, u32[]{:S(2)}) %all-to-all-start.6) | async-done | bytes 393248 | tf_op jit(solution)/shard_map/all_to_all | solution.py:280
  190.0 0.8 finish.1
  (28 shorter events, 0.1 us)
Async XLA Ops:
  1.4 1.0 copy-start.5
  2.4 0.9 copy-start.7
  3.3 0.7 copy-start.10
  7.1 48.3 %copy-start.4 = (bf16[1,8,256,128]{3,2,1,0:T(8,128)(2,1)S(1)}, bf16[1,8,256,128]{3,2,1,0:T(8,128)(2,1)}, u32[]{:S(2)}) copy-start(bf16[1,8,256,128]{3,2,1,0:T(8,128)(2,1)} %param.8) | copy-start | bytes 1572868
  7.1 48.3 %copy-start.8 = (bf16[128,640]{1,0:T(8,128)(2,1)S(1)}, bf16[128,640]{1,0:T(8,128)(2,1)}, u32[]{:S(2)}) copy-start(bf16[128,640]{1,0:T(8,128)(2,1)} %refs_1_.1) | copy-start | bytes 491524
  7.2 48.3 %copy-start.9 = (bf16[128,128]{1,0:T(8,128)(2,1)S(1)}, bf16[128,128]{1,0:T(8,128)(2,1)}, u32[]{:S(2)}) copy-start(bf16[128,128]{1,0:T(8,128)(2,1)} %refs_3_.1) | copy-start | bytes 98308
  7.2 48.3 %copy-start.12 = (f32[128]{0:T(128)S(1)}, f32[128]{0:T(128)}, u32[]{:S(2)}) copy-start(f32[128]{0:T(128)} %param.13) | copy-start | bytes 1540
  46.8 22.3 %all-to-all-start.1 = ((bf16[32,2,32,128]{3,2,1,0:T(8,128)(2,1)}), bf16[32,2,32,128]{3,2,1,0:T(8,128)(2,1)S(1)}, u32[]{:S(2)}, u32[]{:S(2)}) async-start(bf16[32,2,32,128]{3,2,1,0:T(8,128)(2,1)} %get-tuple-element.22), calls=%async_computation.1 | async-start | bytes 1048576 | tf_op jit(solution)/shard_map/all_to_all | solution.py:280
  58.6 2.0 %copy-start = (f32[8,4,128,256]{3,2,1,0:T(8,128)}, f32[8,4,128,256]{3,2,1,0:T(8,128)S(1)}, u32[]{:S(2)}) copy-start(f32[8,4,128,256]{3,2,1,0:T(8,128)S(1)} %get-tuple-element.26.factors_ref) | copy-start | bytes 12582916
  60.6 1.0 copy-start.13
  61.6 1.0 copy-start.15
  62.6 30.9 %copy-start.17 = (bf16[8,128,256]{2,1,0:T(8,128)(2,1)}, bf16[8,128,256]{2,1,0:T(8,128)(2,1)S(1)}, u32[]{:S(2)}) copy-start(bf16[8,128,256]{2,1,0:T(8,128)(2,1)S(1)} %get-tuple-element.27.gated_ref) | copy-start | bytes 1572868
  69.1 1.2 copy-start.14
  93.5 33.2 %all-to-all-start.3 = ((bf16[32,2,2,32,128]{4,3,2,1,0:T(8,128)(2,1)}), bf16[32,2,2,32,128]{4,3,2,1,0:T(8,128)(2,1)S(1)}, u32[]{:S(2)}, u32[]{:S(2)}) async-start(bf16[32,2,2,32,128]{4,3,2,1,0:T(8,128)(2,1)} %operands_back.1), calls=%async_computation.3 | async-start | bytes 2097152 | tf_op jit(solution)/shard_map/all_to_all | solution.py:280
  102.1 1.2 copy-start.16
  103.3 1.0 copy-start.18
  126.7 2.2 %copy-start.1 = (f32[8,4,128,256]{3,2,1,0:T(8,128)S(1)}, f32[8,4,128,256]{3,2,1,0:T(8,128)}, u32[]{:S(2)}) copy-start(f32[8,4,128,256]{3,2,1,0:T(8,128)} %copy-done) | copy-start | bytes 12582916
  130.2 41.0 %copy-start.2 = (bf16[8,512,256]{2,1,0:T(8,128)(2,1)}, bf16[8,512,256]{2,1,0:T(8,128)(2,1)S(1)}, u32[]{:S(2)}) copy-start(bf16[8,512,256]{2,1,0:T(8,128)(2,1)S(1)} %get-tuple-element.30.pieces_ref) | copy-start | bytes 6291460
  148.7 28.1 %copy-start.6 = (bf16[1,8,256,128]{3,2,1,0:T(8,128)(2,1)S(1)}, bf16[1,8,256,128]{3,2,1,0:T(8,128)(2,1)}, u32[]{:S(2)}) copy-start(bf16[1,8,256,128]{3,2,1,0:T(8,128)(2,1)} %param.7) | copy-start | bytes 1572868
  148.8 28.1 %copy-start.11 = (f32[128]{0:T(128)S(1)}, f32[128]{0:T(128)}, u32[]{:S(2)}) copy-start(f32[128]{0:T(128)} %param.11) | copy-start | bytes 1540
  171.9 18.0 %all-to-all-start.6 = ((f32[32,24,128]{2,1,0:T(8,128)}), f32[32,24,128]{2,1,0:T(8,128)S(1)}, u32[]{:S(2)}, u32[]{:S(2)}) async-start(f32[32,24,128]{2,1,0:T(8,128)} %fold_outer.1), calls=%async_computation.6 | async-start | bytes 786432 | tf_op jit(solution)/shard_map/all_to_all | solution.py:280
  176.8 1.6 copy-start.3

commit v3 on v2

--- a/solution.py
+++ b/solution.py
@@ -45,29 +45,112 @@
     return centred * inverse, inverse
 
 
-def row_of_masks(scalars_ref, i, width):
-    length = scalars_ref[0]
+def row_of_masks(length, i, rows, width):
     columns = lax.broadcasted_iota(jnp.int32, (1, width), 1)
-    keep = jnp.logical_and(columns < length, scalars_ref[1] + i < length)
-    return keep.astype(F32)
+    row = lax.axis_index("dap").astype(jnp.int32) * rows + i
+    return jnp.logical_and(columns < length, row < length).astype(F32)
 
 
 def wide(gain, width):
     return jnp.concatenate([gain] * (width // gain.shape[1]), axis=1)
 
 
-def project_kernel(scalars_ref, pair_ref, w_ref, gain_ref, send_ref, norm_ref, wt_ref, stage_ref):
-    rows, width, channels = pair_ref.shape
+def transposed_blocks(w_ref, wt_ref):
+    for n in range(wt_ref.shape[0]):
+        block = w_ref[:, n * LANES : (n + 1) * LANES]
+        wt_ref[n] = jnp.transpose(block.astype(F32)).astype(BF16)
+
+
+def output_ahead(
+    length, norm_ref, cotangent_ref, wt_ref, w_out_ref, gain_ref, outs, stages, sems
+):
+    rows, width, channels = cotangent_ref.shape
+    upstream_ref, factors_ref, gated_ref, slope_ref = stages
     eye = identity(channels)
     gain = wide(column(gain_ref[...], channels), width)
-    for n in range(4):
-        block = w_ref[:, n * channels : (n + 1) * channels]
-        wt_ref[n] = jnp.transpose(block.astype(F32)).astype(BF16)
+    w_out = w_out_ref[...]
+    copies = []
     for i in range(rows):
+        norm = norm_ref[i]
+        cotangent = dot(eye, cotangent_ref[i], NT)
+        out_gate = sigmoid(dot(wt_ref[4], norm, NN))
+        gated = cotangent * out_gate
+        slope_ref[i] = gated * (1.0 - out_gate)
+        gated = gated.astype(BF16)
+        gated_ref[i] = gated
+        upstream = dot(w_out, gated, NN) * gain
+        upstream = upstream - jnp.sum(upstream, axis=0, keepdims=True) * (1.0 / channels)
+        for half in range(width // LANES):
+            upstream_ref[half, pl.ds(i, channels, stride=rows), :] = upstream[
+                :, half * LANES : (half + 1) * LANES
+            ]
+        mask = row_of_masks(length, i, rows, width)
+        for side in range(2):
+            value = dot(wt_ref[2 * side], norm, NN)
+            gate = sigmoid(dot(wt_ref[2 * side + 1], norm, NN))
+            masked = mask * gate
+            factors_ref[i, 2 * side] = masked.astype(BF16)
+            factors_ref[i, 2 * side + 1] = (masked * value * (1.0 - gate)).astype(BF16)
+        for n in range(1, 4):
+            copies.append(
+                pltpu.make_async_copy(stages[n].at[i], outs[n].at[i], sems.at[n, i])
+            )
+            copies[-1].start()
+    for half in range(width // LANES):
+        copies.append(
+            pltpu.make_async_copy(upstream_ref.at[half], outs[0].at[half], sems.at[0, half])
+        )
+        copies[-1].start()
+    for copy in copies:
+        copy.wait()
+
+
+def first_core():
+    return lax.rem(lax.axis_index("dp").astype(jnp.int32), 2) == 0
+
+
+def project_kernel(
+    lengths_ref, pair_hbm, cotangent_hbm, w_hbm, gain_hbm, w_out_hbm, gain_out_hbm,
+    send_ref, norm_ref, *rest,
+):
+    outs, stages = rest[:4], rest[4:8]
+    pair_ref, cotangent_ref, w_ref, gain_ref, w_out_ref, gain_out_ref = rest[8:14]
+    wt_ref, stage_ref, sems, in_sems = rest[14:]
+    rows, width, channels = pair_ref.shape
+    length = lengths_ref[0]
+    whole = [
+        pltpu.make_async_copy(source, target, in_sems.at[2, n])
+        for n, (source, target) in enumerate(
+            (
+                (w_hbm, w_ref),
+                (gain_hbm, gain_ref),
+                (w_out_hbm, w_out_ref),
+                (gain_out_hbm, gain_out_ref),
+            )
+        )
+    ]
+    by_row = [
+        [
+            pltpu.make_async_copy(source.at[i], target.at[i], in_sems.at[n, i])
+            for i in range(rows)
+        ]
+        for n, (source, target) in enumerate(
+            ((pair_hbm, pair_ref), (cotangent_hbm, cotangent_ref))
+        )
+    ]
+    for copy in whole[:2] + by_row[0] + whole[2:] + by_row[1]:
+        copy.start()
+    eye = identity(channels)
+    whole[0].wait()
+    transposed_blocks(w_ref, wt_ref)
+    whole[1].wait()
+    gain = wide(column(gain_ref[...], channels), width)
+    for i in range(rows):
+        by_row[0][i].wait()
         hat, _ = norm_sublanes(dot(eye, pair_ref[i], NT))
         norm = (hat * gain).astype(BF16)
         norm_ref[i] = norm
-        mask = row_of_masks(scalars_ref, i, width)
+        mask = row_of_masks(length, i, rows, width)
         for side in range(2):
             value = dot(wt_ref[2 * side], norm, NN)
             gate = sigmoid(dot(wt_ref[2 * side + 1], norm, NN))
@@ -82,6 +165,28 @@
             send_ref[:, side, half] = (
                 stage_ref[side, half].reshape(peers, -1, LANES).astype(BF16)
             )
+    for copy in whole[2:] + by_row[1]:
+        copy.wait()
+
+    @pl.when(first_core())
+    def _():
+        output_ahead(
+            length, norm_ref, cotangent_ref, wt_ref, w_out_ref, gain_out_ref, outs, stages, sems
+        )
+
+
+def output_ahead_kernel(
+    lengths_ref, norm_ref, cotangent_ref, w_ref, w_out_ref, gain_ref, *rest
+):
+    outs, stages = rest[4:8], rest[8:12]
+    wt_ref, sems = rest[12:]
+
+    @pl.when(jnp.logical_not(first_core()))
+    def _():
+        transposed_blocks(w_ref, wt_ref)
+        output_ahead(
+            lengths_ref[0], norm_ref, cotangent_ref, wt_ref, w_out_ref, gain_ref, outs, stages, sems
+        )
 
 
 def regroup(block, group):
@@ -108,49 +213,22 @@
         send_ref[:, out] = stage_ref[out].astype(BF16)
 
 
-def output_ahead_kernel(
-    scalars_ref, norm_ref, cotangent_ref, w_ref, w_out_ref, gain_ref,
-    upstream_ref, factors_ref, gated_ref, slope_ref, wt_ref,
-):
-    rows, width, channels = cotangent_ref.shape
-    eye = identity(channels)
-    gain = wide(column(gain_ref[...], channels), width)
-    for n in range(5):
-        block = w_ref[:, n * channels : (n + 1) * channels]
-        wt_ref[n] = jnp.transpose(block.astype(F32)).astype(BF16)
-    w_out = w_out_ref[...]
-    for i in range(rows):
-        norm = norm_ref[i]
-        cotangent = dot(eye, cotangent_ref[i], NT)
-        out_gate = sigmoid(dot(wt_ref[4], norm, NN))
-        gated = cotangent * out_gate
-        slope_ref[i] = gated * (1.0 - out_gate)
-        gated = gated.astype(BF16)
-        gated_ref[i] = gated
-        upstream = dot(w_out, gated, NN) * gain
-        upstream = upstream - jnp.sum(upstream, axis=0, keepdims=True) * (1.0 / channels)
-        for half in range(width // LANES):
-            upstream_ref[half, pl.ds(i, channels, stride=rows), :] = upstream[
-                :, half * LANES : (half + 1) * LANES
-            ]
-        mask = row_of_masks(scalars_ref, i, width)
-        for side in range(2):
-            value = dot(wt_ref[2 * side], norm, NN)
-            gate = sigmoid(dot(wt_ref[2 * side + 1], norm, NN))
-            masked = mask * gate
-            factors_ref[i, 2 * side] = masked
-            factors_ref[i, 2 * side + 1] = masked * value * (1.0 - gate)
-
-
 def norm_blocks(block):
     product = block.astype(F32).reshape(-1, SUB, block.shape[-1])
     return norm_sublanes(product)
 
 
-def output_back_kernel(got_ref, upstream_ref, send_ref):
+def output_back_kernel(got_ref, upstream_hbm, send_ref, upstream_ref, sems):
     peers, halves, packed, lanes = got_ref.shape
+    copies = [
+        pltpu.make_async_copy(upstream_hbm.at[half], upstream_ref.at[half], sems.at[half])
+        for half in range(halves)
+    ]
+    for copy in copies:
+        copy.start()
     for half in range(halves):
         hat, inverse = norm_blocks(got_ref[:, half])
+        copies[half].wait()
         upstream = upstream_ref[half].reshape(hat.shape)
         second = jnp.sum(upstream * hat, axis=0, keepdims=True) * (1.0 / hat.shape[0])
         grad = inverse * (upstream - hat * second)
@@ -208,15 +286,22 @@
 
 
 def input_weights_kernel(
-    got_ref, factors_ref, norm_ref, sums_ref, parts_ref, pieces_ref, stage_ref
+    got_ref, factors_hbm, norm_ref, sums_ref, parts_ref, pieces_ref, stage_ref, factors_ref, sems
 ):
     halves = got_ref.shape[2]
     rows, channels, _ = norm_ref.shape
+    copies = [
+        pltpu.make_async_copy(factors_hbm.at[i], factors_ref.at[i], sems.at[i])
+        for i in range(rows)
+    ]
+    for copy in copies:
+        copy.start()
     for side in range(2):
         for half in range(halves):
             stage_ref[side, half] = got_ref[:, side, half].astype(F32).reshape(-1, LANES)
     totals = [jnp.zeros((channels, 2 * channels), F32) for _ in range(2)]
     for i in range(rows):
+        copies[i].wait()
         for half in range(halves):
             lanes = slice(half * LANES, (half + 1) * LANES)
             norm = norm_ref[i, :, lanes]
@@ -233,9 +318,9 @@
                 totals[side] = totals[side] + dot(norm, pieces, NT)
     for side in range(2):
         for n in range(2):
-            parts_ref[2 * side + n] = totals[side][:, n * channels : (n + 1) * channels]
-    parts_ref[4] = sums_ref[0]
-    parts_ref[5] = sums_ref[1]
+            parts_ref[2 * side + n] = totals[side][:, n * channels : (n + 1) * channels].astype(BF16)
+    parts_ref[4] = sums_ref[0].astype(BF16)
+    parts_ref[5] = sums_ref[1].astype(BF16)
 
 
 def input_back_kernel(pieces_ref, gate_grad_ref, pair_ref, w_ref, gain_ref, out_ref):
@@ -265,12 +350,12 @@
     channels = w_out_ref.shape[0]
     dots = jnp.zeros((channels, channels), F32)
     for n in range(5):
-        total = got_ref[n] * factor
+        total = got_ref[n].astype(F32) * factor
         lanes = slice(n * channels, (n + 1) * channels)
         w_in_grad_ref[:, lanes] = total
         dots = dots + total * w_ref[:, lanes].astype(F32)
     gain_in_grad_ref[...] = jnp.sum(jnp.transpose(dots), axis=0, keepdims=True) / gain_in_ref[...]
-    total = got_ref[5] * factor
+    total = got_ref[5].astype(F32) * factor
     w_out_grad_ref[...] = total
     dots = total * w_out_ref[...].astype(F32)
     gain_out_grad_ref[...] = jnp.sum(jnp.transpose(dots), axis=0, keepdims=True) / gain_out_ref[...]
@@ -280,17 +365,21 @@
     return lax.all_to_all(values, axis, split_axis=0, concat_axis=0, tiled=True)
 
 
-def call(kernel, name, out_shape, scratch=(), scalars=False, inputs=1, flops=10**9):
-    in_specs = [pl.BlockSpec(memory_space=pltpu.VMEM)] * inputs
-    if scalars:
-        in_specs[0] = pl.BlockSpec(memory_space=pltpu.SMEM)
+VMEM = pl.BlockSpec(memory_space=pltpu.VMEM)
+SMEM = pl.BlockSpec(memory_space=pltpu.SMEM)
+HBM = pl.BlockSpec(memory_space=pltpu.HBM)
+COPIES = pltpu.SemaphoreType.DMA
+
+
+def call(kernel, name, ins, outs, scratch=(), aliases=None, flops=10**9, grant=24):
     return pl.pallas_call(
         kernel,
-        out_shape=[jax.ShapeDtypeStruct(shape, dtype) for shape, dtype in out_shape],
-        in_specs=in_specs,
-        out_specs=[pl.BlockSpec(memory_space=pltpu.VMEM)] * len(out_shape),
-        scratch_shapes=[pltpu.VMEM(shape, dtype) for shape, dtype in scratch],
-        compiler_params=pltpu.CompilerParams(vmem_limit_bytes=40 * 2**20),
+        out_shape=[jax.ShapeDtypeStruct(shape, dtype) for shape, dtype, _ in outs],
+        in_specs=ins,
+        out_specs=[spec for _, _, spec in outs],
+        scratch_shapes=[pltpu.VMEM(*item) if isinstance(item, tuple) else item for item in scratch],
+        input_output_aliases=aliases or {},
+        compiler_params=pltpu.CompilerParams(vmem_limit_bytes=grant * 2**20),
         cost_estimate=pl.CostEstimate(flops=flops, bytes_accessed=4 * 2**20, transcendentals=0),
         name=name,
     )
@@ -299,85 +388,103 @@
 def per_device(pair, cotangent, lengths, w_in, gain_in, w_out, gain_out):
     _, rows, width, channels = pair.shape
     inner, outer = lax.axis_size("dap"), lax.axis_size("dp")
-    halves, packed = width // LANES, channels // inner * rows
-    group = channels // inner
+    halves, group = width // LANES, channels // inner
+    packed = group * rows
     pair, cotangent = pair[0], cotangent[0]
     gain_in, gain_out = gain_in[None], gain_out[None]
-    scalars = jnp.stack([lengths[0], lax.axis_index("dap").astype(jnp.int32) * rows])
     one_side, two_sides = (inner, halves, packed, LANES), (inner, 2, halves, packed, LANES)
-    flat = (rows, channels, width)
-
-    send, norm = call(
-        project_kernel, "project", [(two_sides, BF16), (flat, BF16)],
-        [((4, channels, channels), BF16), ((2, halves, channels * rows, LANES), F32)],
-        scalars=True, inputs=4,
-    )(scalars, pair, w_in, gain_in)
+    flat, square, row = (rows, channels, width), (channels, channels), (1, channels)
+    mixed = (halves, channels * rows, LANES)
+
+    ahead = [
+        (mixed, F32),
+        ((rows, 4, channels, width), BF16),
+        (flat, BF16),
+        (flat, F32),
+    ]
+    ahead_outs = [(shape, dtype, HBM) for shape, dtype in ahead]
+    transposed = ((5,) + square, BF16)
+    send, norm, *ahead_parts = call(
+        project_kernel, "project", [SMEM] + [HBM] * 6,
+        [(two_sides, BF16, VMEM), (flat, BF16, VMEM)] + ahead_outs,
+        ahead
+        + [
+            ((rows, width, channels), BF16),
+            ((rows, width, channels), BF16),
+            ((channels, 5 * channels), BF16),
+            (row, F32),
+            (square, BF16),
+            (row, F32),
+            transposed,
+            ((2,) + mixed, F32),
+            COPIES((4, rows)),
+            COPIES((3, rows)),
+        ],
+        grant=60,
+    )(lengths, pair, cotangent, w_in, gain_in, w_out, gain_out)
     got_operands = exchange(send, "dap")
     upstream, factors, gated, slope = call(
-        output_ahead_kernel, "output_ahead",
-        [
-            ((halves, channels * rows, LANES), F32),
-            ((rows, 4, channels, width), F32),
-            (flat, BF16),
-            (flat, F32),
-        ],
-        [((5, channels, channels), BF16)],
-        scalars=True, inputs=6, flops=6 * 10**9,
-    )(scalars, norm, cotangent, w_in, w_out, gain_out)
+        output_ahead_kernel, "output_ahead", [SMEM] + [VMEM] * 5 + [HBM] * 4, ahead_outs,
+        ahead + [transposed, COPIES((4, rows))],
+        aliases={6 + n: n for n in range(4)}, flops=6 * 10**9, grant=60,
+    )(lengths, norm, cotangent, w_in, w_out, gain_out, *ahead_parts)
 
     send, held = call(
-        product_kernel, "product",
-        [(one_side, BF16), ((2, halves, group, width, LANES), BF16)],
+        product_kernel, "product", [VMEM],
+        [(one_side, BF16, VMEM), ((2, halves, group, width, LANES), BF16, VMEM)],
         [((halves, inner, packed, LANES), F32)],
     )(got_operands)
     got_product = exchange(send, "dap")
 
-    (send,) = call(output_back_kernel, "output_back", [(one_side, BF16)], inputs=2)(
-        got_product, upstream
-    )
+    (send,) = call(
+        output_back_kernel, "output_back", [VMEM, HBM], [(one_side, BF16, VMEM)],
+        [(mixed, F32), COPIES((halves,))], grant=60,
+    )(got_product, upstream)
     got_grad = exchange(send, "dap")
     gate_grad, sums = call(
-        output_weights_kernel, "output_weights",
-        [(flat, BF16), ((2, channels, channels), F32)],
-        [((halves, channels * rows, LANES), F32)],
-        inputs=6, flops=4 * 10**9,
+        output_weights_kernel, "output_weights", [VMEM] * 6,
+        [(flat, BF16, VMEM), ((2,) + square, F32, VMEM)],
+        [(mixed, F32)], flops=4 * 10**9,
     )(got_product, norm, gated, slope, w_out, gain_out)
 
     (send,) = call(
-        operands_back_kernel, "operands_back", [(two_sides, BF16)],
-        [((2, halves, inner, packed, LANES), F32)], inputs=2,
+        operands_back_kernel, "operands_back", [VMEM, VMEM], [(two_sides, BF16, VMEM)],
+        [((2, halves, inner, packed, LANES), F32)],
     )(got_grad, held)
     got_operand_grads = exchange(send, "dap")
 
     parts, pieces = call(
-        input_weights_kernel, "input_weights",
-        [((6, channels, channels), F32), ((rows, 4 * channels, width), BF16)],
-        [((2, halves, channels * rows, LANES), F32)], inputs=4,
+        input_weights_kernel, "input_weights", [VMEM, HBM, VMEM, VMEM],
+        [((6,) + square, BF16, VMEM), ((rows, 4 * channels, width), BF16, VMEM)],
+        [((2,) + mixed, F32), ahead[1], COPIES((rows,))], grant=60,
     )(got_operand_grads, factors, norm, sums)
     share = 6 * channels // inner
     got = exchange(parts.reshape(inner, share, channels), "dap")
     (pair_grad,) = call(
-        input_back_kernel, "input_back", [((rows, width, channels), BF16)], inputs=5,
+        input_back_kernel, "input_back", [VMEM] * 5, [((rows, width, channels), BF16, VMEM)],
         flops=6 * 10**9,
     )(pieces, gate_grad, pair, w_in, gain_in)
-    (send,) = call(fold_kernel, "fold_inner", [((outer, share, channels), F32)])(got)
+    (send,) = call(
+        fold_kernel, "fold_inner", [VMEM], [((outer, share, channels), BF16, VMEM)]
+    )(got)
     got = exchange(send, "dp")
-    (send,) = call(fold_kernel, "fold_outer", [((inner, share, channels), F32)])(got)
-    got = exchange(send, "dap").reshape(6, channels, channels)
+    (send,) = call(
+        fold_kernel, "fold_outer", [VMEM], [((inner, share, channels), BF16, VMEM)]
+    )(got)
+    got = exchange(send, "dap").reshape((6,) + square)
     factor = 1.0 / (width * math.sqrt(outer))
 
     def finish(*refs):
         finish_kernel(factor, *refs)
 
     w_in_grad, gain_in_grad, w_out_grad, gain_out_grad = call(
-        finish, "finish",
+        finish, "finish", [VMEM] * 5,
         [
-            ((channels, 5 * channels), F32),
-            ((1, channels), F32),
-            ((channels, channels), F32),
-            ((1, channels), F32),
+            ((channels, 5 * channels), F32, VMEM),
+            (row, F32, VMEM),
+            (square, F32, VMEM),
+            (row, F32, VMEM),
         ],
-        inputs=5,
     )(got, w_in, gain_in, w_out, gain_out)
     return (pair_grad[None], w_in_grad, gain_in_grad[0], w_out_grad, gain_out_grad[0])
 

time: 192 us -> 175 us (0.911)
  local copies, waits for them, and re-layouts: 13.8 us -> 1.5 us
  Pallas kernels: 17.1 us -> 29.1 us
  waiting for transfers between devices: 36.4 us -> 28.8 us
  blocking collectives: 99.9 us -> 92.9 us
  starting transfers between devices: 22 us -> 19.9 us
    unnamed x38 -> x24, local copies, waits for them, and re-layouts: 13.8 us -> 1.5 us
    pallas_call x11, Pallas kernels: 17.1 us -> 29.1 us  [the longest x1 6.63 us: per_device(): call(project_kernel, 'project', [SMEM] + [HBM] * 6, [(two_sides, BF16, VM...]
    all_to_all x3, waiting for transfers between devices: 36.4 us -> 28.8 us  [exchange(): return lax.all_to_all(values, axis, split_axis=0, concat_axis=0, tiled=True)]
    all_to_all x4, blocking collectives: 99.9 us -> 92.9 us  [exchange(): return lax.all_to_all(values, axis, split_axis=0, concat_axis=0, tiled=True)]
    all_to_all x3, starting transfers between devices: 22 us -> 19.9 us  [exchange(): return lax.all_to_all(values, axis, split_axis=0, concat_axis=0, tiled=True)]
  transfers between devices with their start and end apart: 3 -> 3, of which waited for: 3 -> 3; matrix products, arithmetic and copies ran while one was open for 0% -> 0% of each run, Pallas kernels for 4% -> 5%
where the time goes in v3:
time: 175 us; the launch traced here: 174 us
  blocking collectives  92.9 us (53%)
  Pallas kernels  29.1 us (17%)
  waiting for transfers between devices  28.8 us (16%)
  starting transfers between devices  19.9 us (11%)
    all_to_all x4, blocking collectives, exchange(): return lax.all_to_all(values, axis, split_axis=0, concat_axis=0, tiled=True)  92.9 us
    all_to_all x3, waiting for transfers between devices, exchange(): return lax.all_to_all(values, axis, split_axis=0, concat_axis=0, tiled=True)  28.8 us
    all_to_all x3, starting transfers between devices, exchange(): return lax.all_to_all(values, axis, split_axis=0, concat_axis=0, tiled=True)  19.9 us
    pallas_call x1, Pallas kernels, per_device(): call(project_kernel, 'project', [SMEM] + [HBM] * 6, [(two_sides, BF16, VM...  6.63 us
    pallas_call x1, Pallas kernels, per_device(): call(output_ahead_kernel, 'output_ahead', [SMEM] + [VMEM] * 5 + [HBM] * 4...  5.41 us
    pallas_call x1, Pallas kernels, per_device(): call(input_weights_kernel, 'input_weights', [VMEM, HBM, VMEM, VMEM], [((6...  4.89 us
  transfers between devices with their start and end apart: 3, of which 3 were waited for; matrix products, arithmetic and copies ran while one was open for 0% of the time, Pallas kernels for 5%

profile of v3, /device:TPU:1, one launch (start us, length us, event | category | flops | bytes accessed | tf_op | source)
XLA Modules:
  0.0 173.7 jit_solution(1409132919922368455)
XLA Ops:
  1.3 6.6 %project.1 = (bf16[32,2,2,32,128]{4,3,2,1,0:T(8,128)(2,1)}, bf16[8,128,256]{2,1,0:T(8,128)(2,1)}, f32[2,1024,128]{2,1,0:T(8,128)}, bf16[8,4,128,256]{3,2,1,0:T(8...) custom-call(s32[1]{0:T(128)S(6)} %copy.20.lengths_ref, bf16[8,256,128]{2,1,0:T(8,128)(2,1)} %bitcast.10, ...), custom_call_target="tpu_custom_call" | custom-call | flops 1000000000 | bytes 4194304 | tf_op jit(solution)/shard_map/project/pallas_call | solution.py:407
  7.9 33.4 %all_to_all.35.got_ref = bf16[32,2,2,32,128]{4,3,2,1,0:T(8,128)(2,1)S(1)} all-to-all(bf16[32,2,2,32,128]{4,3,2,1,0:T(8,128)(2,1)} %get-tuple-element.25), channel_id=1, replica_groups=mesh['dp'=16,'dap'=32] {'dap'}, dimensions={0} | all-to-all | bytes 2097152 | tf_op jit(solution)/shard_map/all_to_all | solution.py:365
  41.3 1.4 product.1
  42.7 9.7 %all-to-all-start.1 = ((bf16[32,2,32,128]{3,2,1,0:T(8,128)(2,1)}), bf16[32,2,32,128]{3,2,1,0:T(8,128)(2,1)S(1)}, u32[]{:S(2)}, u32[]{:S(2)}) async-start(bf16[32,2,32,128]{3,2,1,0:T(8,128)(2,1)} %get-tuple-element.26), calls=%async_computation.1 | async-start | bytes 1048576 | tf_op jit(solution)/shard_map/all_to_all | solution.py:365
  52.4 5.4 %output_ahead.1 = (f32[2,1024,128]{2,1,0:T(8,128)}, bf16[8,4,128,256]{3,2,1,0:T(8,128)(2,1)}, bf16[8,128,256]{2,1,0:T(8,128)(2,1)}, f32[8,128,256]{2,1,0:T(8,128)}) custom-call(s32[1]{0:T(128)S(6)} %copy.20.lengths_ref, bf16[8,128,256]{2,1,0:T(8,128)(2,1)} %get-tuple-element.27.norm_ref, ...), custom_call_target="tpu_custom_call", output_to_operand_aliasing={{0}: (6, {}), {1}: (7, {}), {2}: (8, {}), {3}: (9, {})} | custom-call | flops 6000000000 | bytes 4194304 | tf_op jit(solution)/shard_map/output_ahead/pallas_call | solution.py:426
  57.8 6.0 %all-to-all-done.1.got_ref = bf16[32,2,32,128]{3,2,1,0:T(8,128)(2,1)S(1)} async-done(((bf16[32,2,32,128]{3,2,1,0:T(8,128)(2,1)}), bf16[32,2,32,128]{3,2,1,0:T(8,128)(2,1)S(1)}, u32[]{:S(2)}, u32[]{:S(2)}) %all-to-all-start.1) | async-done | bytes 524320 | tf_op jit(solution)/shard_map/all_to_all | solution.py:365
  63.9 0.8 copy-done
  64.7 3.5 %output_back.1 = bf16[32,2,32,128]{3,2,1,0:T(8,128)(2,1)} custom-call(bf16[32,2,32,128]{3,2,1,0:T(8,128)(2,1)} %copy-done, f32[2,1024,128]{2,1,0:T(8,128)} %get-tuple-element.32.upstream_hbm), custom_call_target="tpu_custom_call" | custom-call | flops 1000000000 | bytes 4194304 | tf_op jit(solution)/shard_map/output_back/pallas_call | solution.py:439
  68.2 16.9 %all_to_all.36.got_ref = bf16[32,2,32,128]{3,2,1,0:T(8,128)(2,1)S(1)} all-to-all(bf16[32,2,32,128]{3,2,1,0:T(8,128)(2,1)} %output_back.1), channel_id=1, replica_groups=mesh['dp'=16,'dap'=32] {'dap'}, dimensions={0} | all-to-all | bytes 1048576 | tf_op jit(solution)/shard_map/all_to_all | solution.py:365
  85.1 0.0 copy-start.11
  85.1 1.7 operands_back.1
  86.8 6.1 %all-to-all-start.3 = ((bf16[32,2,2,32,128]{4,3,2,1,0:T(8,128)(2,1)}), bf16[32,2,2,32,128]{4,3,2,1,0:T(8,128)(2,1)}, u32[]{:S(2)}, u32[]{:S(2)}) async-start(bf16[32,2,2,32,128]{4,3,2,1,0:T(8,128)(2,1)} %operands_back.1), calls=%async_computation.3 | async-start | bytes 2097152 | tf_op jit(solution)/shard_map/all_to_all | solution.py:365
  92.9 0.0 copy-done.1
  92.9 0.0 copy-done.2
  92.9 0.0 copy-done.7
  92.9 0.0 copy-done.9
  92.9 0.0 copy-done.11
  92.9 0.0 copy-done.10
  92.9 2.2 %output_weights.1 = (bf16[8,128,256]{2,1,0:T(8,128)(2,1)S(1)}, f32[2,128,128]{2,1,0:T(8,128)S(1)}) custom-call(bf16[32,2,32,128]{3,2,1,0:T(8,128)(2,1)S(1)} %copy-done.1, bf16[8,128,256]{2,1,0:T(8,128)(2,1)S(1)} %copy-done.2, bf16[8,128,256]{2,1,0:T(8,128)(2,1)S(1)} %copy-done.11, f32[8,128,256]{2,1,0:T(8,128)S(1)} %copy-done.10, ...), custom_call_target="tpu_custom_call" | custom-call | flops 4000000000 | bytes 4194304 | tf_op jit(solution)/shard_map/output_weights/pallas_call | solution.py:444
  95.2 0.0 copy-start.3
  95.2 0.6 copy-done.3
  95.8 14.8 %all-to-all-done.3.got_ref = bf16[32,2,2,32,128]{4,3,2,1,0:T(8,128)(2,1)} async-done(((bf16[32,2,2,32,128]{4,3,2,1,0:T(8,128)(2,1)}), bf16[32,2,2,32,128]{4,3,2,1,0:T(8,128)(2,1)}, u32[]{:S(2)}, u32[]{:S(2)}) %all-to-all-start.3) | async-done | bytes 1048608 | tf_op jit(solution)/shard_map/all_to_all | solution.py:365
  110.7 4.9 %input_weights.1 = (bf16[6,128,128]{2,1,0:T(8,128)(2,1)}, bf16[8,512,256]{2,1,0:T(8,128)(2,1)}) custom-call(bf16[32,2,2,32,128]{4,3,2,1,0:T(8,128)(2,1)} %all-to-all-done.3.got_ref, bf16[8,4,128,256]{3,2,1,0:T(8,128)(2,1)} %get-tuple-element.34.factors_hbm, bf16[8,128,256]{2,1,0:T(8,128)(2,1)} %get-tuple-element.27.norm_ref, f32[2,128,128]{2,1,0:T(8,128)} %copy-done.3), custom_call_target="tpu_custom_call" | custom-call | flops 1000000000 | bytes 4194304 | tf_op jit(solution)/shard_map/input_weights/pallas_call | solution.py:456
  115.6 17.6 %all_to_all.37.got_ref = bf16[32,24,128]{2,1,0:T(8,128)(2,1)S(1)} all-to-all(bf16[32,24,128]{2,1,0:T(8,128)(2,1)} %bitcast.19), channel_id=1, replica_groups=mesh['dp'=16,'dap'=32] {'dap'}, dimensions={0} | all-to-all | bytes 393216 | tf_op jit(solution)/shard_map/all_to_all | solution.py:365
  133.2 25.0 %all_to_all.38.got_ref = bf16[16,24,128]{2,1,0:T(8,128)(2,1)S(1)} all-to-all(bf16[16,24,128]{2,1,0:T(8,128)(2,1)S(1)} %fold_inner.1), channel_id=1, replica_groups=mesh['dp'=16,'dap'=32] {'dp'}, dimensions={0} | all-to-all | bytes 196608 | tf_op jit(solution)/shard_map/all_to_all | solution.py:365
  158.3 0.7 fold_outer.1
  159.0 4.1 %all-to-all-start.6 = ((bf16[32,24,128]{2,1,0:T(8,128)(2,1)}), bf16[32,24,128]{2,1,0:T(8,128)(2,1)S(1)}, u32[]{:S(2)}, u32[]{:S(2)}) async-start(bf16[32,24,128]{2,1,0:T(8,128)(2,1)} %fold_outer.1), calls=%async_computation.6 | async-start | bytes 393216 | tf_op jit(solution)/shard_map/all_to_all | solution.py:365
  163.1 0.0 copy-done.4
  163.1 0.0 copy-done.5
  163.1 1.8 %input_back.1 = bf16[8,256,128]{2,1,0:T(8,128)(2,1)} custom-call(bf16[8,512,256]{2,1,0:T(8,128)(2,1)S(1)} %copy-done.4, bf16[8,128,256]{2,1,0:T(8,128)(2,1)S(1)} %get-tuple-element.39.gate_grad_ref, bf16[8,256,128]{2,1,0:T(8,128)(2,1)S(1)} %bitcast.11, bf16[128,640]{1,0:T(8,128)(2,1)S(1)} %copy-done.6, f32[1,128]{1,0:T(1,128)S(1)} %bitcast.13), custom_call_target="tpu_custom_call" | custom-call | flops 6000000000 | bytes 4194304 | tf_op jit(solution)/shard_map/input_back/pallas_call | solution.py:463
  164.9 8.0 %all-to-all-done.6 = bf16[32,24,128]{2,1,0:T(8,128)(2,1)S(1)} async-done(((bf16[32,24,128]{2,1,0:T(8,128)(2,1)}), bf16[32,24,128]{2,1,0:T(8,128)(2,1)S(1)}, u32[]{:S(2)}, u32[]{:S(2)}) %all-to-all-start.6) | async-done | bytes 196640 | tf_op jit(solution)/shard_map/all_to_all | solution.py:365
  172.9 0.8 finish.1
  (13 shorter events, 0.1 us)
Async XLA Ops:
  42.7 21.2 %all-to-all-start.1 = ((bf16[32,2,32,128]{3,2,1,0:T(8,128)(2,1)}), bf16[32,2,32,128]{3,2,1,0:T(8,128)(2,1)S(1)}, u32[]{:S(2)}, u32[]{:S(2)}) async-start(bf16[32,2,32,128]{3,2,1,0:T(8,128)(2,1)} %get-tuple-element.26), calls=%async_computation.1 | async-start | bytes 1048576 | tf_op jit(solution)/shard_map/all_to_all | solution.py:365
  63.9 0.8 copy-start
  85.0 7.8 %copy-start.1 = (bf16[32,2,32,128]{3,2,1,0:T(8,128)(2,1)S(1)}, bf16[32,2,32,128]{3,2,1,0:T(8,128)(2,1)}, u32[]{:S(2)}) copy-start(bf16[32,2,32,128]{3,2,1,0:T(8,128)(2,1)} %copy-done) | copy-start | bytes 1572868
  85.0 7.8 %copy-start.2 = (bf16[8,128,256]{2,1,0:T(8,128)(2,1)S(1)}, bf16[8,128,256]{2,1,0:T(8,128)(2,1)}, u32[]{:S(2)}) copy-start(bf16[8,128,256]{2,1,0:T(8,128)(2,1)} %get-tuple-element.27.norm_ref) | copy-start | bytes 1572868
  85.1 7.8 %copy-start.7 = (bf16[128,128]{1,0:T(8,128)(2,1)S(1)}, bf16[128,128]{1,0:T(8,128)(2,1)}, u32[]{:S(2)}) copy-start(bf16[128,128]{1,0:T(8,128)(2,1)} %refs_3_.1) | copy-start | bytes 98308
  85.1 7.9 %copy-start.9 = (f32[128]{0:T(128)S(1)}, f32[128]{0:T(128)}, u32[]{:S(2)}) copy-start(f32[128]{0:T(128)} %param.13) | copy-start | bytes 1540
  85.1 7.9 %copy-start.11 = (bf16[8,128,256]{2,1,0:T(8,128)(2,1)S(1)}, bf16[8,128,256]{2,1,0:T(8,128)(2,1)}, u32[]{:S(2)}) copy-start(bf16[8,128,256]{2,1,0:T(8,128)(2,1)} %get-tuple-element.35.gated_ref) | copy-start | bytes 1572868
  86.8 6.2 %copy-start.10 = (f32[8,128,256]{2,1,0:T(8,128)S(1)}, f32[8,128,256]{2,1,0:T(8,128)}, u32[]{:S(2)}) copy-start(f32[8,128,256]{2,1,0:T(8,128)} %get-tuple-element.36.slope_ref) | copy-start | bytes 3145732
  86.8 23.9 %all-to-all-start.3 = ((bf16[32,2,2,32,128]{4,3,2,1,0:T(8,128)(2,1)}), bf16[32,2,2,32,128]{4,3,2,1,0:T(8,128)(2,1)}, u32[]{:S(2)}, u32[]{:S(2)}) async-start(bf16[32,2,2,32,128]{4,3,2,1,0:T(8,128)(2,1)} %operands_back.1), calls=%async_computation.3 | async-start | bytes 2097152 | tf_op jit(solution)/shard_map/all_to_all | solution.py:365
  95.2 0.7 copy-start.3
  158.2 4.8 %copy-start.4 = (bf16[8,512,256]{2,1,0:T(8,128)(2,1)S(1)}, bf16[8,512,256]{2,1,0:T(8,128)(2,1)}, u32[]{:S(2)}) copy-start(bf16[8,512,256]{2,1,0:T(8,128)(2,1)} %get-tuple-element.38.pieces_ref) | copy-start | bytes 6291460
  158.2 4.8 %copy-start.5 = (bf16[1,8,256,128]{3,2,1,0:T(8,128)(2,1)S(1)}, bf16[1,8,256,128]{3,2,1,0:T(8,128)(2,1)}, u32[]{:S(2)}) copy-start(bf16[1,8,256,128]{3,2,1,0:T(8,128)(2,1)} %param.7) | copy-start | bytes 1572868
  158.2 4.8 %copy-start.6 = (bf16[128,640]{1,0:T(8,128)(2,1)S(1)}, bf16[128,640]{1,0:T(8,128)(2,1)}, u32[]{:S(2)}) copy-start(bf16[128,640]{1,0:T(8,128)(2,1)} %refs_1_.1) | copy-start | bytes 491524
  158.2 4.9 %copy-start.8 = (f32[128]{0:T(128)S(1)}, f32[128]{0:T(128)}, u32[]{:S(2)}) copy-start(f32[128]{0:T(128)} %param.11) | copy-start | bytes 1540
  159.0 13.9 %all-to-all-start.6 = ((bf16[32,24,128]{2,1,0:T(8,128)(2,1)}), bf16[32,24,128]{2,1,0:T(8,128)(2,1)S(1)}, u32[]{:S(2)}, u32[]{:S(2)}) async-start(bf16[32,24,128]{2,1,0:T(8,128)(2,1)} %fold_outer.1), calls=%async_computation.6 | async-start | bytes 393216 | tf_op jit(solution)/shard_map/all_to_all | solution.py:365

commit v4 on v3

--- a/solution.py
+++ b/solution.py
@@ -111,11 +111,11 @@
 
 def project_kernel(
     lengths_ref, pair_hbm, cotangent_hbm, w_hbm, gain_hbm, w_out_hbm, gain_out_hbm,
-    send_ref, norm_ref, *rest,
+    send_hbm, norm_hbm, *rest,
 ):
     outs, stages = rest[:4], rest[4:8]
     pair_ref, cotangent_ref, w_ref, gain_ref, w_out_ref, gain_out_ref = rest[8:14]
-    wt_ref, stage_ref, sems, in_sems = rest[14:]
+    wt_ref, stage_ref, send_ref, norm_ref, sems, in_sems = rest[14:]
     rows, width, channels = pair_ref.shape
     length = lengths_ref[0]
     whole = [
@@ -145,11 +145,14 @@
     transposed_blocks(w_ref, wt_ref)
     whole[1].wait()
     gain = wide(column(gain_ref[...], channels), width)
+    done = []
     for i in range(rows):
         by_row[0][i].wait()
         hat, _ = norm_sublanes(dot(eye, pair_ref[i], NT))
         norm = (hat * gain).astype(BF16)
         norm_ref[i] = norm
+        done.append(pltpu.make_async_copy(norm_ref.at[i], norm_hbm.at[i], in_sems.at[3, i]))
+        done[-1].start()
         mask = row_of_masks(length, i, rows, width)
         for side in range(2):
             value = dot(wt_ref[2 * side], norm, NN)
@@ -165,6 +168,14 @@
             send_ref[:, side, half] = (
                 stage_ref[side, half].reshape(peers, -1, LANES).astype(BF16)
             )
+            done.append(
+                pltpu.make_async_copy(
+                    send_ref.at[:, side, half],
+                    send_hbm.at[:, side, half],
+                    in_sems.at[2, 4 + 2 * side + half],
+                )
+            )
+            done[-1].start()
     for copy in whole[2:] + by_row[1]:
         copy.wait()
 
@@ -173,6 +184,9 @@
         output_ahead(
             length, norm_ref, cotangent_ref, wt_ref, w_out_ref, gain_out_ref, outs, stages, sems
         )
+
+    for copy in done:
+        copy.wait()
 
 
 def output_ahead_kernel(
@@ -218,17 +232,10 @@
     return norm_sublanes(product)
 
 
-def output_back_kernel(got_ref, upstream_hbm, send_ref, upstream_ref, sems):
+def output_back_kernel(got_ref, upstream_ref, send_ref):
     peers, halves, packed, lanes = got_ref.shape
-    copies = [
-        pltpu.make_async_copy(upstream_hbm.at[half], upstream_ref.at[half], sems.at[half])
-        for half in range(halves)
-    ]
-    for copy in copies:
-        copy.start()
     for half in range(halves):
         hat, inverse = norm_blocks(got_ref[:, half])
-        copies[half].wait()
         upstream = upstream_ref[half].reshape(hat.shape)
         second = jnp.sum(upstream * hat, axis=0, keepdims=True) * (1.0 / hat.shape[0])
         grad = inverse * (upstream - hat * second)
@@ -285,36 +292,34 @@
             send_ref[:, side, out] = stage_ref[side, out].astype(BF16)
 
 
-def input_weights_kernel(
-    got_ref, factors_hbm, norm_ref, sums_ref, parts_ref, pieces_ref, stage_ref, factors_ref, sems
-):
+def unpack(got_ref, stage_ref):
+    for side in range(got_ref.shape[1]):
+        for half in range(got_ref.shape[2]):
+            stage_ref[side, half] = got_ref[:, side, half].astype(F32).reshape(-1, LANES)
+
+
+def pieces_of(stage_ref, factors_ref, i, side, half, rows, channels):
+    lanes = slice(half * LANES, (half + 1) * LANES)
+    grad = stage_ref[side, half, pl.ds(i, channels, stride=rows), :]
+    return jnp.concatenate(
+        [
+            (grad * factors_ref[i, 2 * side + n, :, lanes].astype(F32)).astype(BF16)
+            for n in range(2)
+        ],
+        axis=0,
+    )
+
+
+def input_weights_kernel(got_ref, factors_ref, norm_ref, sums_ref, parts_ref, stage_ref):
     halves = got_ref.shape[2]
     rows, channels, _ = norm_ref.shape
-    copies = [
-        pltpu.make_async_copy(factors_hbm.at[i], factors_ref.at[i], sems.at[i])
-        for i in range(rows)
-    ]
-    for copy in copies:
-        copy.start()
-    for side in range(2):
-        for half in range(halves):
-            stage_ref[side, half] = got_ref[:, side, half].astype(F32).reshape(-1, LANES)
+    unpack(got_ref, stage_ref)
     totals = [jnp.zeros((channels, 2 * channels), F32) for _ in range(2)]
     for i in range(rows):
-        copies[i].wait()
         for half in range(halves):
-            lanes = slice(half * LANES, (half + 1) * LANES)
-            norm = norm_ref[i, :, lanes]
+            norm = norm_ref[i, :, half * LANES : (half + 1) * LANES]
             for side in range(2):
-                grad = stage_ref[side, half, pl.ds(i, channels, stride=rows), :]
-                pieces = jnp.concatenate(
-                    [
-                        (grad * factors_ref[i, 2 * side, :, lanes]).astype(BF16),
-                        (grad * factors_ref[i, 2 * side + 1, :, lanes]).astype(BF16),
-                    ],
-                    axis=0,
-                )
-                pieces_ref[i, 2 * side * channels : 2 * (side + 1) * channels, lanes] = pieces
+                pieces = pieces_of(stage_ref, factors_ref, i, side, half, rows, channels)
                 totals[side] = totals[side] + dot(norm, pieces, NT)
     for side in range(2):
         for n in range(2):
@@ -323,14 +328,26 @@
     parts_ref[5] = sums_ref[1].astype(BF16)
 
 
-def input_back_kernel(pieces_ref, gate_grad_ref, pair_ref, w_ref, gain_ref, out_ref):
+def input_back_kernel(
+    got_ref, factors_ref, gate_grad_ref, pair_ref, w_ref, gain_ref, out_ref, stage_ref
+):
     rows, width, channels = pair_ref.shape
     eye = identity(channels)
     gain = wide(column(gain_ref[...], channels), width)
+    unpack(got_ref, stage_ref)
     for i in range(rows):
         hat, inverse = norm_sublanes(dot(eye, pair_ref[i], NT))
-        grad = dot(w_ref[:, : 4 * channels], pieces_ref[i], NN)
-        grad = grad + dot(w_ref[:, 4 * channels :], gate_grad_ref[i], NN)
+        grad = dot(w_ref[:, 4 * channels :], gate_grad_ref[i], NN)
+        for side in range(2):
+            pieces = jnp.concatenate(
+                [
+                    pieces_of(stage_ref, factors_ref, i, side, half, rows, channels)
+                    for half in range(width // LANES)
+                ],
+                axis=1,
+            )
+            block = w_ref[:, 2 * side * channels : 2 * (side + 1) * channels]
+            grad = grad + dot(block, pieces, NN)
         grad = grad * gain
         first = jnp.sum(grad, axis=0, keepdims=True) * (1.0 / channels)
         second = jnp.sum(grad * hat, axis=0, keepdims=True) * (1.0 / channels)
@@ -406,7 +423,7 @@
     transposed = ((5,) + square, BF16)
     send, norm, *ahead_parts = call(
         project_kernel, "project", [SMEM] + [HBM] * 6,
-        [(two_sides, BF16, VMEM), (flat, BF16, VMEM)] + ahead_outs,
+        [(two_sides, BF16, HBM), (flat, BF16, HBM)] + ahead_outs,
         ahead
         + [
             ((rows, width, channels), BF16),
@@ -417,8 +434,10 @@
             (row, F32),
             transposed,
             ((2,) + mixed, F32),
+            (two_sides, BF16),
+            (flat, BF16),
             COPIES((4, rows)),
-            COPIES((3, rows)),
+            COPIES((4, rows)),
         ],
         grant=60,
     )(lengths, pair, cotangent, w_in, gain_in, w_out, gain_out)
@@ -429,6 +448,7 @@
         aliases={6 + n: n for n in range(4)}, flops=6 * 10**9, grant=60,
     )(lengths, norm, cotangent, w_in, w_out, gain_out, *ahead_parts)
 
+    got_operands, upstream = lax.optimization_barrier((got_operands, upstream))
     send, held = call(
         product_kernel, "product", [VMEM],
         [(one_side, BF16, VMEM), ((2, halves, group, width, LANES), BF16, VMEM)],
@@ -437,8 +457,7 @@
     got_product = exchange(send, "dap")
 
     (send,) = call(
-        output_back_kernel, "output_back", [VMEM, HBM], [(one_side, BF16, VMEM)],
-        [(mixed, F32), COPIES((halves,))], grant=60,
+        output_back_kernel, "output_back", [VMEM, VMEM], [(one_side, BF16, VMEM)],
     )(got_product, upstream)
     got_grad = exchange(send, "dap")
     gate_grad, sums = call(
@@ -453,17 +472,16 @@
     )(got_grad, held)
     got_operand_grads = exchange(send, "dap")
 
-    parts, pieces = call(
-        input_weights_kernel, "input_weights", [VMEM, HBM, VMEM, VMEM],
-        [((6,) + square, BF16, VMEM), ((rows, 4 * channels, width), BF16, VMEM)],
-        [((2,) + mixed, F32), ahead[1], COPIES((rows,))], grant=60,
+    (parts,) = call(
+        input_weights_kernel, "input_weights", [VMEM] * 4, [((6,) + square, BF16, VMEM)],
+        [((2,) + mixed, F32)],
     )(got_operand_grads, factors, norm, sums)
     share = 6 * channels // inner
     got = exchange(parts.reshape(inner, share, channels), "dap")
     (pair_grad,) = call(
-        input_back_kernel, "input_back", [VMEM] * 5, [((rows, width, channels), BF16, VMEM)],
-        flops=6 * 10**9,
-    )(pieces, gate_grad, pair, w_in, gain_in)
+        input_back_kernel, "input_back", [VMEM] * 6, [((rows, width, channels), BF16, VMEM)],
+        [((2,) + mixed, F32)], flops=6 * 10**9,
+    )(got_operand_grads, factors, gate_grad, pair, w_in, gain_in)
     (send,) = call(
         fold_kernel, "fold_inner", [VMEM], [((outer, share, channels), BF16, VMEM)]
     )(got)

time: 175 us -> 168 us (0.960)
  blocking collectives: 92.9 us -> 79.2 us
  Pallas kernels: 29.1 us -> 22.1 us
  local copies, waits for them, and re-layouts: 1.5 us -> 8.28 us
  waiting for transfers between devices: 28.8 us -> 33 us
  starting transfers between devices: 19.9 us -> 23.3 us
    all_to_all x4, blocking collectives: 92.9 us -> 79.2 us  [exchange(): return lax.all_to_all(values, axis, split_axis=0, concat_axis=0, tiled=True)]
    unnamed x24 -> x30, local copies, waits for them, and re-layouts: 1.5 us -> 8.28 us
    pallas_call x4, Pallas kernels: 16.8 us -> 10.6 us  [the longest x1 6.48 us: per_device(): call(project_kernel, 'project', [SMEM] + [HBM] * 6, [(two_sides, BF16, HB...]
    all_to_all x3, waiting for transfers between devices: 28.8 us -> 33 us  [exchange(): return lax.all_to_all(values, axis, split_axis=0, concat_axis=0, tiled=True)]
    all_to_all x3, starting transfers between devices: 19.9 us -> 23.3 us  [exchange(): return lax.all_to_all(values, axis, split_axis=0, concat_axis=0, tiled=True)]
  transfers between devices with their start and end apart: 3 -> 3, of which waited for: 3 -> 3; matrix products, arithmetic and copies ran while one was open for 0% -> 0% of each run, Pallas kernels for 5% -> 6%
where the time goes in v4:
time: 168 us; the launch traced here: 167 us
  blocking collectives  79.2 us (47%)
  waiting for transfers between devices  33 us (20%)
  starting transfers between devices  23.3 us (14%)
  Pallas kernels  22.1 us (13%)
  local copies, waits for them, and re-layouts  8.28 us (5%)
    all_to_all x4, blocking collectives, exchange(): return lax.all_to_all(values, axis, split_axis=0, concat_axis=0, tiled=True)  79.2 us
    all_to_all x3, waiting for transfers between devices, exchange(): return lax.all_to_all(values, axis, split_axis=0, concat_axis=0, tiled=True)  33 us
    all_to_all x3, starting transfers between devices, exchange(): return lax.all_to_all(values, axis, split_axis=0, concat_axis=0, tiled=True)  23.3 us
    unnamed x30, local copies, waits for them, and re-layouts  8.28 us
    pallas_call x1, Pallas kernels, per_device(): call(project_kernel, 'project', [SMEM] + [HBM] * 6, [(two_sides, BF16, HB...  6.48 us
    pallas_call x1, Pallas kernels, per_device(): call(output_ahead_kernel, 'output_ahead', [SMEM] + [VMEM] * 5 + [HBM] * 4...  5.45 us
  transfers between devices with their start and end apart: 3, of which 3 were waited for; matrix products, arithmetic and copies ran while one was open for 0% of the time, Pallas kernels for 6%

profile of v4, /device:TPU:1, one launch (start us, length us, event | category | flops | bytes accessed | tf_op | source)
XLA Modules:
  0.0 167.3 jit_solution(10892943368808135563)
XLA Ops:
  1.3 6.5 %project.1 = (bf16[32,2,2,32,128]{4,3,2,1,0:T(8,128)(2,1)}, bf16[8,128,256]{2,1,0:T(8,128)(2,1)}, f32[2,1024,128]{2,1,0:T(8,128)}, bf16[8,4,128,256]{3,2,1,0:T(8...) custom-call(s32[1]{0:T(128)S(6)} %copy.20.lengths_ref, bf16[8,256,128]{2,1,0:T(8,128)(2,1)} %bitcast.11, ...), custom_call_target="tpu_custom_call" | custom-call | flops 1000000000 | bytes 4194304 | tf_op jit(solution)/shard_map/project/pallas_call | solution.py:424
  7.8 13.7 %all-to-all-start = ((bf16[32,2,2,32,128]{4,3,2,1,0:T(8,128)(2,1)}), bf16[32,2,2,32,128]{4,3,2,1,0:T(8,128)(2,1)S(1)}, u32[]{:S(2)}, u32[]{:S(2)}) async-start(bf16[32,2,2,32,128]{4,3,2,1,0:T(8,128)(2,1)} %get-tuple-element.25), calls=%async_computation | async-start | bytes 2097152 | tf_op jit(solution)/shard_map/all_to_all | solution.py:382
  21.5 5.5 %output_ahead.1 = (f32[2,1024,128]{2,1,0:T(8,128)}, bf16[8,4,128,256]{3,2,1,0:T(8,128)(2,1)}, bf16[8,128,256]{2,1,0:T(8,128)(2,1)}, f32[8,128,256]{2,1,0:T(8,128)}) custom-call(s32[1]{0:T(128)S(6)} %copy.20.lengths_ref, bf16[8,128,256]{2,1,0:T(8,128)(2,1)} %get-tuple-element.26.norm_ref, ...), custom_call_target="tpu_custom_call", output_to_operand_aliasing={{0}: (6, {}), {1}: (7, {}), {2}: (8, {}), {3}: (9, {})} | custom-call | flops 6000000000 | bytes 4194304 | tf_op jit(solution)/shard_map/output_ahead/pallas_call | solution.py:445
  27.0 16.0 %all-to-all-done.got_ref = bf16[32,2,2,32,128]{4,3,2,1,0:T(8,128)(2,1)S(1)} async-done(((bf16[32,2,2,32,128]{4,3,2,1,0:T(8,128)(2,1)}), bf16[32,2,2,32,128]{4,3,2,1,0:T(8,128)(2,1)S(1)}, u32[]{:S(2)}, u32[]{:S(2)}) %all-to-all-start) | async-done | bytes 1048608 | tf_op jit(solution)/shard_map/all_to_all | solution.py:382
  43.0 0.5 product.1
  43.5 19.9 %all_to_all.35.got_ref = bf16[32,2,32,128]{3,2,1,0:T(8,128)(2,1)S(1)} all-to-all(bf16[32,2,32,128]{3,2,1,0:T(8,128)(2,1)S(1)} %get-tuple-element.33), channel_id=1, replica_groups=mesh['dp'=16,'dap'=32] {'dap'}, dimensions={0} | all-to-all | bytes 1048576 | tf_op jit(solution)/shard_map/all_to_all | solution.py:382
  63.4 0.7 output_back.1
  64.1 18.2 %all_to_all.36.got_ref = bf16[32,2,32,128]{3,2,1,0:T(8,128)(2,1)S(1)} all-to-all(bf16[32,2,32,128]{3,2,1,0:T(8,128)(2,1)S(1)} %output_back.1), channel_id=1, replica_groups=mesh['dp'=16,'dap'=32] {'dap'}, dimensions={0} | all-to-all | bytes 1048576 | tf_op jit(solution)/shard_map/all_to_all | solution.py:382
  82.3 1.7 %operands_back.1 = bf16[32,2,2,32,128]{4,3,2,1,0:T(8,128)(2,1)} custom-call(bf16[32,2,32,128]{3,2,1,0:T(8,128)(2,1)S(1)} %all_to_all.36.got_ref, bf16[2,2,4,256,128]{4,3,2,1,0:T(8,128)(2,1)S(1)} %get-tuple-element.35.held_ref), custom_call_target="tpu_custom_call" | custom-call | flops 1000000000 | bytes 4194304 | tf_op jit(solution)/shard_map/operands_back/pallas_call | solution.py:469
  84.0 5.6 %all-to-all-start.3 = ((bf16[32,2,2,32,128]{4,3,2,1,0:T(8,128)(2,1)}), bf16[32,2,2,32,128]{4,3,2,1,0:T(8,128)(2,1)S(1)}, u32[]{:S(2)}, u32[]{:S(2)}) async-start(bf16[32,2,2,32,128]{4,3,2,1,0:T(8,128)(2,1)} %operands_back.1), calls=%async_computation.3 | async-start | bytes 2097152 | tf_op jit(solution)/shard_map/all_to_all | solution.py:382
  89.6 0.0 copy-start.1
  89.7 1.0 copy-done.1
  90.7 1.0 copy-done.4
  91.7 1.2 copy-done.11
  93.0 1.0 copy-done.12
  94.0 2.2 %output_weights.1 = (bf16[8,128,256]{2,1,0:T(8,128)(2,1)S(1)}, f32[2,128,128]{2,1,0:T(8,128)S(1)}) custom-call(bf16[32,2,32,128]{3,2,1,0:T(8,128)(2,1)S(1)} %copy-done.4, bf16[8,128,256]{2,1,0:T(8,128)(2,1)S(1)} %copy-done.1, bf16[8,128,256]{2,1,0:T(8,128)(2,1)S(1)} %copy-done.12, f32[8,128,256]{2,1,0:T(8,128)S(1)} %copy-done.11, ...), custom_call_target="tpu_custom_call" | custom-call | flops 4000000000 | bytes 4194304 | tf_op jit(solution)/shard_map/output_weights/pallas_call | solution.py:463
  96.3 0.8 copy-done.13
  97.0 11.8 %all-to-all-done.3.got_ref = bf16[32,2,2,32,128]{4,3,2,1,0:T(8,128)(2,1)S(1)} async-done(((bf16[32,2,2,32,128]{4,3,2,1,0:T(8,128)(2,1)}), bf16[32,2,2,32,128]{4,3,2,1,0:T(8,128)(2,1)S(1)}, u32[]{:S(2)}, u32[]{:S(2)}) %all-to-all-start.3) | async-done | bytes 1048608 | tf_op jit(solution)/shard_map/all_to_all | solution.py:382
  108.8 1.0 copy-done.2
  109.9 0.9 input_weights.1
  110.8 16.6 %all_to_all.37.got_ref = bf16[32,24,128]{2,1,0:T(8,128)(2,1)S(1)} all-to-all(bf16[32,24,128]{2,1,0:T(8,128)(2,1)S(1)} %bitcast.9), channel_id=1, replica_groups=mesh['dp'=16,'dap'=32] {'dap'}, dimensions={0} | all-to-all | bytes 393216 | tf_op jit(solution)/shard_map/all_to_all | solution.py:382
  127.5 0.0 copy-start.6
  127.5 0.0 copy-start.8
  127.5 24.5 %all_to_all.38.got_ref = bf16[16,24,128]{2,1,0:T(8,128)(2,1)S(1)} all-to-all(bf16[16,24,128]{2,1,0:T(8,128)(2,1)S(1)} %fold_inner.1), channel_id=1, replica_groups=mesh['dp'=16,'dap'=32] {'dp'}, dimensions={0} | all-to-all | bytes 196608 | tf_op jit(solution)/shard_map/all_to_all | solution.py:382
  152.0 0.7 fold_outer.1
  152.7 4.0 %all-to-all-start.6 = ((bf16[32,24,128]{2,1,0:T(8,128)(2,1)}), bf16[32,24,128]{2,1,0:T(8,128)(2,1)S(1)}, u32[]{:S(2)}, u32[]{:S(2)}) async-start(bf16[32,24,128]{2,1,0:T(8,128)(2,1)} %fold_outer.1), calls=%async_computation.6 | async-start | bytes 393216 | tf_op jit(solution)/shard_map/all_to_all | solution.py:382
  156.7 0.0 copy-start.5
  156.7 1.0 copy-done.5
  157.7 1.0 copy-done.14
  158.8 2.5 %input_back.1 = bf16[8,256,128]{2,1,0:T(8,128)(2,1)} custom-call(bf16[32,2,2,32,128]{4,3,2,1,0:T(8,128)(2,1)S(1)} %all-to-all-done.3.got_ref, bf16[8,4,128,256]{3,2,1,0:T(8,128)(2,1)S(1)} %copy-done, bf16[8,128,256]{2,1,0:T(8,128)(2,1)S(1)} %copy-done.14, bf16[8,256,128]{2,1,0:T(8,128)(2,1)S(1)} %bitcast.12, bf16[128,640]{1,0:T(8,128)(2,1)S(1)} %copy-done.6, ...), custom_call_target="tpu_custom_call" | custom-call | flops 6000000000 | bytes 4194304 | tf_op jit(solution)/shard_map/input_back/pallas_call | solution.py:481
  161.3 5.2 %all-to-all-done.6 = bf16[32,24,128]{2,1,0:T(8,128)(2,1)S(1)} async-done(((bf16[32,24,128]{2,1,0:T(8,128)(2,1)}), bf16[32,24,128]{2,1,0:T(8,128)(2,1)S(1)}, u32[]{:S(2)}, u32[]{:S(2)}) %all-to-all-start.6) | async-done | bytes 196640 | tf_op jit(solution)/shard_map/all_to_all | solution.py:382
  166.5 0.8 finish.1
  (19 shorter events, 0.1 us)
Async XLA Ops:
  7.8 35.2 %all-to-all-start = ((bf16[32,2,2,32,128]{4,3,2,1,0:T(8,128)(2,1)}), bf16[32,2,2,32,128]{4,3,2,1,0:T(8,128)(2,1)S(1)}, u32[]{:S(2)}, u32[]{:S(2)}) async-start(bf16[32,2,2,32,128]{4,3,2,1,0:T(8,128)(2,1)} %get-tuple-element.25), calls=%async_computation | async-start | bytes 2097152 | tf_op jit(solution)/shard_map/all_to_all | solution.py:382
  43.0 20.5 %copy-start.10 = (f32[2,1024,128]{2,1,0:T(8,128)S(1)}, f32[2,1024,128]{2,1,0:T(8,128)}, u32[]{:S(2)}) copy-start(f32[2,1024,128]{2,1,0:T(8,128)} %get-tuple-element.34.upstream_ref) | copy-start | bytes 3145732
  63.4 18.9 %copy-start.3 = (bf16[32,2,32,128]{3,2,1,0:T(8,128)(2,1)}, bf16[32,2,32,128]{3,2,1,0:T(8,128)(2,1)S(1)}, u32[]{:S(2)}) copy-start(bf16[32,2,32,128]{3,2,1,0:T(8,128)(2,1)S(1)} %all_to_all.35.got_ref) | copy-start | bytes 1572868
  82.3 7.3 %copy-start.7 = (bf16[128,128]{1,0:T(8,128)(2,1)S(1)}, bf16[128,128]{1,0:T(8,128)(2,1)}, u32[]{:S(2)}) copy-start(bf16[128,128]{1,0:T(8,128)(2,1)} %refs_3_.1) | copy-start | bytes 98308
  82.3 7.3 %copy-start.9 = (f32[128]{0:T(128)S(1)}, f32[128]{0:T(128)}, u32[]{:S(2)}) copy-start(f32[128]{0:T(128)} %param.13) | copy-start | bytes 1540
  84.0 24.8 %all-to-all-start.3 = ((bf16[32,2,2,32,128]{4,3,2,1,0:T(8,128)(2,1)}), bf16[32,2,2,32,128]{4,3,2,1,0:T(8,128)(2,1)S(1)}, u32[]{:S(2)}, u32[]{:S(2)}) async-start(bf16[32,2,2,32,128]{4,3,2,1,0:T(8,128)(2,1)} %operands_back.1), calls=%async_computation.3 | async-start | bytes 2097152 | tf_op jit(solution)/shard_map/all_to_all | solution.py:382
  89.6 1.0 copy-start.1
  90.7 1.0 copy-start.4
  91.7 1.2 copy-start.11
  93.0 1.0 copy-start.12
  94.0 14.8 %copy-start = (bf16[8,4,128,256]{3,2,1,0:T(8,128)(2,1)S(1)}, bf16[8,4,128,256]{3,2,1,0:T(8,128)(2,1)}, u32[]{:S(2)}) copy-start(bf16[8,4,128,256]{3,2,1,0:T(8,128)(2,1)} %get-tuple-element.36.factors_ref) | copy-start | bytes 6291460
  96.2 0.8 copy-start.13
  108.8 1.0 copy-start.2
  127.5 29.2 %copy-start.6 = (bf16[128,640]{1,0:T(8,128)(2,1)S(1)}, bf16[128,640]{1,0:T(8,128)(2,1)}, u32[]{:S(2)}) copy-start(bf16[128,640]{1,0:T(8,128)(2,1)} %refs_1_.1) | copy-start | bytes 491524
  127.5 29.2 %copy-start.8 = (f32[128]{0:T(128)S(1)}, f32[128]{0:T(128)}, u32[]{:S(2)}) copy-start(f32[128]{0:T(128)} %param.11) | copy-start | bytes 1540
  152.7 13.8 %all-to-all-start.6 = ((bf16[32,24,128]{2,1,0:T(8,128)(2,1)}), bf16[32,24,128]{2,1,0:T(8,128)(2,1)S(1)}, u32[]{:S(2)}, u32[]{:S(2)}) async-start(bf16[32,24,128]{2,1,0:T(8,128)(2,1)} %fold_outer.1), calls=%async_computation.6 | async-start | bytes 393216 | tf_op jit(solution)/shard_map/all_to_all | solution.py:382
  156.7 1.0 copy-start.5
  157.7 1.0 copy-start.14

commit v5 on v4

--- a/solution.py
+++ b/solution.py
@@ -56,9 +56,16 @@
 
 
 def transposed_blocks(w_ref, wt_ref):
-    for n in range(wt_ref.shape[0]):
-        block = w_ref[:, n * LANES : (n + 1) * LANES]
-        wt_ref[n] = jnp.transpose(block.astype(F32)).astype(BF16)
+    eye = identity(LANES)
+    for n in range(wt_ref.shape[0] // LANES):
+        rows = slice(n * LANES, (n + 1) * LANES)
+        wt_ref[rows] = dot(eye, w_ref[:, rows], NT).astype(BF16)
+
+
+def projections(wt_ref, norm, blocks):
+    channels = norm.shape[0]
+    whole = dot(wt_ref[: blocks * channels], norm, NN)
+    return [whole[n * channels : (n + 1) * channels] for n in range(blocks)]
 
 
 def output_ahead(
@@ -73,7 +80,8 @@
     for i in range(rows):
         norm = norm_ref[i]
         cotangent = dot(eye, cotangent_ref[i], NT)
-        out_gate = sigmoid(dot(wt_ref[4], norm, NN))
+        projected = projections(wt_ref, norm, 5)
+        out_gate = sigmoid(projected[4])
         gated = cotangent * out_gate
         slope_ref[i] = gated * (1.0 - out_gate)
         gated = gated.astype(BF16)
@@ -86,20 +94,18 @@
             ]
         mask = row_of_masks(length, i, rows, width)
         for side in range(2):
-            value = dot(wt_ref[2 * side], norm, NN)
-            gate = sigmoid(dot(wt_ref[2 * side + 1], norm, NN))
+            value, gate = projected[2 * side], sigmoid(projected[2 * side + 1])
             masked = mask * gate
             factors_ref[i, 2 * side] = masked.astype(BF16)
             factors_ref[i, 2 * side + 1] = (masked * value * (1.0 - gate)).astype(BF16)
-        for n in range(1, 4):
+        if 2 * (i + 1) % rows == 0:
+            some = pl.ds(i + 1 - rows // 2, rows // 2)
             copies.append(
-                pltpu.make_async_copy(stages[n].at[i], outs[n].at[i], sems.at[n, i])
+                pltpu.make_async_copy(factors_ref.at[some], outs[1].at[some], sems.at[1, i])
             )
             copies[-1].start()
-    for half in range(width // LANES):
-        copies.append(
-            pltpu.make_async_copy(upstream_ref.at[half], outs[0].at[half], sems.at[0, half])
-        )
+    for n in (0, 2, 3):
+        copies.append(pltpu.make_async_copy(stages[n], outs[n], sems.at[n, 0]))
         copies[-1].start()
     for copy in copies:
         copy.wait()
@@ -118,69 +124,63 @@
     wt_ref, stage_ref, send_ref, norm_ref, sems, in_sems = rest[14:]
     rows, width, channels = pair_ref.shape
     length = lengths_ref[0]
-    whole = [
-        pltpu.make_async_copy(source, target, in_sems.at[2, n])
-        for n, (source, target) in enumerate(
-            (
-                (w_hbm, w_ref),
-                (gain_hbm, gain_ref),
-                (w_out_hbm, w_out_ref),
-                (gain_out_hbm, gain_out_ref),
-            )
-        )
+    def fetch(source, target, n):
+        return pltpu.make_async_copy(source, target, in_sems.at[n])
+
+    first = [
+        fetch(w_hbm, w_ref, 0),
+        fetch(gain_hbm, gain_ref, 1),
+        fetch(pair_hbm.at[: rows // 2], pair_ref.at[: rows // 2], 2),
+        fetch(pair_hbm.at[rows // 2 :], pair_ref.at[rows // 2 :], 3),
     ]
-    by_row = [
-        [
-            pltpu.make_async_copy(source.at[i], target.at[i], in_sems.at[n, i])
-            for i in range(rows)
-        ]
-        for n, (source, target) in enumerate(
-            ((pair_hbm, pair_ref), (cotangent_hbm, cotangent_ref))
-        )
+    later = [
+        fetch(cotangent_hbm, cotangent_ref, 4),
+        fetch(w_out_hbm, w_out_ref, 5),
+        fetch(gain_out_hbm, gain_out_ref, 6),
     ]
-    for copy in whole[:2] + by_row[0] + whole[2:] + by_row[1]:
+    for copy in first:
         copy.start()
+
+    @pl.when(first_core())
+    def _():
+        for copy in later:
+            copy.start()
+
     eye = identity(channels)
-    whole[0].wait()
+    first[0].wait()
     transposed_blocks(w_ref, wt_ref)
-    whole[1].wait()
+    first[1].wait()
     gain = wide(column(gain_ref[...], channels), width)
-    done = []
     for i in range(rows):
-        by_row[0][i].wait()
+        if 2 * i % rows == 0:
+            first[2 + 2 * i // rows].wait()
         hat, _ = norm_sublanes(dot(eye, pair_ref[i], NT))
         norm = (hat * gain).astype(BF16)
         norm_ref[i] = norm
-        done.append(pltpu.make_async_copy(norm_ref.at[i], norm_hbm.at[i], in_sems.at[3, i]))
-        done[-1].start()
+        projected = projections(wt_ref, norm, 4)
         mask = row_of_masks(length, i, rows, width)
         for side in range(2):
-            value = dot(wt_ref[2 * side], norm, NN)
-            gate = sigmoid(dot(wt_ref[2 * side + 1], norm, NN))
+            value, gate = projected[2 * side], sigmoid(projected[2 * side + 1])
             value = mask * gate * value
             for half in range(width // LANES):
                 stage_ref[side, half, pl.ds(i, channels, stride=rows), :] = value[
                     :, half * LANES : (half + 1) * LANES
                 ]
+    done = [fetch(norm_ref, norm_hbm, 7)]
+    done[0].start()
     peers = send_ref.shape[0]
     for side in range(2):
         for half in range(width // LANES):
             send_ref[:, side, half] = (
                 stage_ref[side, half].reshape(peers, -1, LANES).astype(BF16)
             )
-            done.append(
-                pltpu.make_async_copy(
-                    send_ref.at[:, side, half],
-                    send_hbm.at[:, side, half],
-                    in_sems.at[2, 4 + 2 * side + half],
-                )
-            )
-            done[-1].start()
-    for copy in whole[2:] + by_row[1]:
-        copy.wait()
+        done.append(fetch(send_ref.at[:, side], send_hbm.at[:, side], 8 + side))
+        done[-1].start()
 
     @pl.when(first_core())
     def _():
+        for copy in later:
+            copy.wait()
         output_ahead(
             length, norm_ref, cotangent_ref, wt_ref, w_out_ref, gain_out_ref, outs, stages, sems
         )
@@ -420,7 +420,7 @@
         (flat, F32),
     ]
     ahead_outs = [(shape, dtype, HBM) for shape, dtype in ahead]
-    transposed = ((5,) + square, BF16)
+    transposed = ((5 * channels, channels), BF16)
     send, norm, *ahead_parts = call(
         project_kernel, "project", [SMEM] + [HBM] * 6,
         [(two_sides, BF16, HBM), (flat, BF16, HBM)] + ahead_outs,
@@ -437,7 +437,7 @@
             (two_sides, BF16),
             (flat, BF16),
             COPIES((4, rows)),
-            COPIES((4, rows)),
+            COPIES((10,)),
         ],
         grant=60,
     )(lengths, pair, cotangent, w_in, gain_in, w_out, gain_out)

time: 168 us -> 165 us (0.982)
  waiting for transfers between devices: 33 us -> 28.7 us
    all_to_all x3, waiting for transfers between devices: 33 us -> 28.7 us  [exchange(): return lax.all_to_all(values, axis, split_axis=0, concat_axis=0, tiled=True)]
    pallas_call x1, Pallas kernels: 6.48 us -> 4.75 us  [per_device(): call(project_kernel, 'project', [SMEM] + [HBM] * 6, [(two_sides, BF16, HB...]
  transfers between devices with their start and end apart: 3 -> 3, of which waited for: 3 -> 3; matrix products, arithmetic and copies ran while one was open for 0% -> 0% of each run, Pallas kernels for 6% -> 7%
where the time goes in v5:
time: 165 us; the launch traced here: 164 us
  blocking collectives  80.2 us (49%)
  waiting for transfers between devices  28.7 us (17%)
  starting transfers between devices  23.5 us (14%)
  Pallas kernels  21.5 us (13%)
  local copies, waits for them, and re-layouts  8.28 us (5%)
    all_to_all x4, blocking collectives, exchange(): return lax.all_to_all(values, axis, split_axis=0, concat_axis=0, tiled=True)  80.2 us
    all_to_all x3, waiting for transfers between devices, exchange(): return lax.all_to_all(values, axis, split_axis=0, concat_axis=0, tiled=True)  28.7 us
    all_to_all x3, starting transfers between devices, exchange(): return lax.all_to_all(values, axis, split_axis=0, concat_axis=0, tiled=True)  23.5 us
    unnamed x30, local copies, waits for them, and re-layouts  8.28 us
    pallas_call x1, Pallas kernels, per_device(): call(output_ahead_kernel, 'output_ahead', [SMEM] + [VMEM] * 5 + [HBM] * 4...  6.6 us
    pallas_call x1, Pallas kernels, per_device(): call(project_kernel, 'project', [SMEM] + [HBM] * 6, [(two_sides, BF16, HB...  4.75 us
  transfers between devices with their start and end apart: 3, of which 3 were waited for; matrix products, arithmetic and copies ran while one was open for 0% of the time, Pallas kernels for 7%

profile of v5, /device:TPU:1, one launch (start us, length us, event | category | flops | bytes accessed | tf_op | source)
XLA Modules:
  0.0 163.6 jit_solution(17458854556697101729)
XLA Ops:
  1.3 4.8 %project.1 = (bf16[32,2,2,32,128]{4,3,2,1,0:T(8,128)(2,1)}, bf16[8,128,256]{2,1,0:T(8,128)(2,1)}, f32[2,1024,128]{2,1,0:T(8,128)}, bf16[8,4,128,256]{3,2,1,0:T(8...) custom-call(s32[1]{0:T(128)S(6)} %copy.20.lengths_ref, bf16[8,256,128]{2,1,0:T(8,128)(2,1)} %bitcast.11, ...), custom_call_target="tpu_custom_call" | custom-call | flops 1000000000 | bytes 4194304 | tf_op jit(solution)/shard_map/project/pallas_call | solution.py:424
  6.0 13.7 %all-to-all-start = ((bf16[32,2,2,32,128]{4,3,2,1,0:T(8,128)(2,1)}), bf16[32,2,2,32,128]{4,3,2,1,0:T(8,128)(2,1)S(1)}, u32[]{:S(2)}, u32[]{:S(2)}) async-start(bf16[32,2,2,32,128]{4,3,2,1,0:T(8,128)(2,1)} %get-tuple-element.25), calls=%async_computation | async-start | bytes 2097152 | tf_op jit(solution)/shard_map/all_to_all | solution.py:382
  19.8 6.6 %output_ahead.1 = (f32[2,1024,128]{2,1,0:T(8,128)}, bf16[8,4,128,256]{3,2,1,0:T(8,128)(2,1)}, bf16[8,128,256]{2,1,0:T(8,128)(2,1)}, f32[8,128,256]{2,1,0:T(8,128)}) custom-call(s32[1]{0:T(128)S(6)} %copy.20.lengths_ref, bf16[8,128,256]{2,1,0:T(8,128)(2,1)} %get-tuple-element.26.norm_ref, ...), custom_call_target="tpu_custom_call", output_to_operand_aliasing={{0}: (6, {}), {1}: (7, {}), {2}: (8, {}), {3}: (9, {})} | custom-call | flops 6000000000 | bytes 4194304 | tf_op jit(solution)/shard_map/output_ahead/pallas_call | solution.py:445
  26.4 13.1 %all-to-all-done.got_ref = bf16[32,2,2,32,128]{4,3,2,1,0:T(8,128)(2,1)S(1)} async-done(((bf16[32,2,2,32,128]{4,3,2,1,0:T(8,128)(2,1)}), bf16[32,2,2,32,128]{4,3,2,1,0:T(8,128)(2,1)S(1)}, u32[]{:S(2)}, u32[]{:S(2)}) %all-to-all-start) | async-done | bytes 1048608 | tf_op jit(solution)/shard_map/all_to_all | solution.py:382
  39.5 0.5 product.1
  40.0 21.0 %all_to_all.35.got_ref = bf16[32,2,32,128]{3,2,1,0:T(8,128)(2,1)S(1)} all-to-all(bf16[32,2,32,128]{3,2,1,0:T(8,128)(2,1)S(1)} %get-tuple-element.33), channel_id=1, replica_groups=mesh['dp'=16,'dap'=32] {'dap'}, dimensions={0} | all-to-all | bytes 1048576 | tf_op jit(solution)/shard_map/all_to_all | solution.py:382
  61.0 0.7 output_back.1
  61.7 16.7 %all_to_all.36.got_ref = bf16[32,2,32,128]{3,2,1,0:T(8,128)(2,1)S(1)} all-to-all(bf16[32,2,32,128]{3,2,1,0:T(8,128)(2,1)S(1)} %output_back.1), channel_id=1, replica_groups=mesh['dp'=16,'dap'=32] {'dap'}, dimensions={0} | all-to-all | bytes 1048576 | tf_op jit(solution)/shard_map/all_to_all | solution.py:382
  78.4 1.7 %operands_back.1 = bf16[32,2,2,32,128]{4,3,2,1,0:T(8,128)(2,1)} custom-call(bf16[32,2,32,128]{3,2,1,0:T(8,128)(2,1)S(1)} %all_to_all.36.got_ref, bf16[2,2,4,256,128]{4,3,2,1,0:T(8,128)(2,1)S(1)} %get-tuple-element.35.held_ref), custom_call_target="tpu_custom_call" | custom-call | flops 1000000000 | bytes 4194304 | tf_op jit(solution)/shard_map/operands_back/pallas_call | solution.py:469
  80.1 5.8 %all-to-all-start.3 = ((bf16[32,2,2,32,128]{4,3,2,1,0:T(8,128)(2,1)}), bf16[32,2,2,32,128]{4,3,2,1,0:T(8,128)(2,1)S(1)}, u32[]{:S(2)}, u32[]{:S(2)}) async-start(bf16[32,2,2,32,128]{4,3,2,1,0:T(8,128)(2,1)} %operands_back.1), calls=%async_computation.3 | async-start | bytes 2097152 | tf_op jit(solution)/shard_map/all_to_all | solution.py:382
  85.9 0.0 copy-start.1
  86.0 1.0 copy-done.1
  87.0 1.0 copy-done.4
  88.0 1.2 copy-done.11
  89.3 1.0 copy-done.12
  90.3 2.2 %output_weights.1 = (bf16[8,128,256]{2,1,0:T(8,128)(2,1)S(1)}, f32[2,128,128]{2,1,0:T(8,128)S(1)}) custom-call(bf16[32,2,32,128]{3,2,1,0:T(8,128)(2,1)S(1)} %copy-done.4, bf16[8,128,256]{2,1,0:T(8,128)(2,1)S(1)} %copy-done.1, bf16[8,128,256]{2,1,0:T(8,128)(2,1)S(1)} %copy-done.12, f32[8,128,256]{2,1,0:T(8,128)S(1)} %copy-done.11, ...), custom_call_target="tpu_custom_call" | custom-call | flops 4000000000 | bytes 4194304 | tf_op jit(solution)/shard_map/output_weights/pallas_call | solution.py:463
  92.6 0.8 copy-done.13
  93.3 10.4 %all-to-all-done.3.got_ref = bf16[32,2,2,32,128]{4,3,2,1,0:T(8,128)(2,1)S(1)} async-done(((bf16[32,2,2,32,128]{4,3,2,1,0:T(8,128)(2,1)}), bf16[32,2,2,32,128]{4,3,2,1,0:T(8,128)(2,1)S(1)}, u32[]{:S(2)}, u32[]{:S(2)}) %all-to-all-start.3) | async-done | bytes 1048608 | tf_op jit(solution)/shard_map/all_to_all | solution.py:382
  103.8 1.0 copy-done.2
  104.8 0.9 input_weights.1
  105.7 17.4 %all_to_all.37.got_ref = bf16[32,24,128]{2,1,0:T(8,128)(2,1)S(1)} all-to-all(bf16[32,24,128]{2,1,0:T(8,128)(2,1)S(1)} %bitcast.9), channel_id=1, replica_groups=mesh['dp'=16,'dap'=32] {'dap'}, dimensions={0} | all-to-all | bytes 393216 | tf_op jit(solution)/shard_map/all_to_all | solution.py:382
  123.1 0.0 copy-start.6
  123.1 0.0 copy-start.8
  123.1 25.1 %all_to_all.38.got_ref = bf16[16,24,128]{2,1,0:T(8,128)(2,1)S(1)} all-to-all(bf16[16,24,128]{2,1,0:T(8,128)(2,1)S(1)} %fold_inner.1), channel_id=1, replica_groups=mesh['dp'=16,'dap'=32] {'dp'}, dimensions={0} | all-to-all | bytes 196608 | tf_op jit(solution)/shard_map/all_to_all | solution.py:382
  148.3 0.7 fold_outer.1
  149.0 4.0 %all-to-all-start.6 = ((bf16[32,24,128]{2,1,0:T(8,128)(2,1)}), bf16[32,24,128]{2,1,0:T(8,128)(2,1)S(1)}, u32[]{:S(2)}, u32[]{:S(2)}) async-start(bf16[32,24,128]{2,1,0:T(8,128)(2,1)} %fold_outer.1), calls=%async_computation.6 | async-start | bytes 393216 | tf_op jit(solution)/shard_map/all_to_all | solution.py:382
  153.0 0.0 copy-start.5
  153.0 1.0 copy-done.5
  154.0 1.0 copy-done.14
  155.1 2.5 %input_back.1 = bf16[8,256,128]{2,1,0:T(8,128)(2,1)} custom-call(bf16[32,2,2,32,128]{4,3,2,1,0:T(8,128)(2,1)S(1)} %all-to-all-done.3.got_ref, bf16[8,4,128,256]{3,2,1,0:T(8,128)(2,1)S(1)} %copy-done, bf16[8,128,256]{2,1,0:T(8,128)(2,1)S(1)} %copy-done.14, bf16[8,256,128]{2,1,0:T(8,128)(2,1)S(1)} %bitcast.12, bf16[128,640]{1,0:T(8,128)(2,1)S(1)} %copy-done.6, ...), custom_call_target="tpu_custom_call" | custom-call | flops 6000000000 | bytes 4194304 | tf_op jit(solution)/shard_map/input_back/pallas_call | solution.py:481
  157.6 5.2 %all-to-all-done.6 = bf16[32,24,128]{2,1,0:T(8,128)(2,1)S(1)} async-done(((bf16[32,24,128]{2,1,0:T(8,128)(2,1)}), bf16[32,24,128]{2,1,0:T(8,128)(2,1)S(1)}, u32[]{:S(2)}, u32[]{:S(2)}) %all-to-all-start.6) | async-done | bytes 196640 | tf_op jit(solution)/shard_map/all_to_all | solution.py:382
  162.8 0.8 finish.1
  (19 shorter events, 0.1 us)
Async XLA Ops:
  6.0 33.4 %all-to-all-start = ((bf16[32,2,2,32,128]{4,3,2,1,0:T(8,128)(2,1)}), bf16[32,2,2,32,128]{4,3,2,1,0:T(8,128)(2,1)S(1)}, u32[]{:S(2)}, u32[]{:S(2)}) async-start(bf16[32,2,2,32,128]{4,3,2,1,0:T(8,128)(2,1)} %get-tuple-element.25), calls=%async_computation | async-start | bytes 2097152 | tf_op jit(solution)/shard_map/all_to_all | solution.py:382
  39.5 21.5 %copy-start.10 = (f32[2,1024,128]{2,1,0:T(8,128)S(1)}, f32[2,1024,128]{2,1,0:T(8,128)}, u32[]{:S(2)}) copy-start(f32[2,1024,128]{2,1,0:T(8,128)} %get-tuple-element.34.upstream_ref) | copy-start | bytes 3145732
  61.0 17.4 %copy-start.3 = (bf16[32,2,32,128]{3,2,1,0:T(8,128)(2,1)}, bf16[32,2,32,128]{3,2,1,0:T(8,128)(2,1)S(1)}, u32[]{:S(2)}) copy-start(bf16[32,2,32,128]{3,2,1,0:T(8,128)(2,1)S(1)} %all_to_all.35.got_ref) | copy-start | bytes 1572868
  78.4 7.6 %copy-start.7 = (bf16[128,128]{1,0:T(8,128)(2,1)S(1)}, bf16[128,128]{1,0:T(8,128)(2,1)}, u32[]{:S(2)}) copy-start(bf16[128,128]{1,0:T(8,128)(2,1)} %refs_3_.1) | copy-start | bytes 98308
  78.4 7.6 %copy-start.9 = (f32[128]{0:T(128)S(1)}, f32[128]{0:T(128)}, u32[]{:S(2)}) copy-start(f32[128]{0:T(128)} %param.13) | copy-start | bytes 1540
  80.1 23.7 %all-to-all-start.3 = ((bf16[32,2,2,32,128]{4,3,2,1,0:T(8,128)(2,1)}), bf16[32,2,2,32,128]{4,3,2,1,0:T(8,128)(2,1)S(1)}, u32[]{:S(2)}, u32[]{:S(2)}) async-start(bf16[32,2,2,32,128]{4,3,2,1,0:T(8,128)(2,1)} %operands_back.1), calls=%async_computation.3 | async-start | bytes 2097152 | tf_op jit(solution)/shard_map/all_to_all | solution.py:382
  85.9 1.0 copy-start.1
  87.0 1.0 copy-start.4
  88.0 1.2 copy-start.11
  89.3 1.0 copy-start.12
  90.3 13.5 %copy-start = (bf16[8,4,128,256]{3,2,1,0:T(8,128)(2,1)S(1)}, bf16[8,4,128,256]{3,2,1,0:T(8,128)(2,1)}, u32[]{:S(2)}) copy-start(bf16[8,4,128,256]{3,2,1,0:T(8,128)(2,1)} %get-tuple-element.36.factors_ref) | copy-start | bytes 6291460
  92.5 0.8 copy-start.13
  103.8 1.0 copy-start.2
  123.1 29.9 %copy-start.6 = (bf16[128,640]{1,0:T(8,128)(2,1)S(1)}, bf16[128,640]{1,0:T(8,128)(2,1)}, u32[]{:S(2)}) copy-start(bf16[128,640]{1,0:T(8,128)(2,1)} %refs_1_.1) | copy-start | bytes 491524
  123.1 29.9 %copy-start.8 = (f32[128]{0:T(128)S(1)}, f32[128]{0:T(128)}, u32[]{:S(2)}) copy-start(f32[128]{0:T(128)} %param.11) | copy-start | bytes 1540
  149.0 13.8 %all-to-all-start.6 = ((bf16[32,24,128]{2,1,0:T(8,128)(2,1)}), bf16[32,24,128]{2,1,0:T(8,128)(2,1)S(1)}, u32[]{:S(2)}, u32[]{:S(2)}) async-start(bf16[32,24,128]{2,1,0:T(8,128)(2,1)} %fold_outer.1), calls=%async_computation.6 | async-start | bytes 393216 | tf_op jit(solution)/shard_map/all_to_all | solution.py:382
  153.0 1.0 copy-start.5
  154.0 1.0 copy-start.14

commit v6 on v5

--- a/solution.py
+++ b/solution.py
@@ -79,7 +79,7 @@
     copies = []
     for i in range(rows):
         norm = norm_ref[i]
-        cotangent = dot(eye, cotangent_ref[i], NT)
+        cotangent = jnp.transpose(cotangent_ref[i].astype(F32))
         projected = projections(wt_ref, norm, 5)
         out_gate = sigmoid(projected[4])
         gated = cotangent * out_gate
@@ -151,31 +151,35 @@
     transposed_blocks(w_ref, wt_ref)
     first[1].wait()
     gain = wide(column(gain_ref[...], channels), width)
-    for i in range(rows):
-        if 2 * i % rows == 0:
-            first[2 + 2 * i // rows].wait()
-        hat, _ = norm_sublanes(dot(eye, pair_ref[i], NT))
-        norm = (hat * gain).astype(BF16)
-        norm_ref[i] = norm
-        projected = projections(wt_ref, norm, 4)
-        mask = row_of_masks(length, i, rows, width)
-        for side in range(2):
-            value, gate = projected[2 * side], sigmoid(projected[2 * side + 1])
-            value = mask * gate * value
+    peers = send_ref.shape[0]
+    done = []
+    for side in range(2):
+        for i in range(rows):
+            if side == 0:
+                if 2 * i % rows == 0:
+                    first[2 + 2 * i // rows].wait()
+                hat, _ = norm_sublanes(jnp.transpose(pair_ref[i].astype(F32)))
+                norm = (hat * gain).astype(BF16)
+                norm_ref[i] = norm
+            else:
+                norm = norm_ref[i]
+            blocks = slice(2 * side * channels, 2 * (side + 1) * channels)
+            projected = dot(wt_ref[blocks], norm, NN)
+            mask = row_of_masks(length, i, rows, width)
+            value = mask * sigmoid(projected[channels:]) * projected[:channels]
             for half in range(width // LANES):
                 stage_ref[side, half, pl.ds(i, channels, stride=rows), :] = value[
                     :, half * LANES : (half + 1) * LANES
                 ]
-    done = [fetch(norm_ref, norm_hbm, 7)]
-    done[0].start()
-    peers = send_ref.shape[0]
-    for side in range(2):
         for half in range(width // LANES):
             send_ref[:, side, half] = (
                 stage_ref[side, half].reshape(peers, -1, LANES).astype(BF16)
             )
         done.append(fetch(send_ref.at[:, side], send_hbm.at[:, side], 8 + side))
         done[-1].start()
+        if side == 0:
+            done.append(fetch(norm_ref, norm_hbm, 7))
+            done[-1].start()
 
     @pl.when(first_core())
     def _():
@@ -215,14 +219,13 @@
     for side in range(2):
         for half in range(halves):
             for c, block in enumerate(regroup(got_ref[:, side, half], group)):
-                held_ref[side, half, c] = block
+                held_ref[side, c, :, half * LANES : (half + 1) * LANES] = block
     for c in range(group):
+        total = dot(held_ref[0, c], held_ref[1, c], NT)
         for out in range(halves):
-            right_rows = pl.ds(out * LANES, LANES)
-            total = dot(held_ref[0, 0, c], held_ref[1, 0, c, right_rows, :], NT)
-            for half in range(1, halves):
-                total = total + dot(held_ref[0, half, c], held_ref[1, half, c, right_rows, :], NT)
-            stage_ref[out, :, c * SUB : (c + 1) * SUB, :] = total.reshape(peers, SUB, LANES)
+            stage_ref[out, :, c * SUB : (c + 1) * SUB, :] = total[
+                :, out * LANES : (out + 1) * LANES
+            ].reshape(peers, SUB, LANES)
     for out in range(halves):
         send_ref[:, out] = stage_ref[out].astype(BF16)
 
@@ -269,27 +272,29 @@
     sums_ref[1] = w_out_sum
 
 
-def operands_back_kernel(got_ref, held_ref, send_ref, stage_ref):
+def operands_back_kernel(got_ref, held_ref, send_hbm, stage_ref, send_ref, sems):
     peers, halves, packed, _ = got_ref.shape
     group = packed // SUB
     blocks = [regroup(got_ref[:, half], group) for half in range(halves)]
-    for c in range(group):
-        for out in range(halves):
-            left = None
-            for half in range(halves):
-                rows = pl.ds(half * LANES, LANES)
-                part = dot(blocks[half][c], held_ref[1, out, c, rows, :], NN)
-                left = part if left is None else left + part
-            stage_ref[0, out, :, c * SUB : (c + 1) * SUB, :] = left.reshape(peers, SUB, LANES)
-            for half in range(halves):
-                right = dot(blocks[half][c], held_ref[0, out, c], TN)
-                span = peers // halves
-                stage_ref[1, out, half * span : (half + 1) * span, c * SUB : (c + 1) * SUB, :] = (
-                    right.reshape(span, SUB, LANES)
-                )
-    for side in range(2):
+    grads = [jnp.concatenate([block[c] for block in blocks], axis=1) for c in range(group)]
+    copies = []
+    for side in (1, 0):
+        for c in range(group):
+            total = dot(grads[c], held_ref[1 - side, c], TN if side else NN)
+            for out in range(halves):
+                stage_ref[side, out, :, c * SUB : (c + 1) * SUB, :] = total[
+                    :, out * LANES : (out + 1) * LANES
+                ].reshape(peers, SUB, LANES)
         for out in range(halves):
             send_ref[:, side, out] = stage_ref[side, out].astype(BF16)
+            copies.append(
+                pltpu.make_async_copy(
+                    send_ref.at[:, side, out], send_hbm.at[:, side, out], sems.at[side, out]
+                )
+            )
+            copies[-1].start()
+    for copy in copies:
+        copy.wait()
 
 
 def unpack(got_ref, stage_ref):
@@ -336,7 +341,7 @@
     gain = wide(column(gain_ref[...], channels), width)
     unpack(got_ref, stage_ref)
     for i in range(rows):
-        hat, inverse = norm_sublanes(dot(eye, pair_ref[i], NT))
+        hat, inverse = norm_sublanes(jnp.transpose(pair_ref[i].astype(F32)))
         grad = dot(w_ref[:, 4 * channels :], gate_grad_ref[i], NN)
         for side in range(2):
             pieces = jnp.concatenate(
@@ -451,7 +456,7 @@
     got_operands, upstream = lax.optimization_barrier((got_operands, upstream))
     send, held = call(
         product_kernel, "product", [VMEM],
-        [(one_side, BF16, VMEM), ((2, halves, group, width, LANES), BF16, VMEM)],
+        [(one_side, BF16, VMEM), ((2, group, width, width), BF16, VMEM)],
         [((halves, inner, packed, LANES), F32)],
     )(got_operands)
     got_product = exchange(send, "dap")
@@ -467,8 +472,8 @@
     )(got_product, norm, gated, slope, w_out, gain_out)
 
     (send,) = call(
-        operands_back_kernel, "operands_back", [VMEM, VMEM], [(two_sides, BF16, VMEM)],
-        [((2, halves, inner, packed, LANES), F32)],
+        operands_back_kernel, "operands_back", [VMEM, VMEM], [(two_sides, BF16, HBM)],
+        [((2, halves, inner, packed, LANES), F32), (two_sides, BF16), COPIES((2, halves))],
     )(got_grad, held)
     got_operand_grads = exchange(send, "dap")
 

time: 165 us -> 163 us (0.988)
  no operation moved by 1% of the time
where the time goes in v6:
time: 163 us
  blocking collectives  80.2 us (49%)
  waiting for transfers between devices  29.1 us (18%)
  starting transfers between devices  23.3 us (14%)
  Pallas kernels  20.1 us (12%)
  local copies, waits for them, and re-layouts  8.28 us (5%)
    all_to_all x4, blocking collectives, exchange(): return lax.all_to_all(values, axis, split_axis=0, concat_axis=0, tiled=True)  80.2 us
    all_to_all x3, waiting for transfers between devices, exchange(): return lax.all_to_all(values, axis, split_axis=0, concat_axis=0, tiled=True)  29.1 us
    all_to_all x3, starting transfers between devices, exchange(): return lax.all_to_all(values, axis, split_axis=0, concat_axis=0, tiled=True)  23.3 us
    unnamed x30, local copies, waits for them, and re-layouts  8.28 us
    pallas_call x1, Pallas kernels, per_device(): call(output_ahead_kernel, 'output_ahead', [SMEM] + [VMEM] * 5 + [HBM] * 4...  6.34 us
    pallas_call x1, Pallas kernels, per_device(): call(project_kernel, 'project', [SMEM] + [HBM] * 6, [(two_sides, BF16, HB...  4.04 us
  transfers between devices with their start and end apart: 3, of which 3 were waited for; matrix products, arithmetic and copies ran while one was open for 0% of the time, Pallas kernels for 7%

profile of v6, /device:TPU:1, one launch (start us, length us, event | category | flops | bytes accessed | tf_op | source)
XLA Modules:
  0.0 162.5 jit_solution(12398459656960088344)
XLA Ops:
  1.3 4.0 %project.1 = (bf16[32,2,2,32,128]{4,3,2,1,0:T(8,128)(2,1)}, bf16[8,128,256]{2,1,0:T(8,128)(2,1)}, f32[2,1024,128]{2,1,0:T(8,128)}, bf16[8,4,128,256]{3,2,1,0:T(8...) custom-call(s32[1]{0:T(128)S(6)} %copy.20.lengths_ref, bf16[8,256,128]{2,1,0:T(8,128)(2,1)} %bitcast.11, ...), custom_call_target="tpu_custom_call" | custom-call | flops 1000000000 | bytes 4194304 | tf_op jit(solution)/shard_map/project/pallas_call | solution.py:429
  5.3 13.7 %all-to-all-start = ((bf16[32,2,2,32,128]{4,3,2,1,0:T(8,128)(2,1)}), bf16[32,2,2,32,128]{4,3,2,1,0:T(8,128)(2,1)S(1)}, u32[]{:S(2)}, u32[]{:S(2)}) async-start(bf16[32,2,2,32,128]{4,3,2,1,0:T(8,128)(2,1)} %get-tuple-element.25), calls=%async_computation | async-start | bytes 2097152 | tf_op jit(solution)/shard_map/all_to_all | solution.py:387
  19.1 6.3 %output_ahead.1 = (f32[2,1024,128]{2,1,0:T(8,128)}, bf16[8,4,128,256]{3,2,1,0:T(8,128)(2,1)}, bf16[8,128,256]{2,1,0:T(8,128)(2,1)}, f32[8,128,256]{2,1,0:T(8,128)}) custom-call(s32[1]{0:T(128)S(6)} %copy.20.lengths_ref, bf16[8,128,256]{2,1,0:T(8,128)(2,1)} %get-tuple-element.26.norm_ref, ...), custom_call_target="tpu_custom_call", output_to_operand_aliasing={{0}: (6, {}), {1}: (7, {}), {2}: (8, {}), {3}: (9, {})} | custom-call | flops 6000000000 | bytes 4194304 | tf_op jit(solution)/shard_map/output_ahead/pallas_call | solution.py:450
  25.4 13.3 %all-to-all-done.got_ref = bf16[32,2,2,32,128]{4,3,2,1,0:T(8,128)(2,1)S(1)} async-done(((bf16[32,2,2,32,128]{4,3,2,1,0:T(8,128)(2,1)}), bf16[32,2,2,32,128]{4,3,2,1,0:T(8,128)(2,1)S(1)}, u32[]{:S(2)}, u32[]{:S(2)}) %all-to-all-start) | async-done | bytes 1048608 | tf_op jit(solution)/shard_map/all_to_all | solution.py:387
  38.7 0.5 product.1
  39.2 21.0 %all_to_all.35.got_ref = bf16[32,2,32,128]{3,2,1,0:T(8,128)(2,1)S(1)} all-to-all(bf16[32,2,32,128]{3,2,1,0:T(8,128)(2,1)S(1)} %get-tuple-element.33), channel_id=1, replica_groups=mesh['dp'=16,'dap'=32] {'dap'}, dimensions={0} | all-to-all | bytes 1048576 | tf_op jit(solution)/shard_map/all_to_all | solution.py:387
  60.2 0.7 output_back.1
  60.9 16.7 %all_to_all.36.got_ref = bf16[32,2,32,128]{3,2,1,0:T(8,128)(2,1)S(1)} all-to-all(bf16[32,2,32,128]{3,2,1,0:T(8,128)(2,1)S(1)} %output_back.1), channel_id=1, replica_groups=mesh['dp'=16,'dap'=32] {'dap'}, dimensions={0} | all-to-all | bytes 1048576 | tf_op jit(solution)/shard_map/all_to_all | solution.py:387
  77.6 1.4 operands_back.1
  79.0 5.6 %all-to-all-start.3 = ((bf16[32,2,2,32,128]{4,3,2,1,0:T(8,128)(2,1)}), bf16[32,2,2,32,128]{4,3,2,1,0:T(8,128)(2,1)S(1)}, u32[]{:S(2)}, u32[]{:S(2)}) async-start(bf16[32,2,2,32,128]{4,3,2,1,0:T(8,128)(2,1)} %operands_back.1), calls=%async_computation.3 | async-start | bytes 2097152 | tf_op jit(solution)/shard_map/all_to_all | solution.py:387
  84.7 0.0 copy-start.1
  84.7 1.0 copy-done.1
  85.7 1.0 copy-done.4
  86.8 1.2 copy-done.11
  88.0 1.0 copy-done.12
  89.0 2.2 %output_weights.1 = (bf16[8,128,256]{2,1,0:T(8,128)(2,1)S(1)}, f32[2,128,128]{2,1,0:T(8,128)S(1)}) custom-call(bf16[32,2,32,128]{3,2,1,0:T(8,128)(2,1)S(1)} %copy-done.4, bf16[8,128,256]{2,1,0:T(8,128)(2,1)S(1)} %copy-done.1, bf16[8,128,256]{2,1,0:T(8,128)(2,1)S(1)} %copy-done.12, f32[8,128,256]{2,1,0:T(8,128)S(1)} %copy-done.11, ...), custom_call_target="tpu_custom_call" | custom-call | flops 4000000000 | bytes 4194304 | tf_op jit(solution)/shard_map/output_weights/pallas_call | solution.py:468
  91.3 0.8 copy-done.13
  92.1 10.6 %all-to-all-done.3.got_ref = bf16[32,2,2,32,128]{4,3,2,1,0:T(8,128)(2,1)S(1)} async-done(((bf16[32,2,2,32,128]{4,3,2,1,0:T(8,128)(2,1)}), bf16[32,2,2,32,128]{4,3,2,1,0:T(8,128)(2,1)S(1)}, u32[]{:S(2)}, u32[]{:S(2)}) %all-to-all-start.3) | async-done | bytes 1048608 | tf_op jit(solution)/shard_map/all_to_all | solution.py:387
  102.6 1.0 copy-done.2
  103.7 0.9 input_weights.1
  104.6 17.4 %all_to_all.37.got_ref = bf16[32,24,128]{2,1,0:T(8,128)(2,1)S(1)} all-to-all(bf16[32,24,128]{2,1,0:T(8,128)(2,1)S(1)} %bitcast.9), channel_id=1, replica_groups=mesh['dp'=16,'dap'=32] {'dap'}, dimensions={0} | all-to-all | bytes 393216 | tf_op jit(solution)/shard_map/all_to_all | solution.py:387
  122.0 0.0 copy-start.6
  122.0 0.0 copy-start.8
  122.0 25.1 %all_to_all.38.got_ref = bf16[16,24,128]{2,1,0:T(8,128)(2,1)S(1)} all-to-all(bf16[16,24,128]{2,1,0:T(8,128)(2,1)S(1)} %fold_inner.1), channel_id=1, replica_groups=mesh['dp'=16,'dap'=32] {'dp'}, dimensions={0} | all-to-all | bytes 196608 | tf_op jit(solution)/shard_map/all_to_all | solution.py:387
  147.2 0.7 fold_outer.1
  147.9 4.0 %all-to-all-start.6 = ((bf16[32,24,128]{2,1,0:T(8,128)(2,1)}), bf16[32,24,128]{2,1,0:T(8,128)(2,1)S(1)}, u32[]{:S(2)}, u32[]{:S(2)}) async-start(bf16[32,24,128]{2,1,0:T(8,128)(2,1)} %fold_outer.1), calls=%async_computation.6 | async-start | bytes 393216 | tf_op jit(solution)/shard_map/all_to_all | solution.py:387
  151.9 0.0 copy-start.5
  151.9 1.0 copy-done.5
  152.9 1.0 copy-done.14
  154.0 2.5 %input_back.1 = bf16[8,256,128]{2,1,0:T(8,128)(2,1)} custom-call(bf16[32,2,2,32,128]{4,3,2,1,0:T(8,128)(2,1)S(1)} %all-to-all-done.3.got_ref, bf16[8,4,128,256]{3,2,1,0:T(8,128)(2,1)S(1)} %copy-done, bf16[8,128,256]{2,1,0:T(8,128)(2,1)S(1)} %copy-done.14, bf16[8,256,128]{2,1,0:T(8,128)(2,1)S(1)} %bitcast.12, bf16[128,640]{1,0:T(8,128)(2,1)S(1)} %copy-done.6, ...), custom_call_target="tpu_custom_call" | custom-call | flops 6000000000 | bytes 4194304 | tf_op jit(solution)/shard_map/input_back/pallas_call | solution.py:486
  156.4 5.3 %all-to-all-done.6 = bf16[32,24,128]{2,1,0:T(8,128)(2,1)S(1)} async-done(((bf16[32,24,128]{2,1,0:T(8,128)(2,1)}), bf16[32,24,128]{2,1,0:T(8,128)(2,1)S(1)}, u32[]{:S(2)}, u32[]{:S(2)}) %all-to-all-start.6) | async-done | bytes 196640 | tf_op jit(solution)/shard_map/all_to_all | solution.py:387
  161.7 0.8 finish.1
  (19 shorter events, 0.1 us)
Async XLA Ops:
  5.3 33.4 %all-to-all-start = ((bf16[32,2,2,32,128]{4,3,2,1,0:T(8,128)(2,1)}), bf16[32,2,2,32,128]{4,3,2,1,0:T(8,128)(2,1)S(1)}, u32[]{:S(2)}, u32[]{:S(2)}) async-start(bf16[32,2,2,32,128]{4,3,2,1,0:T(8,128)(2,1)} %get-tuple-element.25), calls=%async_computation | async-start | bytes 2097152 | tf_op jit(solution)/shard_map/all_to_all | solution.py:387
  38.7 21.5 %copy-start.10 = (f32[2,1024,128]{2,1,0:T(8,128)S(1)}, f32[2,1024,128]{2,1,0:T(8,128)}, u32[]{:S(2)}) copy-start(f32[2,1024,128]{2,1,0:T(8,128)} %get-tuple-element.34.upstream_ref) | copy-start | bytes 3145732
  60.2 17.4 %copy-start.3 = (bf16[32,2,32,128]{3,2,1,0:T(8,128)(2,1)}, bf16[32,2,32,128]{3,2,1,0:T(8,128)(2,1)S(1)}, u32[]{:S(2)}) copy-start(bf16[32,2,32,128]{3,2,1,0:T(8,128)(2,1)S(1)} %all_to_all.35.got_ref) | copy-start | bytes 1572868
  77.6 7.0 %copy-start.7 = (bf16[128,128]{1,0:T(8,128)(2,1)S(1)}, bf16[128,128]{1,0:T(8,128)(2,1)}, u32[]{:S(2)}) copy-start(bf16[128,128]{1,0:T(8,128)(2,1)} %refs_3_.1) | copy-start | bytes 98308
  77.6 7.1 %copy-start.9 = (f32[128]{0:T(128)S(1)}, f32[128]{0:T(128)}, u32[]{:S(2)}) copy-start(f32[128]{0:T(128)} %param.13) | copy-start | bytes 1540
  79.0 23.6 %all-to-all-start.3 = ((bf16[32,2,2,32,128]{4,3,2,1,0:T(8,128)(2,1)}), bf16[32,2,2,32,128]{4,3,2,1,0:T(8,128)(2,1)S(1)}, u32[]{:S(2)}, u32[]{:S(2)}) async-start(bf16[32,2,2,32,128]{4,3,2,1,0:T(8,128)(2,1)} %operands_back.1), calls=%async_computation.3 | async-start | bytes 2097152 | tf_op jit(solution)/shard_map/all_to_all | solution.py:387
  84.7 1.0 copy-start.1
  85.7 1.0 copy-start.4
  86.8 1.2 copy-start.11
  88.0 1.0 copy-start.12
  89.0 13.6 %copy-start = (bf16[8,4,128,256]{3,2,1,0:T(8,128)(2,1)S(1)}, bf16[8,4,128,256]{3,2,1,0:T(8,128)(2,1)}, u32[]{:S(2)}) copy-start(bf16[8,4,128,256]{3,2,1,0:T(8,128)(2,1)} %get-tuple-element.36.factors_ref) | copy-start | bytes 6291460
  91.3 0.8 copy-start.13
  102.6 1.0 copy-start.2
  122.0 29.9 %copy-start.6 = (bf16[128,640]{1,0:T(8,128)(2,1)S(1)}, bf16[128,640]{1,0:T(8,128)(2,1)}, u32[]{:S(2)}) copy-start(bf16[128,640]{1,0:T(8,128)(2,1)} %refs_1_.1) | copy-start | bytes 491524
  122.0 29.9 %copy-start.8 = (f32[128]{0:T(128)S(1)}, f32[128]{0:T(128)}, u32[]{:S(2)}) copy-start(f32[128]{0:T(128)} %param.11) | copy-start | bytes 1540
  147.9 13.8 %all-to-all-start.6 = ((bf16[32,24,128]{2,1,0:T(8,128)(2,1)}), bf16[32,24,128]{2,1,0:T(8,128)(2,1)S(1)}, u32[]{:S(2)}, u32[]{:S(2)}) async-start(bf16[32,24,128]{2,1,0:T(8,128)(2,1)} %fold_outer.1), calls=%async_computation.6 | async-start | bytes 393216 | tf_op jit(solution)/shard_map/all_to_all | solution.py:387
  151.9 1.0 copy-start.5
  152.9 1.0 copy-start.14

commit v7 on v6

--- a/solution.py
+++ b/solution.py
@@ -72,7 +72,8 @@
     length, norm_ref, cotangent_ref, wt_ref, w_out_ref, gain_ref, outs, stages, sems
 ):
     rows, width, channels = cotangent_ref.shape
-    upstream_ref, factors_ref, gated_ref, slope_ref = stages
+    upstream_ref, left_ref, gated_ref, slope_ref, right_ref = stages
+    factors = (left_ref, right_ref)
     eye = identity(channels)
     gain = wide(column(gain_ref[...], channels), width)
     w_out = w_out_ref[...]
@@ -96,15 +97,9 @@
         for side in range(2):
             value, gate = projected[2 * side], sigmoid(projected[2 * side + 1])
             masked = mask * gate
-            factors_ref[i, 2 * side] = masked.astype(BF16)
-            factors_ref[i, 2 * side + 1] = (masked * value * (1.0 - gate)).astype(BF16)
-        if 2 * (i + 1) % rows == 0:
-            some = pl.ds(i + 1 - rows // 2, rows // 2)
-            copies.append(
-                pltpu.make_async_copy(factors_ref.at[some], outs[1].at[some], sems.at[1, i])
-            )
-            copies[-1].start()
-    for n in (0, 2, 3):
+            factors[side][i, 0] = masked.astype(BF16)
+            factors[side][i, 1] = (masked * value * (1.0 - gate)).astype(BF16)
+    for n in range(5):
         copies.append(pltpu.make_async_copy(stages[n], outs[n], sems.at[n, 0]))
         copies[-1].start()
     for copy in copies:
@@ -119,9 +114,9 @@
     lengths_ref, pair_hbm, cotangent_hbm, w_hbm, gain_hbm, w_out_hbm, gain_out_hbm,
     send_hbm, norm_hbm, *rest,
 ):
-    outs, stages = rest[:4], rest[4:8]
-    pair_ref, cotangent_ref, w_ref, gain_ref, w_out_ref, gain_out_ref = rest[8:14]
-    wt_ref, stage_ref, send_ref, norm_ref, sems, in_sems = rest[14:]
+    outs, stages = rest[:5], rest[5:10]
+    pair_ref, cotangent_ref, w_ref, gain_ref, w_out_ref, gain_out_ref = rest[10:16]
+    wt_ref, stage_ref, send_ref, norm_ref, sems, in_sems = rest[16:]
     rows, width, channels = pair_ref.shape
     length = lengths_ref[0]
     def fetch(source, target, n):
@@ -196,8 +191,8 @@
 def output_ahead_kernel(
     lengths_ref, norm_ref, cotangent_ref, w_ref, w_out_ref, gain_ref, *rest
 ):
-    outs, stages = rest[4:8], rest[8:12]
-    wt_ref, sems = rest[12:]
+    outs, stages = rest[5:10], rest[10:15]
+    wt_ref, sems = rest[15:]
 
     @pl.when(jnp.logical_not(first_core()))
     def _():
@@ -297,56 +292,58 @@
         copy.wait()
 
 
-def unpack(got_ref, stage_ref):
-    for side in range(got_ref.shape[1]):
-        for half in range(got_ref.shape[2]):
-            stage_ref[side, half] = got_ref[:, side, half].astype(F32).reshape(-1, LANES)
-
-
-def pieces_of(stage_ref, factors_ref, i, side, half, rows, channels):
+def unpack(got_ref, stage_ref, side):
+    for half in range(got_ref.shape[2]):
+        stage_ref[half] = got_ref[:, side, half].astype(F32).reshape(-1, LANES)
+
+
+def pieces_of(stage_ref, factors_ref, i, half, rows, channels):
     lanes = slice(half * LANES, (half + 1) * LANES)
-    grad = stage_ref[side, half, pl.ds(i, channels, stride=rows), :]
+    grad = stage_ref[half, pl.ds(i, channels, stride=rows), :]
     return jnp.concatenate(
-        [
-            (grad * factors_ref[i, 2 * side + n, :, lanes].astype(F32)).astype(BF16)
-            for n in range(2)
-        ],
+        [(grad * factors_ref[i, n, :, lanes].astype(F32)).astype(BF16) for n in range(2)],
         axis=0,
     )
 
 
-def input_weights_kernel(got_ref, factors_ref, norm_ref, sums_ref, parts_ref, stage_ref):
-    halves = got_ref.shape[2]
+def side_weights(got_ref, factors_ref, norm_ref, parts_ref, stage_ref, side):
     rows, channels, _ = norm_ref.shape
-    unpack(got_ref, stage_ref)
-    totals = [jnp.zeros((channels, 2 * channels), F32) for _ in range(2)]
+    unpack(got_ref, stage_ref, side)
+    total = jnp.zeros((channels, 2 * channels), F32)
     for i in range(rows):
-        for half in range(halves):
+        for half in range(got_ref.shape[2]):
             norm = norm_ref[i, :, half * LANES : (half + 1) * LANES]
-            for side in range(2):
-                pieces = pieces_of(stage_ref, factors_ref, i, side, half, rows, channels)
-                totals[side] = totals[side] + dot(norm, pieces, NT)
-    for side in range(2):
-        for n in range(2):
-            parts_ref[2 * side + n] = totals[side][:, n * channels : (n + 1) * channels].astype(BF16)
+            total = total + dot(norm, pieces_of(stage_ref, factors_ref, i, half, rows, channels), NT)
+    for n in range(2):
+        parts_ref[2 * side + n] = total[:, n * channels : (n + 1) * channels].astype(BF16)
+
+
+def left_weights_kernel(got_ref, factors_ref, norm_ref, parts_ref, stage_ref):
+    side_weights(got_ref, factors_ref, norm_ref, parts_ref, stage_ref, 0)
+
+
+def right_weights_kernel(got_ref, factors_ref, norm_ref, sums_ref, left_ref, parts_ref, stage_ref):
+    parts_ref[:2] = left_ref[...]
+    side_weights(got_ref, factors_ref, norm_ref, parts_ref, stage_ref, 1)
     parts_ref[4] = sums_ref[0].astype(BF16)
     parts_ref[5] = sums_ref[1].astype(BF16)
 
 
 def input_back_kernel(
-    got_ref, factors_ref, gate_grad_ref, pair_ref, w_ref, gain_ref, out_ref, stage_ref
+    got_ref, left_ref, right_ref, gate_grad_ref, pair_ref, w_ref, gain_ref, out_ref, *stages
 ):
     rows, width, channels = pair_ref.shape
     eye = identity(channels)
     gain = wide(column(gain_ref[...], channels), width)
-    unpack(got_ref, stage_ref)
+    for side in range(2):
+        unpack(got_ref, stages[side], side)
     for i in range(rows):
         hat, inverse = norm_sublanes(jnp.transpose(pair_ref[i].astype(F32)))
         grad = dot(w_ref[:, 4 * channels :], gate_grad_ref[i], NN)
         for side in range(2):
             pieces = jnp.concatenate(
                 [
-                    pieces_of(stage_ref, factors_ref, i, side, half, rows, channels)
+                    pieces_of(stages[side], (left_ref, right_ref)[side], i, half, rows, channels)
                     for half in range(width // LANES)
                 ],
                 axis=1,
@@ -420,9 +417,10 @@
 
     ahead = [
         (mixed, F32),
-        ((rows, 4, channels, width), BF16),
+        ((rows, 2, channels, width), BF16),
         (flat, BF16),
         (flat, F32),
+        ((rows, 2, channels, width), BF16),
     ]
     ahead_outs = [(shape, dtype, HBM) for shape, dtype in ahead]
     transposed = ((5 * channels, channels), BF16)
@@ -441,16 +439,16 @@
             ((2,) + mixed, F32),
             (two_sides, BF16),
             (flat, BF16),
-            COPIES((4, rows)),
+            COPIES((5, rows)),
             COPIES((10,)),
         ],
         grant=60,
     )(lengths, pair, cotangent, w_in, gain_in, w_out, gain_out)
     got_operands = exchange(send, "dap")
-    upstream, factors, gated, slope = call(
-        output_ahead_kernel, "output_ahead", [SMEM] + [VMEM] * 5 + [HBM] * 4, ahead_outs,
-        ahead + [transposed, COPIES((4, rows))],
-        aliases={6 + n: n for n in range(4)}, flops=6 * 10**9, grant=60,
+    upstream, left_factors, gated, slope, right_factors = call(
+        output_ahead_kernel, "output_ahead", [SMEM] + [VMEM] * 5 + [HBM] * 5, ahead_outs,
+        ahead + [transposed, COPIES((5, rows))],
+        aliases={6 + n: n for n in range(5)}, flops=6 * 10**9, grant=60,
     )(lengths, norm, cotangent, w_in, w_out, gain_out, *ahead_parts)
 
     got_operands, upstream = lax.optimization_barrier((got_operands, upstream))
@@ -477,16 +475,20 @@
     )(got_grad, held)
     got_operand_grads = exchange(send, "dap")
 
+    (left_parts,) = call(
+        left_weights_kernel, "left_weights", [VMEM] * 3, [((2,) + square, BF16, VMEM)],
+        [(mixed, F32)],
+    )(got_operand_grads, left_factors, norm)
     (parts,) = call(
-        input_weights_kernel, "input_weights", [VMEM] * 4, [((6,) + square, BF16, VMEM)],
-        [((2,) + mixed, F32)],
-    )(got_operand_grads, factors, norm, sums)
+        right_weights_kernel, "right_weights", [VMEM] * 5, [((6,) + square, BF16, VMEM)],
+        [(mixed, F32)],
+    )(got_operand_grads, right_factors, norm, sums, left_parts)
     share = 6 * channels // inner
     got = exchange(parts.reshape(inner, share, channels), "dap")
     (pair_grad,) = call(
-        input_back_kernel, "input_back", [VMEM] * 6, [((rows, width, channels), BF16, VMEM)],
-        [((2,) + mixed, F32)], flops=6 * 10**9,
-    )(got_operand_grads, factors, gate_grad, pair, w_in, gain_in)
+        input_back_kernel, "input_back", [VMEM] * 7, [((rows, width, channels), BF16, VMEM)],
+        [(mixed, F32), (mixed, F32)], flops=6 * 10**9,
+    )(got_operand_grads, left_factors, right_factors, gate_grad, pair, w_in, gain_in)
     (send,) = call(
         fold_kernel, "fold_inner", [VMEM], [((outer, share, channels), BF16, VMEM)]
     )(got)

time: 163 us -> 164 us (level)
  local copies, waits for them, and re-layouts: 8.28 us -> 6.25 us
    unnamed x30 -> x28, local copies, waits for them, and re-layouts: 8.28 us -> 6.25 us
    pallas_call x3 -> x4, Pallas kernels: 9.68 us -> 10.5 us  [the longest x1 6.98 us: per_device(): call(output_ahead_kernel, 'output_ahead', [SMEM] + [VMEM] * 5 + [HBM] * 5...]
where the time goes in v7:
time: 164 us; the launch traced here: 163 us
  blocking collectives  80.9 us (49%)
  waiting for transfers between devices  30.1 us (18%)
  starting transfers between devices  23.4 us (14%)
  Pallas kernels  20.9 us (13%)
  local copies, waits for them, and re-layouts  6.25 us (4%)
    all_to_all x4, blocking collectives, exchange(): return lax.all_to_all(values, axis, split_axis=0, concat_axis=0, tiled=True)  80.9 us
    all_to_all x3, waiting for transfers between devices, exchange(): return lax.all_to_all(values, axis, split_axis=0, concat_axis=0, tiled=True)  30.1 us
    all_to_all x3, starting transfers between devices, exchange(): return lax.all_to_all(values, axis, split_axis=0, concat_axis=0, tiled=True)  23.4 us
    pallas_call x1, Pallas kernels, per_device(): call(output_ahead_kernel, 'output_ahead', [SMEM] + [VMEM] * 5 + [HBM] * 5...  6.98 us
    unnamed x28, local copies, waits for them, and re-layouts  6.25 us
    pallas_call x1, Pallas kernels, per_device(): call(project_kernel, 'project', [SMEM] + [HBM] * 6, [(two_sides, BF16, HB...  4.09 us
  transfers between devices with their start and end apart: 3, of which 3 were waited for; matrix products, arithmetic and copies ran while one was open for 0% of the time, Pallas kernels for 7%

profile of v7, /device:TPU:1, one launch (start us, length us, event | category | flops | bytes accessed | tf_op | source)
XLA Modules:
  0.0 163.0 jit_solution(8117365184486706947)
XLA Ops:
  1.3 4.1 %project.1 = (bf16[32,2,2,32,128]{4,3,2,1,0:T(8,128)(2,1)}, bf16[8,128,256]{2,1,0:T(8,128)(2,1)}, f32[2,1024,128]{2,1,0:T(8,128)}, bf16[8,2,128,256]{3,2,1,0:T(8...) custom-call(s32[1]{0:T(128)S(6)} %copy.22.lengths_ref, ...), custom_call_target="tpu_custom_call" | custom-call | flops 1000000000 | bytes 4194304 | tf_op jit(solution)/shard_map/project/pallas_call | solution.py:427
  5.4 13.7 %all-to-all-start = ((bf16[32,2,2,32,128]{4,3,2,1,0:T(8,128)(2,1)}), bf16[32,2,2,32,128]{4,3,2,1,0:T(8,128)(2,1)S(1)}, u32[]{:S(2)}, u32[]{:S(2)}) async-start(bf16[32,2,2,32,128]{4,3,2,1,0:T(8,128)(2,1)} %get-tuple-element.27), calls=%async_computation | async-start | bytes 2097152 | tf_op jit(solution)/shard_map/all_to_all | solution.py:384
  19.1 7.0 %output_ahead.1 = (f32[2,1024,128]{2,1,0:T(8,128)}, bf16[8,2,128,256]{3,2,1,0:T(8,128)(2,1)}, bf16[8,128,256]{2,1,0:T(8,128)(2,1)}, f32[8,128,256]{2,1,0:T(8,128)}, bf16[8,2,128,256]{3,2,1,0:T(8,128)(2,1)}) custom-call(s32[1]{0:T(128)S(6)} %copy.22.lengths_ref, ...), custom_call_target="tpu_custom_call", output_to_operand_aliasing={{0}: (6, {}), {1}: (7, {}), {2}: (8, {}), {3}: (9, {}), {4}... | custom-call | flops 6000000000 | bytes 4194304 | tf_op jit(solution)/shard_map/output_ahead/pallas_call | solution.py:448
  26.1 12.4 %all-to-all-done.got_ref = bf16[32,2,2,32,128]{4,3,2,1,0:T(8,128)(2,1)S(1)} async-done(((bf16[32,2,2,32,128]{4,3,2,1,0:T(8,128)(2,1)}), bf16[32,2,2,32,128]{4,3,2,1,0:T(8,128)(2,1)S(1)}, u32[]{:S(2)}, u32[]{:S(2)}) %all-to-all-start) | async-done | bytes 1048608 | tf_op jit(solution)/shard_map/all_to_all | solution.py:384
  38.5 0.5 product.1
  39.0 20.6 %all_to_all.35.got_ref = bf16[32,2,32,128]{3,2,1,0:T(8,128)(2,1)S(1)} all-to-all(bf16[32,2,32,128]{3,2,1,0:T(8,128)(2,1)S(1)} %get-tuple-element.36), channel_id=1, replica_groups=mesh['dp'=16,'dap'=32] {'dap'}, dimensions={0} | all-to-all | bytes 1048576 | tf_op jit(solution)/shard_map/all_to_all | solution.py:384
  59.6 0.7 output_back.1
  60.3 16.6 %all_to_all.36.got_ref = bf16[32,2,32,128]{3,2,1,0:T(8,128)(2,1)S(1)} all-to-all(bf16[32,2,32,128]{3,2,1,0:T(8,128)(2,1)S(1)} %output_back.1), channel_id=1, replica_groups=mesh['dp'=16,'dap'=32] {'dap'}, dimensions={0} | all-to-all | bytes 1048576 | tf_op jit(solution)/shard_map/all_to_all | solution.py:384
  76.9 1.4 operands_back.1
  78.3 0.0 copy-start.2
  78.3 0.0 copy-start.6
  78.4 5.6 %all-to-all-start.3 = ((bf16[32,2,2,32,128]{4,3,2,1,0:T(8,128)(2,1)}), bf16[32,2,2,32,128]{4,3,2,1,0:T(8,128)(2,1)S(1)}, u32[]{:S(2)}, u32[]{:S(2)}) async-start(bf16[32,2,2,32,128]{4,3,2,1,0:T(8,128)(2,1)} %operands_back.1), calls=%async_computation.3 | async-start | bytes 2097152 | tf_op jit(solution)/shard_map/all_to_all | solution.py:384
  84.0 0.0 copy-start.4
  84.0 0.6 copy-done.4
  84.6 1.0 copy-done.11
  85.7 2.2 %output_weights.1 = (bf16[8,128,256]{2,1,0:T(8,128)(2,1)S(1)}, f32[2,128,128]{2,1,0:T(8,128)S(1)}) custom-call(bf16[32,2,32,128]{3,2,1,0:T(8,128)(2,1)S(1)} %all_to_all.35.got_ref, bf16[8,128,256]{2,1,0:T(8,128)(2,1)S(1)} %copy-done.6, bf16[8,128,256]{2,1,0:T(8,128)(2,1)S(1)} %copy-done.11, f32[8,128,256]{2,1,0:T(8,128)S(1)} %copy-done.10, ...), custom_call_target="tpu_custom_call" | custom-call | flops 4000000000 | bytes 4194304 | tf_op jit(solution)/shard_map/output_weights/pallas_call | solution.py:466
  87.9 0.8 copy-done.12
  88.7 12.2 %all-to-all-done.3.got_ref = bf16[32,2,2,32,128]{4,3,2,1,0:T(8,128)(2,1)S(1)} async-done(((bf16[32,2,2,32,128]{4,3,2,1,0:T(8,128)(2,1)}), bf16[32,2,2,32,128]{4,3,2,1,0:T(8,128)(2,1)S(1)}, u32[]{:S(2)}, u32[]{:S(2)}) %all-to-all-start.3) | async-done | bytes 1048608 | tf_op jit(solution)/shard_map/all_to_all | solution.py:384
  100.9 1.2 copy-done.7
  102.2 0.5 left_weights.1.left_ref
  102.7 0.7 copy-done.5
  103.4 0.5 right_weights.1
  103.9 17.8 %all_to_all.37.got_ref = bf16[32,24,128]{2,1,0:T(8,128)(2,1)S(1)} all-to-all(bf16[32,24,128]{2,1,0:T(8,128)(2,1)S(1)} %bitcast.10), channel_id=1, replica_groups=mesh['dp'=16,'dap'=32] {'dap'}, dimensions={0} | all-to-all | bytes 393216 | tf_op jit(solution)/shard_map/all_to_all | solution.py:384
  121.7 25.9 %all_to_all.38.got_ref = bf16[16,24,128]{2,1,0:T(8,128)(2,1)S(1)} all-to-all(bf16[16,24,128]{2,1,0:T(8,128)(2,1)S(1)} %fold_inner.1), channel_id=1, replica_groups=mesh['dp'=16,'dap'=32] {'dp'}, dimensions={0} | all-to-all | bytes 196608 | tf_op jit(solution)/shard_map/all_to_all | solution.py:384
  147.6 0.7 fold_outer.1
  148.3 4.1 %all-to-all-start.6 = ((bf16[32,24,128]{2,1,0:T(8,128)(2,1)}), bf16[32,24,128]{2,1,0:T(8,128)(2,1)S(1)}, u32[]{:S(2)}, u32[]{:S(2)}) async-start(bf16[32,24,128]{2,1,0:T(8,128)(2,1)} %fold_outer.1), calls=%async_computation.6 | async-start | bytes 393216 | tf_op jit(solution)/shard_map/all_to_all | solution.py:384
  152.4 0.0 copy-start.3
  152.4 0.6 copy-done.3
  153.1 1.2 copy-done.8
  154.3 2.4 %input_back.1 = bf16[8,256,128]{2,1,0:T(8,128)(2,1)} custom-call(bf16[32,2,2,32,128]{4,3,2,1,0:T(8,128)(2,1)S(1)} %all-to-all-done.3.got_ref, bf16[8,2,128,256]{3,2,1,0:T(8,128)(2,1)S(1)} %copy-done.8, bf16[8,2,128,256]{3,2,1,0:T(8,128)(2,1)S(1)} %copy-done.5, bf16[8,128,256]{2,1,0:T(8,128)(2,1)S(1)} %copy-done.13, bf16[8,256,128]{2,1,0:T(8,128)(2,1)S(1)} %bitcast.12, ...), custom_call_target="tpu_custom_call" | custom-call | flops 6000000000 | bytes 4194304 | tf_op jit(solution)/shard_map/input_back/pallas_call | solution.py:488
  156.7 5.5 %all-to-all-done.6 = bf16[32,24,128]{2,1,0:T(8,128)(2,1)S(1)} async-done(((bf16[32,24,128]{2,1,0:T(8,128)(2,1)}), bf16[32,24,128]{2,1,0:T(8,128)(2,1)S(1)}, u32[]{:S(2)}, u32[]{:S(2)}) %all-to-all-start.6) | async-done | bytes 196640 | tf_op jit(solution)/shard_map/all_to_all | solution.py:384
  162.2 0.8 finish.1
  (18 shorter events, 0.1 us)
Async XLA Ops:
  5.4 33.1 %all-to-all-start = ((bf16[32,2,2,32,128]{4,3,2,1,0:T(8,128)(2,1)}), bf16[32,2,2,32,128]{4,3,2,1,0:T(8,128)(2,1)S(1)}, u32[]{:S(2)}, u32[]{:S(2)}) async-start(bf16[32,2,2,32,128]{4,3,2,1,0:T(8,128)(2,1)} %get-tuple-element.27), calls=%async_computation | async-start | bytes 2097152 | tf_op jit(solution)/shard_map/all_to_all | solution.py:384
  38.9 20.6 %copy-start.9 = (f32[2,1024,128]{2,1,0:T(8,128)S(1)}, f32[2,1024,128]{2,1,0:T(8,128)}, u32[]{:S(2)}) copy-start(f32[2,1024,128]{2,1,0:T(8,128)} %get-tuple-element.37.upstream_ref) | copy-start | bytes 3145732
  78.3 5.7 %copy-start.2 = (bf16[128,128]{1,0:T(8,128)(2,1)S(1)}, bf16[128,128]{1,0:T(8,128)(2,1)}, u32[]{:S(2)}) copy-start(bf16[128,128]{1,0:T(8,128)(2,1)} %refs_3_.1) | copy-start | bytes 98308
  78.3 5.7 %copy-start.6 = (bf16[8,128,256]{2,1,0:T(8,128)(2,1)S(1)}, bf16[8,128,256]{2,1,0:T(8,128)(2,1)}, u32[]{:S(2)}) copy-start(bf16[8,128,256]{2,1,0:T(8,128)(2,1)} %get-tuple-element.28.norm_ref) | copy-start | bytes 1572868
  78.3 5.7 %copy-start.10 = (f32[8,128,256]{2,1,0:T(8,128)S(1)}, f32[8,128,256]{2,1,0:T(8,128)}, u32[]{:S(2)}) copy-start(f32[8,128,256]{2,1,0:T(8,128)} %get-tuple-element.42.slope_ref) | copy-start | bytes 3145732
  78.4 22.6 %all-to-all-start.3 = ((bf16[32,2,2,32,128]{4,3,2,1,0:T(8,128)(2,1)}), bf16[32,2,2,32,128]{4,3,2,1,0:T(8,128)(2,1)S(1)}, u32[]{:S(2)}, u32[]{:S(2)}) async-start(bf16[32,2,2,32,128]{4,3,2,1,0:T(8,128)(2,1)} %operands_back.1), calls=%async_computation.3 | async-start | bytes 2097152 | tf_op jit(solution)/shard_map/all_to_all | solution.py:384
  84.0 0.7 copy-start.4
  84.6 1.0 copy-start.11
  87.9 0.8 copy-start.12
  100.9 1.2 copy-start.7
  102.2 1.2 copy-start.5
  147.6 4.8 %copy-start = (bf16[1,8,256,128]{3,2,1,0:T(8,128)(2,1)S(1)}, bf16[1,8,256,128]{3,2,1,0:T(8,128)(2,1)}, u32[]{:S(2)}) copy-start(bf16[1,8,256,128]{3,2,1,0:T(8,128)(2,1)} %param.7) | copy-start | bytes 1572868
  147.6 4.8 %copy-start.13 = (bf16[8,128,256]{2,1,0:T(8,128)(2,1)S(1)}, bf16[8,128,256]{2,1,0:T(8,128)(2,1)}, u32[]{:S(2)}) copy-start(bf16[8,128,256]{2,1,0:T(8,128)(2,1)} %copy-done.12) | copy-start | bytes 1572868
  148.3 4.1 %copy-start.1 = (bf16[128,640]{1,0:T(8,128)(2,1)S(1)}, bf16[128,640]{1,0:T(8,128)(2,1)}, u32[]{:S(2)}) copy-start(bf16[128,640]{1,0:T(8,128)(2,1)} %refs_1_.1) | copy-start | bytes 491524
  148.3 13.9 %all-to-all-start.6 = ((bf16[32,24,128]{2,1,0:T(8,128)(2,1)}), bf16[32,24,128]{2,1,0:T(8,128)(2,1)S(1)}, u32[]{:S(2)}, u32[]{:S(2)}) async-start(bf16[32,24,128]{2,1,0:T(8,128)(2,1)} %fold_outer.1), calls=%async_computation.6 | async-start | bytes 393216 | tf_op jit(solution)/shard_map/all_to_all | solution.py:384
  152.4 0.7 copy-start.3
  153.1 1.2 copy-start.8
